TPU v7x, 512 devices: a whole 4x8x8 slice. The times are simulated.
512 devices in a mesh: node: 32 (over x, z), feat: 16 (over y, core).
Axes of the slice: x: 4, y: 8, z: 8, core: 2. Of those that a mesh axis runs over, the one named last changes fastest.
Arguments:
- features: bfloat16 [16384, 4096], P('node', 'feat'), may hold values from -6 to 6
- own_features: bfloat16 [6144, 4096], P('node', 'feat'), may hold values from -6 to 6
- neigh_index: int32 [32, 6144, 4], P('node'), may hold values from 0 to 511
- neigh_count: int32 [32, 6144], P('node'), may hold values from 0 to 4, as said below
- degree: int32 [6144], P('node'), may hold values from 1 to 128, as said below
- local_index: int32 [6144, 10], P('node'), may hold values from 0 to 191
- local_count: int32 [6144], P('node'), may hold values from 0 to 10
- self_weight: bfloat16 [4096, 1024], P('feat'), may hold values from -0.09375 to 0.09375
- neigh_weight: bfloat16 [4096, 1024], P('feat'), may hold values from -0.09375 to 0.09375
- weight_two: bfloat16 [1024, 1024], replicated, may hold values from -0.1875 to 0.1875
- weight_three: bfloat16 [1024, 172], replicated, may hold values from -0.1875 to 0.1875
- cotangent: bfloat16 [6144, 172], P('node'), may hold values from -6 to 6
Outputs:
- grad_self: bfloat16 [4096, 1024], P('feat')
- grad_neigh: bfloat16 [4096, 1024], P('feat')
- logits: bfloat16 [6144, 172], P('node')
Inputs may be any that keep to these rules, and one draw needn't show every extreme that they name: `neigh_count`: slab s is full (4 live slots) at row s. degree[r] is the sum of neigh_count[s, r] over all slabs s.
All inputs are finite; a program needn't handle non-finite values.
Results may differ from a plain program's by a relative error of at most 0.015.
Values may be sent and summed in bfloat16 or wider, within the bound.
No kernel may reach another device: no remote copies, remote signals or barrier semaphores. Data moves between devices by JAX's collectives and lax.ppermute only.
A program may use at most 64 MiB of HBM per device.

v0:
```python
import math

import jax
import jax.numpy as jnp
from jax import lax
from jax.sharding import PartitionSpec as P


def silu_slope(value):
    gate = jax.nn.sigmoid(value)
    return gate + value * gate * (1.0 - gate)


def slab_partial(table, index, count):
    running = jnp.zeros((index.shape[0], table.shape[1]), jnp.float32)
    for slot in range(index.shape[1]):
        picked = table[index[:, slot]].astype(jnp.float32)
        running = running + jnp.where((count > slot)[:, None], picked, 0.0)
    return running.astype(jnp.bfloat16)


def second_layer(first_hidden, local_index, local_count, weight_two, weight_three, cotangent):
    row_count = first_hidden.shape[0]
    slot_ids = jnp.arange(local_index.shape[1], dtype=jnp.int32)
    live_slots = slot_ids[None, :] < local_count[:, None]
    slot_hits = (
        local_index[:, :, None] == jnp.arange(row_count, dtype=jnp.int32)[None, None, :]
    ) & live_slots[:, :, None]
    adjacency = jnp.sum(slot_hits.astype(jnp.float32), axis=1) + jnp.eye(
        row_count, dtype=jnp.float32
    )
    inv_count = 1.0 / (1.0 + local_count.astype(jnp.float32))
    mixed_rows = (
        jnp.dot(adjacency.astype(jnp.bfloat16), first_hidden, preferred_element_type=jnp.float32)
        * inv_count[:, None]
    ).astype(jnp.bfloat16)
    pre_two = jnp.dot(mixed_rows, weight_two, preferred_element_type=jnp.float32)
    second_hidden = jax.nn.silu(pre_two).astype(jnp.bfloat16)
    logits = jnp.dot(second_hidden, weight_three, preferred_element_type=jnp.float32).astype(
        jnp.bfloat16
    )
    back_two = jnp.dot(cotangent, weight_three.T, preferred_element_type=jnp.float32)
    grad_pre_two = (back_two * silu_slope(pre_two)).astype(jnp.bfloat16)
    grad_mixed = (
        jnp.dot(grad_pre_two, weight_two.T, preferred_element_type=jnp.float32) * inv_count[:, None]
    )
    grad_hidden = jnp.dot(
        adjacency.T, grad_mixed, precision=lax.Precision.HIGHEST, preferred_element_type=jnp.float32
    )
    return (logits, grad_hidden)


def body(
    features,
    own_features,
    neigh_index,
    neigh_count,
    degree,
    local_index,
    local_count,
    self_weight,
    neigh_weight,
    weight_two,
    weight_three,
    cotangent,
):
    index = neigh_index[0]
    count = neigh_count[0]
    total_rows = index.shape[0]
    slot_total = index.shape[1]
    block = math.gcd(total_rows, 512)

    def one_block(group):
        return slab_partial(features, group[0], group[1])

    parts = lax.map(
        one_block,
        (
            index.reshape(total_rows // block, block, slot_total),
            count.reshape(total_rows // block, block),
        ),
    )
    groups = lax.axis_size("node")
    own_rows = total_rows // groups
    stacked = parts.reshape(groups, own_rows, features.shape[1])
    neighbour_sum = jnp.sum(
        lax.all_to_all(stacked, "node", split_axis=0, concat_axis=0, tiled=True).astype(
            jnp.float32
        ),
        axis=0,
    )
    mean_rows = (neighbour_sum / degree[:, None].astype(jnp.float32)).astype(jnp.bfloat16)
    pre_part = jnp.dot(own_features, self_weight, preferred_element_type=jnp.float32) + jnp.dot(
        mean_rows, neigh_weight, preferred_element_type=jnp.float32
    )
    pre_one = lax.psum(pre_part, "feat")
    first_hidden = jax.nn.silu(pre_one).astype(jnp.bfloat16)
    slope_one = silu_slope(pre_one).astype(jnp.bfloat16)
    logits, grad_hidden = second_layer(
        first_hidden, local_index, local_count, weight_two, weight_three, cotangent
    )
    grad_pre_one = (grad_hidden * slope_one.astype(jnp.float32)).astype(jnp.bfloat16)
    self_part = jnp.dot(own_features.T, grad_pre_one, preferred_element_type=jnp.float32)
    neigh_part = jnp.dot(mean_rows.T, grad_pre_one, preferred_element_type=jnp.float32)
    grad_self, grad_neigh = lax.psum((self_part, neigh_part), "node")
    return (grad_self.astype(jnp.bfloat16), grad_neigh.astype(jnp.bfloat16), logits)


def solution(mesh):
    in_specs = (
        P("node", "feat"),
        P("node", "feat"),
        P("node", None, None),
        P("node", None),
        P("node"),
        P("node", None),
        P("node"),
        P("feat", None),
        P("feat", None),
        P(),
        P(),
        P("node", None),
    )
    out_specs = (P("feat", None), P("feat", None), P("node", None))
    return jax.shard_map(body, mesh=mesh, in_specs=in_specs, out_specs=out_specs, check_vma=False)
```

profile of v0, /device:TPU:24, one launch (start us, length us, event | category | flops | bytes accessed | tf_op | source)
XLA Modules:
  0.0 528.5 jit_solution(15095239543371929666)
XLA Ops:
  7.7 1.5 reduce.11
  9.3 124.5 %while.10 = (s32[]{:T(128)}, bf16[12,512,256]{2,1,0:T(8,128)(2,1)}, s32[12,512]{1,0:T(8,128)S(1)}, s32[12,512,4]{1,2,0:T(4,128)}, bf16[512,256]{1,0:T(8,128)(2,1)}, /*index=5*/s32[]{:T(128)}) while((s32[]{:T(128)}, bf16[12,512,256]{2,1,0:T(8,128)(2,1)}, s32[12,512]{1,0:T(8,128)S(1)}, s32[12,512,4]{1,2,0:T(4,128)}, bf16[512,256]{1,0:T(8,128)(2,1)}, ...), condition=%wide.region_2.3_spmd, body=%wide.region_1.2_spmd.sunk | while | flops 1585154 | bytes 4528745 | solution.py:76
  10.1 2.5 gather_fusion.2
  12.6 2.0 gather_fusion.3
  14.6 2.0 gather_fusion
  16.6 2.0 gather_fusion.1
  20.4 2.5 gather_fusion.2
  23.0 2.0 gather_fusion.3
  25.0 2.0 gather_fusion
  27.0 2.0 gather_fusion.1
  30.8 2.5 gather_fusion.2
  33.4 2.0 gather_fusion.3
  35.4 2.0 gather_fusion
  37.3 2.0 gather_fusion.1
  41.2 2.5 gather_fusion.2
  43.8 2.0 gather_fusion.3
  45.7 2.0 gather_fusion
  47.7 2.0 gather_fusion.1
  51.5 2.5 gather_fusion.2
  54.1 2.0 gather_fusion.3
  56.1 2.0 gather_fusion
  58.1 2.0 gather_fusion.1
  61.9 2.5 gather_fusion.2
  64.5 2.0 gather_fusion.3
  66.5 2.0 gather_fusion
  68.4 2.0 gather_fusion.1
  72.3 2.5 gather_fusion.2
  74.8 2.0 gather_fusion.3
  76.8 2.0 gather_fusion
  78.8 2.0 gather_fusion.1
  82.6 2.5 gather_fusion.2
  85.2 2.0 gather_fusion.3
  87.2 2.0 gather_fusion
  89.2 2.0 gather_fusion.1
  91.2 1.1 fusion.47
  93.0 2.5 gather_fusion.2
  95.6 2.0 gather_fusion.3
  97.6 2.0 gather_fusion
  99.5 2.0 gather_fusion.1
  103.4 2.5 gather_fusion.2
  106.0 2.0 gather_fusion.3
  107.9 2.0 gather_fusion
  109.9 2.0 gather_fusion.1
  111.9 1.1 fusion.47
  113.8 2.5 gather_fusion.2
  116.3 2.0 gather_fusion.3
  118.3 2.0 gather_fusion
  120.3 2.0 gather_fusion.1
  124.1 2.5 gather_fusion.2
  126.7 2.0 gather_fusion.3
  128.7 2.0 gather_fusion
  130.7 2.0 gather_fusion.1
  133.7 13.4 %all-to-all-start = ((bf16[32,192,256]{2,1,0:T(8,128)(2,1)}), bf16[32,192,256]{2,1,0:T(8,128)(2,1)}, u32[]{:S(2)}, u32[]{:S(2)}) async-start(bf16[32,192,256]{2,1,0:T(8,128)(2,1)} %bitcast.52), calls=%async_computation | async-start | bytes 6291456 | tf_op jit(solution)/shard_map/all_to_all | solution.py:87
  147.2 1.3 fusion.33
  148.6 73.2 %all-to-all-done = bf16[32,192,256]{2,1,0:T(8,128)(2,1)} async-done(((bf16[32,192,256]{2,1,0:T(8,128)(2,1)}), bf16[32,192,256]{2,1,0:T(8,128)(2,1)}, u32[]{:S(2)}, u32[]{:S(2)}) %all-to-all-start) | async-done | bytes 3145760 | tf_op jit(solution)/shard_map/all_to_all | solution.py:87
  221.8 2.3 convert_reduce_fusion
  224.2 2.3 convolution_add_fusion
  227.3 111.7 %all-reduce.4.cloned.1.call-done = f32[192,1024]{1,0:T(8,128)} async-done(((f32[192,1024]{1,0:T(8,128)}), f32[192,1024]{1,0:T(8,128)}) %all-reduce.4.cloned.1.call-update) | async-done | bytes 786448 | tf_op jit(solution)/shard_map/psum | solution.py:96
  339.0 2.9 fusion.9
  341.9 3.1 convolution_multiply_fusion.1
  345.0 2.5 fusion.6
  347.9 1.3 convolution_bitcast_fusion
  350.3 169.3 %all-reduce.5 = (bf16[256,1024]{0,1:T(8,128)(2,1)}, bf16[256,1024]{1,0:T(8,128)(2,1)}) all-reduce(f32[256,1024]{0,1:T(8,128)} %convolution_bitcast_fusion, f32[256,1024]{1,0:T(8,128)S(1)} %fusion.32), channel_id=1, replica_groups=mesh['node'=32,'feat'=16] {'node'}, use_global_device_ids=true, to_apply=%region_5.6 | all-reduce | flops 524288 | bytes 3145728 | tf_op jit(solution)/shard_map/psum | solution.py:105
  519.6 2.0 copy.17
  (147 shorter events, 23.3 us)
Async XLA Ops:
  7.2 331.8 %copy-start = (bf16[1024,1024]{1,0:T(8,128)(2,1)S(1)}, bf16[1024,1024]{1,0:T(8,128)(2,1)}, u32[]{:S(2)}) copy-start(bf16[1024,1024]{1,0:T(8,128)(2,1)} %param.23) | copy-start | bytes 6291460
  9.3 3.4 copy-start.1
  19.7 3.3 copy-start.1
  30.0 3.3 copy-start.1
  40.4 3.3 copy-start.1
  50.8 3.3 copy-start.1
  61.1 3.3 copy-start.1
  71.5 3.3 copy-start.1
  81.9 3.3 copy-start.1
  92.2 3.3 copy-start.1
  102.6 3.3 copy-start.1
  113.0 3.3 copy-start.1
  123.4 3.3 copy-start.1
  133.7 13.5 %copy-start.5 = (s32[192]{0:T(256)S(1)}, s32[192]{0:T(256)}, u32[]{:S(2)}) copy-start(s32[192]{0:T(256)} %param.18) | copy-start | bytes 2308
  133.7 13.5 %copy-start.2 = (bf16[192,256]{1,0:T(8,128)(2,1)S(1)}, bf16[192,256]{1,0:T(8,128)(2,1)}, u32[]{:S(2)}) copy-start(bf16[192,256]{1,0:T(8,128)(2,1)} %param.15) | copy-start | bytes 294916
  133.7 88.1 %all-to-all-start = ((bf16[32,192,256]{2,1,0:T(8,128)(2,1)}), bf16[32,192,256]{2,1,0:T(8,128)(2,1)}, u32[]{:S(2)}, u32[]{:S(2)}) async-start(bf16[32,192,256]{2,1,0:T(8,128)(2,1)} %bitcast.52), calls=%async_computation | async-start | bytes 6291456 | tf_op jit(solution)/shard_map/all_to_all | solution.py:87
  147.2 191.8 %all-reduce.4.cloned.1.call-start = ((), (), s32[]{:S(2)}) async-start(), calls=%async_computation.1 | async-start | bytes 1572864 | tf_op jit(solution)/shard_map/psum | solution.py:96
  148.6 77.9 %copy-start.4 = (s32[192]{0:T(256)S(1)}, s32[192]{0:T(256)}, u32[]{:S(2)}) copy-start(s32[192]{0:T(256)} %param.20) | copy-start | bytes 2308
  148.6 77.9 %copy-start.3 = (s32[192,10]{0,1:T(8,128)S(1)}, s32[192,10]{0,1:T(8,128)}, u32[]{:S(2)}) copy-start(s32[192,10]{0,1:T(8,128)} %param.19) | copy-start | bytes 23044
  227.3 114.6 %copy-start.6 = (bf16[1024,172]{0,1:T(8,128)(2,1)S(1)}, bf16[1024,172]{0,1:T(8,128)(2,1)}, u32[]{:S(2)}) copy-start(bf16[1024,172]{0,1:T(8,128)(2,1)} %param.24) | copy-start | bytes 1056772
  227.3 114.6 %copy-start.8 = (bf16[192,172]{0,1:T(8,128)(2,1)S(1)}, bf16[192,172]{0,1:T(8,128)(2,1)}, u32[]{:S(2)}) copy-start(bf16[192,172]{0,1:T(8,128)(2,1)} %param.25) | copy-start | bytes 198148
  345.0 4.2 copy-start.7
  345.0 4.2 copy-start.9
Sparse Core Ops, SparseCore 0:
  226.6 112.3 all-reduce.3
where the time goes:
time: 529 us; the launch traced here: 528 us
  waiting for transfers between devices  185 us (35%)
  blocking collectives  169 us (32%)
  local copies, waits for them, and re-layouts  112 us (21%)
  other arithmetic  18.3 us (3%)
  matrix products  14.8 us (3%)
  between operations  14.2 us (3%)
  starting transfers between devices  13.5 us (3%)
    psum x1, blocking collectives, body(): grad_self, grad_neigh = lax.psum((self_part, neigh_part), 'node')  169 us
    psum x1, waiting for transfers between devices, body(): pre_one = lax.psum(pre_part, 'feat')  112 us
    gather x48, local copies, waits for them, and re-layouts, slab_partial(): picked = table[index[:, slot]].astype(jnp.float32)  101 us
    all_to_all x1, waiting for transfers between devices, body(): lax.all_to_all(stacked, 'node', split_axis=0, concat_axis=0, tiled=True)  73.2 us
    all_to_all x1, starting transfers between devices, body(): lax.all_to_all(stacked, 'node', split_axis=0, concat_axis=0, tiled=True)  13.4 us
    dynamic_update_slice x12, other arithmetic, body(): lax.map(one_block, (index.reshape(total_rows // block, block, slot_total)...  12.7 us
  transfers between devices with their start and end apart: 2, of which 2 were waited for; matrix products, arithmetic and copies ran while one was open for 0% of the time, Pallas kernels for 0%

commit v1 on v0

--- a/solution.py
+++ b/solution.py
@@ -3,6 +3,8 @@
 import jax
 import jax.numpy as jnp
 from jax import lax
+from jax.experimental import pallas as pl
+from jax.experimental.pallas import tpu as pltpu
 from jax.sharding import PartitionSpec as P
 
 
@@ -11,12 +13,40 @@
     return gate + value * gate * (1.0 - gate)
 
 
+def gather_kernel(index_ref, count_ref, table_ref, out_ref):
+    slots, rows = index_ref.shape
+    nodes = table_ref.shape[0]
+    index = index_ref[...]
+    count = count_ref[...]
+    slot = lax.broadcasted_iota(jnp.int32, (slots, rows), 0)
+    live = jnp.where(slot < count, index, -1)
+    columns = jnp.concatenate([live, jnp.zeros((8 - slots, rows), jnp.int32)], axis=0).T
+    node = lax.broadcasted_iota(jnp.int32, (rows, nodes), 1)
+    hits = jnp.zeros((rows, nodes), jnp.float32)
+    for k in range(slots):
+        hits = hits + jnp.where(columns[:, k : k + 1] == node, 1.0, 0.0)
+    out_ref[...] = jnp.dot(
+        hits.astype(jnp.bfloat16), table_ref[...], preferred_element_type=jnp.float32
+    ).astype(jnp.bfloat16)
+
+
 def slab_partial(table, index, count):
-    running = jnp.zeros((index.shape[0], table.shape[1]), jnp.float32)
-    for slot in range(index.shape[1]):
-        picked = table[index[:, slot]].astype(jnp.float32)
-        running = running + jnp.where((count > slot)[:, None], picked, 0.0)
-    return running.astype(jnp.bfloat16)
+    slots, total = index.shape
+    block = math.gcd(total, 512)
+    nodes, width = table.shape
+    return pl.pallas_call(
+        gather_kernel,
+        grid=(total // block,),
+        in_specs=[
+            pl.BlockSpec((slots, block), lambda i: (0, i)),
+            pl.BlockSpec((1, block), lambda i: (0, i)),
+            pl.BlockSpec((nodes, width), lambda i: (0, 0)),
+        ],
+        out_specs=pl.BlockSpec((block, width), lambda i: (i, 0)),
+        out_shape=jax.ShapeDtypeStruct((total, width), jnp.bfloat16),
+        compiler_params=pltpu.CompilerParams(vmem_limit_bytes=32 * 1024 * 1024),
+        name="slab_partial",
+    )(index, count, table)
 
 
 def second_layer(first_hidden, local_index, local_count, weight_two, weight_three, cotangent):
@@ -50,6 +80,10 @@
     return (logits, grad_hidden)
 
 
+def exchange(pieces, axis):
+    return lax.all_to_all(pieces, axis, split_axis=0, concat_axis=0, tiled=True)
+
+
 def body(
     features,
     own_features,
@@ -64,46 +98,55 @@
     weight_three,
     cotangent,
 ):
-    index = neigh_index[0]
-    count = neigh_count[0]
-    total_rows = index.shape[0]
-    slot_total = index.shape[1]
-    block = math.gcd(total_rows, 512)
-
-    def one_block(group):
-        return slab_partial(features, group[0], group[1])
-
-    parts = lax.map(
-        one_block,
-        (
-            index.reshape(total_rows // block, block, slot_total),
-            count.reshape(total_rows // block, block),
-        ),
-    )
     groups = lax.axis_size("node")
-    own_rows = total_rows // groups
-    stacked = parts.reshape(groups, own_rows, features.shape[1])
+    splits = lax.axis_size("feat")
+    parts = slab_partial(features, neigh_index[0].T, neigh_count)
+    own_rows = parts.shape[0] // groups
+    width = features.shape[1]
     neighbour_sum = jnp.sum(
-        lax.all_to_all(stacked, "node", split_axis=0, concat_axis=0, tiled=True).astype(
-            jnp.float32
-        ),
-        axis=0,
+        exchange(parts.reshape(groups, own_rows, width), "node").astype(jnp.float32), axis=0
     )
     mean_rows = (neighbour_sum / degree[:, None].astype(jnp.float32)).astype(jnp.bfloat16)
     pre_part = jnp.dot(own_features, self_weight, preferred_element_type=jnp.float32) + jnp.dot(
         mean_rows, neigh_weight, preferred_element_type=jnp.float32
     )
-    pre_one = lax.psum(pre_part, "feat")
+    hidden = pre_part.shape[1]
+    halves = 2
+    tiles = splits // halves
+    pieces = (
+        pre_part.astype(jnp.bfloat16)
+        .reshape(halves, own_rows // halves, tiles, hidden // tiles)
+        .transpose(2, 0, 1, 3)
+        .reshape(splits, own_rows // halves, hidden // tiles)
+    )
+    pre_piece = jnp.sum(exchange(pieces, "feat").astype(jnp.float32), axis=0).astype(jnp.bfloat16)
+    pre_one = (
+        lax.all_gather(pre_piece, "feat", axis=0, tiled=False)
+        .reshape(tiles, halves, own_rows // halves, hidden // tiles)
+        .transpose(1, 2, 0, 3)
+        .reshape(own_rows, hidden)
+        .astype(jnp.float32)
+    )
     first_hidden = jax.nn.silu(pre_one).astype(jnp.bfloat16)
     slope_one = silu_slope(pre_one).astype(jnp.bfloat16)
     logits, grad_hidden = second_layer(
         first_hidden, local_index, local_count, weight_two, weight_three, cotangent
     )
     grad_pre_one = (grad_hidden * slope_one.astype(jnp.float32)).astype(jnp.bfloat16)
-    self_part = jnp.dot(own_features.T, grad_pre_one, preferred_element_type=jnp.float32)
-    neigh_part = jnp.dot(mean_rows.T, grad_pre_one, preferred_element_type=jnp.float32)
-    grad_self, grad_neigh = lax.psum((self_part, neigh_part), "node")
-    return (grad_self.astype(jnp.bfloat16), grad_neigh.astype(jnp.bfloat16), logits)
+    both = jnp.concatenate([own_features, mean_rows], axis=1)
+    grad_part = jnp.dot(both.T, grad_pre_one, preferred_element_type=jnp.float32).astype(
+        jnp.bfloat16
+    )
+    grad_piece = jnp.sum(
+        exchange(grad_part.reshape(groups, 2 * width // groups, hidden), "node").astype(
+            jnp.float32
+        ),
+        axis=0,
+    ).astype(jnp.bfloat16)
+    grads = exchange(
+        jnp.broadcast_to(grad_piece[None], (groups,) + grad_piece.shape), "node"
+    ).reshape(2 * width, hidden)
+    return (grads[:width], grads[width:], logits)
 
 
 def solution(mesh):

time: 529 us -> 223 us (0.42)
  the two profiles are of different devices: /device:TPU:24 before, /device:TPU:64 now
where the time goes in v1:
time: 223 us; the launch traced here: 222 us
  waiting for transfers between devices  110 us (49%)
  blocking collectives  54.3 us (24%)
  starting transfers between devices  25.6 us (11%)
  matrix products  10.3 us (5%)
  Pallas kernels  9.84 us (4%)
  local copies, waits for them, and re-layouts  7.93 us (4%)
  other arithmetic  3.52 us (2%)
    all_to_all x3, waiting for transfers between devices, exchange(): return lax.all_to_all(pieces, axis, split_axis=0, concat_axis=0, tiled=True)  110 us
    all_to_all x1, blocking collectives, exchange(): return lax.all_to_all(pieces, axis, split_axis=0, concat_axis=0, tiled=True)  37.9 us
    all_to_all x3, starting transfers between devices, exchange(): return lax.all_to_all(pieces, axis, split_axis=0, concat_axis=0, tiled=True)  25.6 us
    all_gather x1, blocking collectives, body(): lax.all_gather(pre_piece, 'feat', axis=0, tiled=False)  16.5 us
    pallas_call x1, Pallas kernels, slab_partial(): pl.pallas_call(gather_kernel, grid=(total // block,), in_specs=[pl.BlockS...  9.84 us
    unnamed x27, local copies, waits for them, and re-layouts  4.52 us
  transfers between devices with their start and end apart: 3, of which 3 were waited for; matrix products, arithmetic and copies ran while one was open for 1% of the time, Pallas kernels for 0%

profile of v1, /device:TPU:64, one launch (start us, length us, event | category | flops | bytes accessed | tf_op | source)
XLA Modules:
  0.0 222.0 jit_solution(5854091553816083467)
XLA Ops:
  0.6 0.0 copy-start
  0.6 0.0 copy-start.2
  0.7 1.1 copy-done.2
  1.7 0.0 copy-start.3
  1.7 0.9 copy-done.3
  2.6 0.0 copy-start.4
  2.6 0.7 copy-done.4
  3.4 9.8 %slab_partial.1 = bf16[6144,256]{1,0:T(8,128)(2,1)S(1)} custom-call(s32[4,6144]{1,0:T(4,128)S(1)} %bitcast.53, s32[1,6144]{1,0:T(1,128)S(1)} %copy-done.4, bf16[512,256]{1,0:T(8,128)(2,1)S(1)} %copy-done.2), custom_call_target="tpu_custom_call" | custom-call | tf_op jit(solution)/shard_map/slab_partial/pallas_call | solution.py:37
  13.2 0.0 copy-start.1
  13.2 1.7 copy-done.1
  14.9 0.0 copy-start.11
  14.9 0.0 copy-start.6
  14.9 0.0 copy-start.7
  14.9 12.8 %all-to-all-start = ((bf16[32,192,256]{2,1,0:T(8,128)(2,1)}), bf16[32,192,256]{2,1,0:T(8,128)(2,1)}, u32[]{:S(2)}, u32[]{:S(2)}) async-start(bf16[32,192,256]{2,1,0:T(8,128)(2,1)} %bitcast.52), calls=%async_computation | async-start | bytes 6291456 | tf_op jit(solution)/shard_map/all_to_all | solution.py:84
  27.7 0.0 copy-done.11
  27.7 0.0 copy-done.6
  27.7 0.0 copy-done.7
  27.7 0.3 fusion.36
  28.0 0.0 copy-start.5
  28.0 70.7 %all-to-all-done = bf16[32,192,256]{2,1,0:T(8,128)(2,1)} async-done(((bf16[32,192,256]{2,1,0:T(8,128)(2,1)}), bf16[32,192,256]{2,1,0:T(8,128)(2,1)}, u32[]{:S(2)}, u32[]{:S(2)}) %all-to-all-start) | async-done | bytes 3145760 | tf_op jit(solution)/shard_map/all_to_all | solution.py:84
  98.7 2.3 %convert_reduce_fusion = f32[192,256]{1,0:T(8,128)S(1)} fusion(bf16[32,192,256]{2,1,0:T(8,128)(2,1)} %all-to-all-done), kind=kLoop, calls=%fused_computation | loop fusion | flops 3096576 | bytes 3342336 | tf_op jit(solution)/shard_map/reduce_sum | solution.py:106
  101.1 0.1 divide_convert_fusion
  101.2 0.0 copy-done.5
  101.2 0.0 copy-start.10
  101.2 0.0 copy-start.9
  101.2 0.3 fusion.6
  101.5 0.1 copy.21
  101.6 0.8 copy.19
  102.4 7.2 %all-to-all-start.1 = ((bf16[16,96,128]{2,1,0:T(8,128)(2,1)}), bf16[16,96,128]{2,1,0:T(8,128)(2,1)S(1)}, u32[]{:S(2)}, u32[]{:S(2)}) async-start(bf16[16,96,128]{2,1,0:T(8,128)(2,1)} %bitcast.4), calls=%async_computation.1 | async-start | bytes 786432 | tf_op jit(solution)/shard_map/all_to_all | solution.py:84
  109.6 0.0 copy-done.10
  109.6 0.0 copy-done.9
  109.6 0.8 convert_reduce_fusion.1
  110.4 12.9 %all-to-all-done.1 = bf16[16,96,128]{2,1,0:T(8,128)(2,1)S(1)} async-done(((bf16[16,96,128]{2,1,0:T(8,128)(2,1)}), bf16[16,96,128]{2,1,0:T(8,128)(2,1)S(1)}, u32[]{:S(2)}, u32[]{:S(2)}) %all-to-all-start.1) | async-done | bytes 393248 | tf_op jit(solution)/shard_map/all_to_all | solution.py:84
  123.3 0.1 reduce_sum.44
  123.3 16.5 %all-gather = bf16[1536,128]{1,0:T(8,128)(2,1)S(1)} all-gather(bf16[96,128]{1,0:T(8,128)(2,1)S(1)} %reduce_sum.44), channel_id=2, replica_groups=mesh['node'=32,'feat'=16] {'feat'}, dimensions={0}, use_global_device_ids=true | all-gather | bytes 417792 | tf_op jit(solution)/shard_map/all_gather | solution.py:124
  139.8 0.1 convert_bitcast_fusion
  139.9 0.5 copy.20
  140.4 0.0 copy-done
  140.4 0.0 copy-start.12
  140.4 1.8 fusion.5
  142.1 0.0 copy-done.12
  142.1 3.1 %convolution_multiply_fusion.1 = f32[192,1024]{1,0:T(8,128)} fusion(bf16[1024,1024]{1,0:T(8,128)(2,1)S(1)} %copy-done, bf16[192,172]{0,1:T(8,128)(2,1)} %param.23, bf16[1024,172]{0,1:T(8,128)(2,1)S(1)} %copy-done.12, f32[192,1024]{1,0:T(8,128)} %fusion.5, f32[192]{0:T(256)S(1)} %add_divide_fusion.2), kind=kOutput, calls=%fused_computation.6 | convolution fusion | flops 472252416 | bytes 4089088 | tf_op jit(solution)/shard_map/dot_general | solution.py:75
  145.3 0.0 copy-start.8
  145.3 2.2 fusion.1
  147.5 0.0 copy-done.8
  147.5 0.5 convolution_convert_fusion
  148.0 37.9 %all_to_all.20 = bf16[32,16,1024]{2,1,0:T(8,128)(2,1)S(1)} all-to-all(bf16[32,16,1024]{2,1,0:T(8,128)(2,1)S(1)} %bitcast.54), channel_id=1, replica_groups=mesh['node'=32,'feat'=16] {'node'}, dimensions={0} | all-to-all | bytes 2097152 | tf_op jit(solution)/shard_map/all_to_all | solution.py:84
  185.8 0.2 reduce_sum.45
  186.0 1.1 broadcast_in_dim.2
  187.1 5.6 %all-to-all-start.3 = ((bf16[32,16,1024]{2,1,0:T(8,128)(2,1)}), bf16[32,16,1024]{2,1,0:T(8,128)(2,1)S(1)}, u32[]{:S(2)}, u32[]{:S(2)}) async-start(bf16[32,16,1024]{2,1,0:T(8,128)(2,1)} %broadcast_in_dim.2), calls=%async_computation.3 | async-start | bytes 2097152 | tf_op jit(solution)/shard_map/all_to_all | solution.py:84
  192.7 2.2 convolution_convert_fusion.1
  194.9 26.1 %all-to-all-done.3 = bf16[32,16,1024]{2,1,0:T(8,128)(2,1)S(1)} async-done(((bf16[32,16,1024]{2,1,0:T(8,128)(2,1)}), bf16[32,16,1024]{2,1,0:T(8,128)(2,1)S(1)}, u32[]{:S(2)}, u32[]{:S(2)}) %all-to-all-start.3) | async-done | bytes 1048608 | tf_op jit(solution)/shard_map/all_to_all | solution.py:84
  220.9 1.0 fusion.35
  (3 shorter events, 0.0 us)
Async XLA Ops:
  0.6 139.7 %copy-start = (bf16[1024,1024]{1,0:T(8,128)(2,1)S(1)}, bf16[1024,1024]{1,0:T(8,128)(2,1)}, u32[]{:S(2)}) copy-start(bf16[1024,1024]{1,0:T(8,128)(2,1)} %param.21) | copy-start | bytes 6291460
  0.6 1.1 copy-start.2
  1.7 0.9 copy-start.3
  2.6 0.7 copy-start.4
  13.2 1.7 copy-start.1
  14.9 12.8 %copy-start.11 = (s32[192]{0:T(256)S(1)}, s32[192]{0:T(256)}, u32[]{:S(2)}) copy-start(s32[192]{0:T(256)} %param.16) | copy-start | bytes 2308
  14.9 12.8 %copy-start.6 = (bf16[256,1024]{1,0:T(8,128)(2,1)S(1)}, bf16[256,1024]{1,0:T(8,128)(2,1)}, u32[]{:S(2)}) copy-start(bf16[256,1024]{1,0:T(8,128)(2,1)} %param.19) | copy-start | bytes 1572868
  14.9 12.8 %copy-start.7 = (bf16[192,256]{1,0:T(8,128)(2,1)S(1)}, bf16[192,256]{1,0:T(8,128)(2,1)}, u32[]{:S(2)}) copy-start(bf16[192,256]{1,0:T(8,128)(2,1)} %param.13) | copy-start | bytes 294916
  14.9 83.8 %all-to-all-start = ((bf16[32,192,256]{2,1,0:T(8,128)(2,1)}), bf16[32,192,256]{2,1,0:T(8,128)(2,1)}, u32[]{:S(2)}, u32[]{:S(2)}) async-start(bf16[32,192,256]{2,1,0:T(8,128)(2,1)} %bitcast.52), calls=%async_computation | async-start | bytes 6291456 | tf_op jit(solution)/shard_map/all_to_all | solution.py:84
  28.0 73.2 %copy-start.5 = (bf16[256,1024]{1,0:T(8,128)(2,1)S(1)}, bf16[256,1024]{1,0:T(8,128)(2,1)}, u32[]{:S(2)}) copy-start(bf16[256,1024]{1,0:T(8,128)(2,1)} %param.20) | copy-start | bytes 1572868
  101.2 8.4 %copy-start.10 = (s32[192]{0:T(256)S(1)}, s32[192]{0:T(256)}, u32[]{:S(2)}) copy-start(s32[192]{0:T(256)} %param.18) | copy-start | bytes 2308
  101.2 8.4 %copy-start.9 = (s32[192,10]{0,1:T(8,128)S(1)}, s32[192,10]{0,1:T(8,128)}, u32[]{:S(2)}) copy-start(s32[192,10]{0,1:T(8,128)} %param.17) | copy-start | bytes 23044
  102.4 20.9 %all-to-all-start.1 = ((bf16[16,96,128]{2,1,0:T(8,128)(2,1)}), bf16[16,96,128]{2,1,0:T(8,128)(2,1)S(1)}, u32[]{:S(2)}, u32[]{:S(2)}) async-start(bf16[16,96,128]{2,1,0:T(8,128)(2,1)} %bitcast.4), calls=%async_computation.1 | async-start | bytes 786432 | tf_op jit(solution)/shard_map/all_to_all | solution.py:84
  140.4 1.8 copy-start.12
  145.3 2.2 copy-start.8
  187.1 33.9 %all-to-all-start.3 = ((bf16[32,16,1024]{2,1,0:T(8,128)(2,1)}), bf16[32,16,1024]{2,1,0:T(8,128)(2,1)S(1)}, u32[]{:S(2)}, u32[]{:S(2)}) async-start(bf16[32,16,1024]{2,1,0:T(8,128)(2,1)} %broadcast_in_dim.2), calls=%async_computation.3 | async-start | bytes 2097152 | tf_op jit(solution)/shard_map/all_to_all | solution.py:84

commit v2 on v0

v2 whole, which is shorter than its diff:
```python
import functools

import jax
import jax.numpy as jnp
from jax import lax
from jax.experimental import pallas as pl
from jax.experimental.pallas import tpu as pltpu
from jax.sharding import Mesh
from jax.sharding import PartitionSpec as P

XS = 4
ROW_BLOCK = 256
DEAD = 512.0
PARAMS = pltpu.CompilerParams(vmem_limit_bytes=48 * 1024 * 1024)
NODE = ("x", "z")
FEAT = ("y", "c")


def silu_slope(value):
    gate = jax.nn.sigmoid(value)
    return gate + value * gate * (1.0 - gate)


def dot(a, b, dims=((1,), (0,))):
    return lax.dot_general(a, b, (dims, ((), ())), preferred_element_type=jnp.float32)


def payload_kernel(place_ref, index_ref, count_ref, table_ref, *refs):
    outs, coded = refs[:-1], refs[-1]
    slots, total = index_ref.shape
    nodes = table_ref.shape[0]
    per_x = total // XS
    blocks = per_x // ROW_BLOCK
    index = index_ref[...]
    slot = lax.broadcasted_iota(jnp.int32, (slots, total), 0)
    code = jnp.where(index < 256, index, 255 - index).astype(jnp.float32)
    code = jnp.where(slot < count_ref[...], code, DEAD)
    extra = coded.shape[1] - slots * blocks
    for x in range(XS):
        pieces = [
            code[:, (x * blocks + c) * ROW_BLOCK : (x * blocks + c + 1) * ROW_BLOCK]
            for c in range(blocks)
        ] + [jnp.full((extra, ROW_BLOCK), DEAD, jnp.float32)]
        coded[x] = jnp.concatenate(pieces, axis=0).astype(jnp.bfloat16)
    for shift in range(XS):
        out = outs[shift]
        out[0:nodes, :] = table_ref[...]
        out[nodes:, :] = coded[lax.rem(place_ref[0] + shift, XS)]


def make_payloads(place, index, count, table):
    slots, total = index.shape
    nodes, width = table.shape
    used = slots * (total // XS // ROW_BLOCK)
    extra = -(-used // 16) * 16
    vmem = pl.BlockSpec(memory_space=pltpu.VMEM)
    return pl.pallas_call(
        payload_kernel,
        in_specs=[pl.BlockSpec(memory_space=pltpu.SMEM), vmem, vmem, vmem],
        out_specs=[vmem] * XS,
        out_shape=[jax.ShapeDtypeStruct((nodes + extra, width), jnp.bfloat16)] * XS,
        scratch_shapes=[pltpu.VMEM((XS, extra, ROW_BLOCK), jnp.bfloat16)],
        compiler_params=PARAMS,
        name="payloads",
    )(place, index, count, table)


def gather_kernel(slots, carried, *refs):
    payloads, out_ref = refs[carried:-1], refs[-1]
    blocks = out_ref.shape[0] // ROW_BLOCK
    extra = -(-slots * blocks // 16) * 16
    nodes = payloads[0].shape[0] - extra
    lane = lax.broadcasted_iota(jnp.int32, (ROW_BLOCK, nodes), 1)
    node_code = jnp.where(lane < 256, lane, 255 - lane).astype(jnp.float32).astype(jnp.bfloat16)
    one = jnp.ones((), jnp.bfloat16)
    zero = jnp.zeros((), jnp.bfloat16)
    codes = [ref[nodes:, :].astype(jnp.float32).T.astype(jnp.bfloat16) for ref in payloads]
    for c in range(blocks):
        rows = slice(c * ROW_BLOCK, (c + 1) * ROW_BLOCK)
        total = refs[0][rows, :].astype(jnp.float32) if carried else None
        for ref, code in zip(payloads, codes):
            hits = None
            for k in range(slots):
                column = slots * c + k
                hit = jnp.where(code[:, column : column + 1] == node_code, one, zero)
                hits = hit if hits is None else hits + hit
            part = dot(hits, ref[0:nodes, :])
            total = part if total is None else total + part
        out_ref[rows, :] = total.astype(out_ref.dtype)


def gather_sum(slots, rows, dtype, carried, payloads):
    width = payloads[0].shape[1]
    operands = ([carried] if carried is not None else []) + list(payloads)
    vmem = pl.BlockSpec(memory_space=pltpu.VMEM)
    return pl.pallas_call(
        functools.partial(gather_kernel, slots, int(carried is not None)),
        in_specs=[vmem] * len(operands),
        out_specs=vmem,
        out_shape=jax.ShapeDtypeStruct((rows, width), dtype),
        compiler_params=PARAMS,
        name="gather_sum",
    )(*operands)


def first_kernel(recv_ref, degree_ref, own_ref, self_ref, neigh_ref, mean_ref, out_ref):
    sums = recv_ref[0].astype(jnp.float32)
    for i in range(1, recv_ref.shape[0]):
        sums = sums + recv_ref[i].astype(jnp.float32)
    mean = (sums / degree_ref[...]).astype(jnp.bfloat16)
    mean_ref[...] = mean
    pre = (dot(own_ref[...], self_ref[...]) + dot(mean, neigh_ref[...])).astype(jnp.bfloat16)
    count, height, width = out_ref.shape
    halves = pre.shape[0] // height
    for i in range(count):
        t, h = i // halves, i % halves
        out_ref[i] = pre[h * height : (h + 1) * height, t * width : (t + 1) * width]


def first_layer(recv, degree, own, self_weight, neigh_weight, pieces):
    rows, width = own.shape
    hidden = self_weight.shape[1]
    vmem = pl.BlockSpec(memory_space=pltpu.VMEM)
    return pl.pallas_call(
        first_kernel,
        in_specs=[vmem] * 5,
        out_specs=[vmem] * 2,
        out_shape=[
            jax.ShapeDtypeStruct((rows, width), jnp.bfloat16),
            jax.ShapeDtypeStruct((pieces, rows // 2, 2 * hidden // pieces), jnp.bfloat16),
        ],
        compiler_params=PARAMS,
        name="first_layer",
    )(recv, degree, own, self_weight, neigh_weight)


def second_kernel(pre_ref, adj_ref, inv_ref, two_ref, back_ref, own_ref, mean_ref, hidden_ref, grad_ref):
    count, height, width = pre_ref.shape
    halves = inv_ref.shape[0] // height
    strips = [
        jnp.concatenate([pre_ref[t * halves + h] for h in range(halves)], axis=0)
        for t in range(count // halves)
    ]
    pre = jnp.concatenate(strips, axis=1).astype(jnp.float32)
    gate = jax.nn.sigmoid(pre)
    first_hidden = (pre * gate).astype(jnp.bfloat16)
    slope = (gate + pre * gate * (1.0 - gate)).astype(jnp.bfloat16).astype(jnp.float32)
    adjacency = adj_ref[...]
    inv = inv_ref[...]
    mixed = (dot(adjacency, first_hidden) * inv).astype(jnp.bfloat16)
    pre_two = dot(mixed, two_ref[...])
    gate_two = jax.nn.sigmoid(pre_two)
    hidden_ref[...] = (pre_two * gate_two).astype(jnp.bfloat16)
    slope_two = gate_two + pre_two * gate_two * (1.0 - gate_two)
    grad_two = (back_ref[...] * slope_two).astype(jnp.bfloat16)
    grad_mixed = dot(grad_two, two_ref[...], ((1,), (1,))) * inv
    high = grad_mixed.astype(jnp.bfloat16)
    rest = grad_mixed - high.astype(jnp.float32)
    middle = rest.astype(jnp.bfloat16)
    low = (rest - middle.astype(jnp.float32)).astype(jnp.bfloat16)
    down = ((0,), (0,))
    grad_hidden = dot(adjacency, high, down) + (
        dot(adjacency, middle, down) + dot(adjacency, low, down)
    )
    grad_one = (grad_hidden * slope).astype(jnp.bfloat16)
    width_in = own_ref.shape[1]
    grad_ref[0:width_in, :] = dot(own_ref[...], grad_one, down).astype(jnp.bfloat16)
    grad_ref[width_in:, :] = dot(mean_ref[...], grad_one, down).astype(jnp.bfloat16)


def second_layer(pre, adjacency, inv_count, weight_two, back_two, own, mean):
    rows, width = own.shape
    hidden = weight_two.shape[0]
    vmem = pl.BlockSpec(memory_space=pltpu.VMEM)
    return pl.pallas_call(
        second_kernel,
        in_specs=[vmem] * 7,
        out_specs=[vmem] * 2,
        out_shape=[
            jax.ShapeDtypeStruct((rows, hidden), jnp.bfloat16),
            jax.ShapeDtypeStruct((2 * width, hidden), jnp.bfloat16),
        ],
        compiler_params=PARAMS,
        name="second_layer",
    )(pre, adjacency, inv_count, weight_two, back_two, own, mean)


def spread_kernel(recv_ref, out_ref):
    sums = recv_ref[0].astype(jnp.float32)
    for i in range(1, recv_ref.shape[0]):
        sums = sums + recv_ref[i].astype(jnp.float32)
    piece = sums.astype(jnp.bfloat16)
    for i in range(recv_ref.shape[0]):
        out_ref[i] = piece


def spread(recv):
    vmem = pl.BlockSpec(memory_space=pltpu.VMEM)
    return pl.pallas_call(
        spread_kernel,
        in_specs=[vmem],
        out_specs=vmem,
        out_shape=jax.ShapeDtypeStruct(recv.shape, recv.dtype),
        compiler_params=PARAMS,
        name="sum_and_spread",
    )(recv)


def exchange(pieces, axis):
    return lax.all_to_all(pieces, axis, split_axis=0, concat_axis=0, tiled=True)


def body(
    features,
    own_features,
    neigh_index,
    neigh_count,
    degree,
    local_index,
    local_count,
    self_weight,
    neigh_weight,
    weight_two,
    weight_three,
    cotangent,
):
    groups = lax.axis_size(NODE)
    splits = lax.axis_size(FEAT)
    own_rows, width = own_features.shape
    slots = neigh_index.shape[2]
    per_x = own_rows * (groups // XS)

    place = lax.axis_index("x").reshape(1).astype(jnp.int32)
    payloads = make_payloads(place, neigh_index[0].T, neigh_count, features)
    arrived = [
        lax.ppermute(payloads[s], "x", [(i, (i + s) % XS) for i in range(XS)]) for s in (2, 1, 3)
    ]
    running = gather_sum(slots, per_x, jnp.float32, None, payloads[:1])
    running = gather_sum(slots, per_x, jnp.float32, running, arrived[1:])
    parts = gather_sum(slots, per_x, jnp.bfloat16, running, arrived[:1])
    recv = exchange(parts.reshape(groups // XS, own_rows, width), "z")
    mean_rows, pieces = first_layer(
        recv,
        degree[:, None].astype(jnp.float32),
        own_features,
        self_weight,
        neigh_weight,
        splits,
    )
    pre_piece = jnp.sum(exchange(pieces, FEAT).astype(jnp.float32), axis=0).astype(jnp.bfloat16)
    pre = lax.all_gather(pre_piece, FEAT, axis=0, tiled=False)

    slot_ids = jnp.arange(local_index.shape[1], dtype=jnp.int32)
    live_slots = slot_ids[None, :] < local_count[:, None]
    slot_hits = (
        local_index[:, :, None] == jnp.arange(own_rows, dtype=jnp.int32)[None, None, :]
    ) & live_slots[:, :, None]
    adjacency = (
        jnp.sum(slot_hits.astype(jnp.float32), axis=1) + jnp.eye(own_rows, dtype=jnp.float32)
    ).astype(jnp.bfloat16)
    inv_count = 1.0 / (1.0 + local_count.astype(jnp.float32))
    back_two = dot(cotangent, weight_three, ((1,), (1,)))
    second_hidden, grad_part = second_layer(
        pre, adjacency, inv_count[:, None], weight_two, back_two, own_features, mean_rows
    )
    grad_recv = exchange(grad_part.reshape(groups, -1, grad_part.shape[1]), NODE)
    grads = exchange(spread(grad_recv), NODE).reshape(grad_part.shape)
    logits = dot(second_hidden, weight_three).astype(jnp.bfloat16)
    return (grads[:width], grads[width:], logits)


def solution(mesh):
    nodes, feats = mesh.devices.shape
    fine = Mesh(mesh.devices.reshape(XS, nodes // XS, feats // 2, 2), ("x", "z", "y", "c"))
    in_specs = (
        P(NODE, FEAT),
        P(NODE, FEAT),
        P(NODE, None, None),
        P(NODE, None),
        P(NODE),
        P(NODE, None),
        P(NODE),
        P(FEAT, None),
        P(FEAT, None),
        P(),
        P(),
        P(NODE, None),
    )
    out_specs = (P(FEAT, None), P(FEAT, None), P(NODE, None))
    return jax.shard_map(body, mesh=fine, in_specs=in_specs, out_specs=out_specs, check_vma=False)
```

time: 529 us -> 172 us (0.33)
  the two profiles are of different devices: /device:TPU:24 before, /device:TPU:64 now
where the time goes in v2:
time: 172 us; the launch traced here: 171 us
  waiting for transfers between devices  64.1 us (37%)
  blocking collectives  51.8 us (30%)
  starting transfers between devices  33.9 us (20%)
  Pallas kernels  9.31 us (5%)
  local copies, waits for them, and re-layouts  6.22 us (4%)
  other arithmetic  2.48 us (1%)
  matrix products  2.09 us (1%)
    all_to_all x3, waiting for transfers between devices, exchange(): return lax.all_to_all(pieces, axis, split_axis=0, concat_axis=0, tiled=True)  57.2 us
    all_to_all x1, blocking collectives, exchange(): return lax.all_to_all(pieces, axis, split_axis=0, concat_axis=0, tiled=True)  35.1 us
    all_to_all x3, starting transfers between devices, exchange(): return lax.all_to_all(pieces, axis, split_axis=0, concat_axis=0, tiled=True)  23.1 us
    all_gather x1, blocking collectives, body(): pre = lax.all_gather(pre_piece, FEAT, axis=0, tiled=False)  16.7 us
    ppermute x3, starting transfers between devices, body(): lax.ppermute(payloads[s], 'x', [(i, (i + s) % XS) for i in range(XS)])  10.8 us
    ppermute x3, waiting for transfers between devices, body(): lax.ppermute(payloads[s], 'x', [(i, (i + s) % XS) for i in range(XS)])  6.88 us
    unnamed x30, local copies, waits for them, and re-layouts  4.94 us
    pallas_call x3, Pallas kernels, gather_sum(): pl.pallas_call(functools.partial(gather_kernel, slots, int(carried is not...  4.47 us
  transfers between devices with their start and end apart: 6, of which 4 were waited for; matrix products, arithmetic and copies ran while one was open for 2% of the time, Pallas kernels for 1%

profile of v2, /device:TPU:64, one launch (start us, length us, event | category | flops | bytes accessed | tf_op | source)
XLA Modules:
  0.0 170.8 jit_solution(6396913355922892331)
XLA Ops:
  0.6 0.0 copy-start
  0.7 0.0 copy-start.7
  0.7 1.0 copy-done.7
  1.6 0.0 copy-start.8
  1.7 0.9 copy-done.8
  2.5 0.0 copy-start.11
  2.5 0.7 copy-done.11
  3.3 0.1 payloads.1
  3.4 3.4 %collective-permute-start = (bf16[544,256]{1,0:T(8,128)(2,1)S(1)}, bf16[544,256]{1,0:T(8,128)(2,1)S(1)}, u32[]{:S(2)}, u32[]{:S(2)}) collective-permute-start(bf16[544,256]{1,0:T(8,128)(2,1)S(1)} %get-tuple-element.12), channel_id=1, source_target_pairs={{0,128},{128,256},{256,384},{384,0},{1,129},{129,257},{257,385},{3... | collective-permute-start | bytes 835592 | tf_op jit(solution)/shard_map/ppermute | solution.py:236
  6.8 3.7 %collective-permute-start.1 = (bf16[544,256]{1,0:T(8,128)(2,1)S(1)}, bf16[544,256]{1,0:T(8,128)(2,1)S(1)}, u32[]{:S(2)}, u32[]{:S(2)}) collective-permute-start(bf16[544,256]{1,0:T(8,128)(2,1)S(1)} %get-tuple-element.13), channel_id=1, source_target_pairs={{0,384},{128,0},{256,128},{384,256},{1,385},{129,1},{257,129},{385... | collective-permute-start | bytes 835592 | tf_op jit(solution)/shard_map/ppermute | solution.py:236
  10.4 3.7 %collective-permute-start.2 = (bf16[544,256]{1,0:T(8,128)(2,1)S(1)}, bf16[544,256]{1,0:T(8,128)(2,1)S(1)}, u32[]{:S(2)}, u32[]{:S(2)}) collective-permute-start(bf16[544,256]{1,0:T(8,128)(2,1)S(1)} %get-tuple-element.14), channel_id=1, source_target_pairs={{0,256},{128,384},{256,0},{384,128},{1,257},{129,385},{257,1},{385... | collective-permute-start | bytes 835592 | tf_op jit(solution)/shard_map/ppermute | solution.py:236
  14.2 1.0 gather_sum.3.refs_0_
  15.2 0.0 collective-permute-done.refs_1_
  15.2 6.9 %collective-permute-done.1.refs_2_ = bf16[544,256]{1,0:T(8,128)(2,1)S(1)} collective-permute-done((bf16[544,256]{1,0:T(8,128)(2,1)S(1)}, bf16[544,256]{1,0:T(8,128)(2,1)S(1)}, u32[]{:S(2)}, u32[]{:S(2)}) %collective-permute-start.1) | collective-permute-done | bytes 278560 | tf_op jit(solution)/shard_map/ppermute | solution.py:236
  22.1 1.6 gather_sum.4.refs_0_
  23.6 0.0 copy-start.14
  23.6 0.0 copy-start.13
  23.6 0.0 copy-start.2
  23.7 0.0 copy-start.3
  23.7 0.0 copy-start.4
  23.7 0.0 collective-permute-done.2.refs_1_
  23.7 1.9 %gather_sum.5 = bf16[1536,256]{1,0:T(8,128)(2,1)} custom-call(f32[1536,256]{1,0:T(8,128)S(1)} %gather_sum.4.refs_0_, bf16[544,256]{1,0:T(8,128)(2,1)S(1)} %collective-permute-done.2.refs_1_), custom_call_target="tpu_custom_call" | custom-call | tf_op jit(solution)/shard_map/gather_sum/pallas_call | solution.py:96
  25.6 0.0 copy-start.12
  25.6 10.1 %all-to-all-start = ((bf16[8,192,256]{2,1,0:T(8,128)(2,1)}), bf16[8,192,256]{2,1,0:T(8,128)(2,1)S(1)}, u32[]{:S(2)}, u32[]{:S(2)}) async-start(bf16[8,192,256]{2,1,0:T(8,128)(2,1)} %bitcast.3), calls=%async_computation | async-start | bytes 1572864 | tf_op jit(solution)/shard_map/all_to_all | solution.py:210
  35.7 0.0 copy-done.14
  35.7 0.1 copy.19.degree_ref
  35.8 0.0 copy-done.13
  35.9 18.3 %all-to-all-done.recv_ref = bf16[8,192,256]{2,1,0:T(8,128)(2,1)S(1)} async-done(((bf16[8,192,256]{2,1,0:T(8,128)(2,1)}), bf16[8,192,256]{2,1,0:T(8,128)(2,1)S(1)}, u32[]{:S(2)}, u32[]{:S(2)}) %all-to-all-start) | async-done | bytes 786464 | tf_op jit(solution)/shard_map/all_to_all | solution.py:210
  54.2 0.0 copy-done.2
  54.2 0.0 copy-done.3
  54.2 0.0 copy-done.4
  54.2 1.2 first_layer.1
  55.4 0.0 copy-start.9
  55.4 0.6 copy-done.9
  56.0 0.0 copy-start.1
  56.0 7.4 %all-to-all-start.1 = ((bf16[16,96,128]{2,1,0:T(8,128)(2,1)}), bf16[16,96,128]{2,1,0:T(8,128)(2,1)}, u32[]{:S(2)}, u32[]{:S(2)}) async-start(bf16[16,96,128]{2,1,0:T(8,128)(2,1)} %get-tuple-element.15), calls=%async_computation.1 | async-start | bytes 786432 | tf_op jit(solution)/shard_map/all_to_all | solution.py:210
  63.4 0.1 copy.20.inv_ref
  63.5 0.0 copy-done.12
  63.6 0.8 convert_reduce_fusion
  64.4 0.0 copy-done
  64.4 1.2 fusion.2.back_ref
  65.6 11.6 %all-to-all-done.1 = bf16[16,96,128]{2,1,0:T(8,128)(2,1)} async-done(((bf16[16,96,128]{2,1,0:T(8,128)(2,1)}), bf16[16,96,128]{2,1,0:T(8,128)(2,1)}, u32[]{:S(2)}, u32[]{:S(2)}) %all-to-all-start.1) | async-done | bytes 393248 | tf_op jit(solution)/shard_map/all_to_all | solution.py:210
  77.2 1.7 reduce_sum.21
  78.8 16.7 %all-gather = bf16[1536,128]{1,0:T(8,128)(2,1)S(1)} all-gather(bf16[96,128]{1,0:T(8,128)(2,1)} %reduce_sum.21), channel_id=2, replica_groups=mesh['x'=4,'z'=8,'y'=8,'c'=2] {'y','c'}, dimensions={0}, use_global_device_ids=true | all-gather | bytes 417792 | tf_op jit(solution)/shard_map/all_gather | solution.py:251
  95.5 0.0 copy-done.1
  95.5 0.0 copy-start.10
  95.5 0.9 copy-done.10
  96.4 2.3 %second_layer.1 = (bf16[192,1024]{1,0:T(8,128)(2,1)S(1)}, bf16[512,1024]{1,0:T(8,128)(2,1)S(1)}) custom-call(bf16[16,96,128]{2,1,0:T(8,128)(2,1)S(1)} %bitcast.15, bf16[192,192]{1,0:T(8,128)(2,1)S(1)} %add_convert_fusion.adj_ref, f32[192,1]{1,0:T(8,128)S(1)} %copy.20.inv_ref, bf16[1024,1024]{1,0:T(8,128)(2,1)S(1)} %copy-done.1, ...), custom_call_target="tpu_custom_call" | custom-call | tf_op jit(solution)/shard_map/second_layer/pallas_call | solution.py:175
  98.8 0.0 copy-start.5
  98.8 0.7 copy-done.5
  99.5 35.1 %all_to_all.20.recv_ref = bf16[32,16,1024]{2,1,0:T(8,128)(2,1)S(1)} all-to-all(bf16[32,16,1024]{2,1,0:T(8,128)(2,1)S(1)} %bitcast.16), channel_id=1, replica_groups=mesh['x'=4,'z'=8,'y'=8,'c'=2] {'x','z'}, dimensions={0} | all-to-all | bytes 2097152 | tf_op jit(solution)/shard_map/all_to_all | solution.py:210
  134.6 0.0 copy-start.6
  134.6 1.2 sum_and_spread.1
  135.9 5.6 %all-to-all-start.3 = ((bf16[32,16,1024]{2,1,0:T(8,128)(2,1)}), bf16[32,16,1024]{2,1,0:T(8,128)(2,1)S(1)}, u32[]{:S(2)}, u32[]{:S(2)}) async-start(bf16[32,16,1024]{2,1,0:T(8,128)(2,1)} %sum_and_spread.1), calls=%async_computation.3 | async-start | bytes 2097152 | tf_op jit(solution)/shard_map/all_to_all | solution.py:210
  141.5 0.0 copy-done.6
  141.5 0.9 convolution_convert_fusion
  142.4 27.3 %all-to-all-done.3 = bf16[32,16,1024]{2,1,0:T(8,128)(2,1)S(1)} async-done(((bf16[32,16,1024]{2,1,0:T(8,128)(2,1)}), bf16[32,16,1024]{2,1,0:T(8,128)(2,1)S(1)}, u32[]{:S(2)}, u32[]{:S(2)}) %all-to-all-start.3) | async-done | bytes 1048608 | tf_op jit(solution)/shard_map/all_to_all | solution.py:210
  169.7 1.0 fusion.1
  (4 shorter events, 0.0 us)
Async XLA Ops:
  0.6 63.7 %copy-start = (bf16[1024,172]{0,1:T(8,128)(2,1)S(1)}, bf16[1024,172]{0,1:T(8,128)(2,1)}, u32[]{:S(2)}) copy-start(bf16[1024,172]{0,1:T(8,128)(2,1)} %param.22) | copy-start | bytes 1056772
  0.7 1.0 copy-start.7
  1.6 0.9 copy-start.8
  2.5 0.7 copy-start.11
  3.4 11.8 %collective-permute-start = (bf16[544,256]{1,0:T(8,128)(2,1)S(1)}, bf16[544,256]{1,0:T(8,128)(2,1)S(1)}, u32[]{:S(2)}, u32[]{:S(2)}) collective-permute-start(bf16[544,256]{1,0:T(8,128)(2,1)S(1)} %get-tuple-element.12), channel_id=1, source_target_pairs={{0,128},{128,256},{256,384},{384,0},{1,129},{129,257},{257,385},{3... | collective-permute-start | bytes 835592 | tf_op jit(solution)/shard_map/ppermute | solution.py:236
  6.8 15.3 %collective-permute-start.1 = (bf16[544,256]{1,0:T(8,128)(2,1)S(1)}, bf16[544,256]{1,0:T(8,128)(2,1)S(1)}, u32[]{:S(2)}, u32[]{:S(2)}) collective-permute-start(bf16[544,256]{1,0:T(8,128)(2,1)S(1)} %get-tuple-element.13), channel_id=1, source_target_pairs={{0,384},{128,0},{256,128},{384,256},{1,385},{129,1},{257,129},{385... | collective-permute-start | bytes 835592 | tf_op jit(solution)/shard_map/ppermute | solution.py:236
  10.4 13.2 %collective-permute-start.2 = (bf16[544,256]{1,0:T(8,128)(2,1)S(1)}, bf16[544,256]{1,0:T(8,128)(2,1)S(1)}, u32[]{:S(2)}, u32[]{:S(2)}) collective-permute-start(bf16[544,256]{1,0:T(8,128)(2,1)S(1)} %get-tuple-element.14), channel_id=1, source_target_pairs={{0,256},{128,384},{256,0},{384,128},{1,257},{129,385},{257,1},{385... | collective-permute-start | bytes 835592 | tf_op jit(solution)/shard_map/ppermute | solution.py:236
  23.6 12.1 %copy-start.14 = (s32[192]{0:T(256)S(1)}, s32[192]{0:T(256)}, u32[]{:S(2)}) copy-start(s32[192]{0:T(256)} %param.16) | copy-start | bytes 2308
  23.6 12.2 %copy-start.13 = (s32[192]{0:T(256)S(1)}, s32[192]{0:T(256)}, u32[]{:S(2)}) copy-start(s32[192]{0:T(256)} %param.18) | copy-start | bytes 2308
  23.6 30.5 %copy-start.2 = (bf16[256,1024]{1,0:T(8,128)(2,1)S(1)}, bf16[256,1024]{1,0:T(8,128)(2,1)}, u32[]{:S(2)}) copy-start(bf16[256,1024]{1,0:T(8,128)(2,1)} %self_ref.1) | copy-start | bytes 1572868
  23.7 30.5 %copy-start.3 = (bf16[256,1024]{1,0:T(8,128)(2,1)S(1)}, bf16[256,1024]{1,0:T(8,128)(2,1)}, u32[]{:S(2)}) copy-start(bf16[256,1024]{1,0:T(8,128)(2,1)} %neigh_ref.1) | copy-start | bytes 1572868
  23.7 30.5 %copy-start.4 = (bf16[192,256]{1,0:T(8,128)(2,1)S(1)}, bf16[192,256]{1,0:T(8,128)(2,1)}, u32[]{:S(2)}) copy-start(bf16[192,256]{1,0:T(8,128)(2,1)} %own_ref.3) | copy-start | bytes 294916
  25.6 37.9 %copy-start.12 = (s32[192,10]{0,1:T(8,128)S(1)}, s32[192,10]{0,1:T(8,128)}, u32[]{:S(2)}) copy-start(s32[192,10]{0,1:T(8,128)} %param.17) | copy-start | bytes 23044
  25.6 28.6 %all-to-all-start = ((bf16[8,192,256]{2,1,0:T(8,128)(2,1)}), bf16[8,192,256]{2,1,0:T(8,128)(2,1)S(1)}, u32[]{:S(2)}, u32[]{:S(2)}) async-start(bf16[8,192,256]{2,1,0:T(8,128)(2,1)} %bitcast.3), calls=%async_computation | async-start | bytes 1572864 | tf_op jit(solution)/shard_map/all_to_all | solution.py:210
  55.4 0.6 copy-start.9
  56.0 39.5 %copy-start.1 = (bf16[1024,1024]{1,0:T(8,128)(2,1)S(1)}, bf16[1024,1024]{1,0:T(8,128)(2,1)}, u32[]{:S(2)}) copy-start(bf16[1024,1024]{1,0:T(8,128)(2,1)} %two_ref.1) | copy-start | bytes 6291460
  56.0 21.1 %all-to-all-start.1 = ((bf16[16,96,128]{2,1,0:T(8,128)(2,1)}), bf16[16,96,128]{2,1,0:T(8,128)(2,1)}, u32[]{:S(2)}, u32[]{:S(2)}) async-start(bf16[16,96,128]{2,1,0:T(8,128)(2,1)} %get-tuple-element.15), calls=%async_computation.1 | async-start | bytes 786432 | tf_op jit(solution)/shard_map/all_to_all | solution.py:210
  95.5 0.9 copy-start.10
  98.8 0.7 copy-start.5
  134.6 6.8 %copy-start.6 = (bf16[192,1024]{1,0:T(8,128)(2,1)S(1)}, bf16[192,1024]{1,0:T(8,128)(2,1)}, u32[]{:S(2)}) copy-start(bf16[192,1024]{1,0:T(8,128)(2,1)} %copy-done.5) | copy-start | bytes 1179652
  135.9 33.9 %all-to-all-start.3 = ((bf16[32,16,1024]{2,1,0:T(8,128)(2,1)}), bf16[32,16,1024]{2,1,0:T(8,128)(2,1)S(1)}, u32[]{:S(2)}, u32[]{:S(2)}) async-start(bf16[32,16,1024]{2,1,0:T(8,128)(2,1)} %sum_and_spread.1), calls=%async_computation.3 | async-start | bytes 2097152 | tf_op jit(solution)/shard_map/all_to_all | solution.py:210

commit v3 on v2

--- a/solution.py
+++ b/solution.py
@@ -11,7 +11,7 @@
 XS = 4
 ROW_BLOCK = 256
 DEAD = 512.0
-PARAMS = pltpu.CompilerParams(vmem_limit_bytes=48 * 1024 * 1024)
+MIB = 1024 * 1024
 NODE = ("x", "z")
 FEAT = ("y", "c")
 
@@ -21,16 +21,31 @@
     return gate + value * gate * (1.0 - gate)
 
 
+def params(mib):
+    return pltpu.CompilerParams(vmem_limit_bytes=mib * MIB)
+
+
 def dot(a, b, dims=((1,), (0,))):
     return lax.dot_general(a, b, (dims, ((), ())), preferred_element_type=jnp.float32)
 
 
-def payload_kernel(place_ref, index_ref, count_ref, table_ref, *refs):
-    outs, coded = refs[:-1], refs[-1]
+def payload_kernel(place_ref, index_hbm, count_hbm, table_hbm, *refs):
+    outs = refs[:XS]
+    index_ref, count_ref, table_ref, coded, sems = refs[XS:]
+    copies = [
+        pltpu.make_async_copy(source, target, sems.at[i])
+        for i, (source, target) in enumerate(
+            [(index_hbm, index_ref), (count_hbm, count_ref), (table_hbm, table_ref)]
+        )
+    ]
+    for copy in copies:
+        copy.start()
     slots, total = index_ref.shape
     nodes = table_ref.shape[0]
     per_x = total // XS
     blocks = per_x // ROW_BLOCK
+    copies[0].wait()
+    copies[1].wait()
     index = index_ref[...]
     slot = lax.broadcasted_iota(jnp.int32, (slots, total), 0)
     code = jnp.where(index < 256, index, 255 - index).astype(jnp.float32)
@@ -42,6 +57,7 @@
             for c in range(blocks)
         ] + [jnp.full((extra, ROW_BLOCK), DEAD, jnp.float32)]
         coded[x] = jnp.concatenate(pieces, axis=0).astype(jnp.bfloat16)
+    copies[2].wait()
     for shift in range(XS):
         out = outs[shift]
         out[0:nodes, :] = table_ref[...]
@@ -54,13 +70,20 @@
     used = slots * (total // XS // ROW_BLOCK)
     extra = -(-used // 16) * 16
     vmem = pl.BlockSpec(memory_space=pltpu.VMEM)
+    hbm = pl.BlockSpec(memory_space=pl.ANY)
     return pl.pallas_call(
         payload_kernel,
-        in_specs=[pl.BlockSpec(memory_space=pltpu.SMEM), vmem, vmem, vmem],
+        in_specs=[pl.BlockSpec(memory_space=pltpu.SMEM), hbm, hbm, hbm],
         out_specs=[vmem] * XS,
         out_shape=[jax.ShapeDtypeStruct((nodes + extra, width), jnp.bfloat16)] * XS,
-        scratch_shapes=[pltpu.VMEM((XS, extra, ROW_BLOCK), jnp.bfloat16)],
-        compiler_params=PARAMS,
+        scratch_shapes=[
+            pltpu.VMEM(index.shape, index.dtype),
+            pltpu.VMEM(count.shape, count.dtype),
+            pltpu.VMEM(table.shape, table.dtype),
+            pltpu.VMEM((XS, extra, ROW_BLOCK), jnp.bfloat16),
+            pltpu.SemaphoreType.DMA((3,)),
+        ],
+        compiler_params=params(60),
         name="payloads",
     )(place, index, count, table)
 
@@ -98,17 +121,19 @@
         in_specs=[vmem] * len(operands),
         out_specs=vmem,
         out_shape=jax.ShapeDtypeStruct((rows, width), dtype),
-        compiler_params=PARAMS,
+        compiler_params=params(16),
         name="gather_sum",
     )(*operands)
 
 
-def first_kernel(recv_ref, degree_ref, own_ref, self_ref, neigh_ref, mean_ref, out_ref):
+def first_kernel(recv_ref, degree_ref, own_ref, self_ref, neigh_ref, both_ref, out_ref):
     sums = recv_ref[0].astype(jnp.float32)
     for i in range(1, recv_ref.shape[0]):
         sums = sums + recv_ref[i].astype(jnp.float32)
     mean = (sums / degree_ref[...]).astype(jnp.bfloat16)
-    mean_ref[...] = mean
+    width_in = own_ref.shape[1]
+    both_ref[:, 0:width_in] = own_ref[...]
+    both_ref[:, width_in:] = mean
     pre = (dot(own_ref[...], self_ref[...]) + dot(mean, neigh_ref[...])).astype(jnp.bfloat16)
     count, height, width = out_ref.shape
     halves = pre.shape[0] // height
@@ -126,15 +151,15 @@
         in_specs=[vmem] * 5,
         out_specs=[vmem] * 2,
         out_shape=[
-            jax.ShapeDtypeStruct((rows, width), jnp.bfloat16),
+            jax.ShapeDtypeStruct((rows, 2 * width), jnp.bfloat16),
             jax.ShapeDtypeStruct((pieces, rows // 2, 2 * hidden // pieces), jnp.bfloat16),
         ],
-        compiler_params=PARAMS,
+        compiler_params=params(16),
         name="first_layer",
     )(recv, degree, own, self_weight, neigh_weight)
 
 
-def second_kernel(pre_ref, adj_ref, inv_ref, two_ref, back_ref, own_ref, mean_ref, hidden_ref, grad_ref):
+def second_kernel(pre_ref, adj_ref, inv_ref, two_ref, back_ref, hidden_ref, grad_ref):
     count, height, width = pre_ref.shape
     halves = inv_ref.shape[0] // height
     strips = [
@@ -163,26 +188,47 @@
         dot(adjacency, middle, down) + dot(adjacency, low, down)
     )
     grad_one = (grad_hidden * slope).astype(jnp.bfloat16)
-    width_in = own_ref.shape[1]
-    grad_ref[0:width_in, :] = dot(own_ref[...], grad_one, down).astype(jnp.bfloat16)
-    grad_ref[width_in:, :] = dot(mean_ref[...], grad_one, down).astype(jnp.bfloat16)
-
-
-def second_layer(pre, adjacency, inv_count, weight_two, back_two, own, mean):
-    rows, width = own.shape
+    quarter = grad_ref.shape[2]
+    for x in range(grad_ref.shape[0]):
+        grad_ref[x] = grad_one[:, x * quarter : (x + 1) * quarter]
+
+
+def second_layer(pre, adjacency, inv_count, weight_two, back_two):
+    rows = adjacency.shape[0]
     hidden = weight_two.shape[0]
     vmem = pl.BlockSpec(memory_space=pltpu.VMEM)
     return pl.pallas_call(
         second_kernel,
-        in_specs=[vmem] * 7,
+        in_specs=[vmem] * 5,
         out_specs=[vmem] * 2,
         out_shape=[
             jax.ShapeDtypeStruct((rows, hidden), jnp.bfloat16),
-            jax.ShapeDtypeStruct((2 * width, hidden), jnp.bfloat16),
+            jax.ShapeDtypeStruct((XS, rows, hidden // XS), jnp.bfloat16),
         ],
-        compiler_params=PARAMS,
+        compiler_params=params(24),
         name="second_layer",
-    )(pre, adjacency, inv_count, weight_two, back_two, own, mean)
+    )(pre, adjacency, inv_count, weight_two, back_two)
+
+
+def gradient_kernel(both_ref, grad_ref, out_ref):
+    rows = grad_ref.shape[1]
+    total = None
+    for x in range(grad_ref.shape[0]):
+        part = dot(both_ref[x * rows : (x + 1) * rows, :], grad_ref[x], ((0,), (0,)))
+        total = part if total is None else total + part
+    out_ref[...] = total.astype(jnp.bfloat16)
+
+
+def gradient_part(both, grad):
+    vmem = pl.BlockSpec(memory_space=pltpu.VMEM)
+    return pl.pallas_call(
+        gradient_kernel,
+        in_specs=[vmem] * 2,
+        out_specs=vmem,
+        out_shape=jax.ShapeDtypeStruct((both.shape[1], grad.shape[2]), jnp.bfloat16),
+        compiler_params=params(16),
+        name="gradient_part",
+    )(both, grad)
 
 
 def spread_kernel(recv_ref, out_ref):
@@ -190,18 +236,18 @@
     for i in range(1, recv_ref.shape[0]):
         sums = sums + recv_ref[i].astype(jnp.float32)
     piece = sums.astype(jnp.bfloat16)
-    for i in range(recv_ref.shape[0]):
+    for i in range(out_ref.shape[0]):
         out_ref[i] = piece
 
 
-def spread(recv):
+def spread(recv, copies):
     vmem = pl.BlockSpec(memory_space=pltpu.VMEM)
     return pl.pallas_call(
         spread_kernel,
         in_specs=[vmem],
         out_specs=vmem,
-        out_shape=jax.ShapeDtypeStruct(recv.shape, recv.dtype),
-        compiler_params=PARAMS,
+        out_shape=jax.ShapeDtypeStruct((copies,) + recv.shape[1:], recv.dtype),
+        compiler_params=params(8),
         name="sum_and_spread",
     )(recv)
 
@@ -239,7 +285,7 @@
     running = gather_sum(slots, per_x, jnp.float32, running, arrived[1:])
     parts = gather_sum(slots, per_x, jnp.bfloat16, running, arrived[:1])
     recv = exchange(parts.reshape(groups // XS, own_rows, width), "z")
-    mean_rows, pieces = first_layer(
+    both, pieces = first_layer(
         recv,
         degree[:, None].astype(jnp.float32),
         own_features,
@@ -247,8 +293,9 @@
         neigh_weight,
         splits,
     )
-    pre_piece = jnp.sum(exchange(pieces, FEAT).astype(jnp.float32), axis=0).astype(jnp.bfloat16)
-    pre = lax.all_gather(pre_piece, FEAT, axis=0, tiled=False)
+    both = lax.all_gather(both, "x", axis=0, tiled=True)
+    pre_piece = spread(exchange(pieces, FEAT), 1)
+    pre = lax.all_gather(pre_piece, FEAT, axis=0, tiled=True)
 
     slot_ids = jnp.arange(local_index.shape[1], dtype=jnp.int32)
     live_slots = slot_ids[None, :] < local_count[:, None]
@@ -260,11 +307,18 @@
     ).astype(jnp.bfloat16)
     inv_count = 1.0 / (1.0 + local_count.astype(jnp.float32))
     back_two = dot(cotangent, weight_three, ((1,), (1,)))
-    second_hidden, grad_part = second_layer(
-        pre, adjacency, inv_count[:, None], weight_two, back_two, own_features, mean_rows
-    )
-    grad_recv = exchange(grad_part.reshape(groups, -1, grad_part.shape[1]), NODE)
-    grads = exchange(spread(grad_recv), NODE).reshape(grad_part.shape)
+    second_hidden, grad_one = second_layer(
+        pre, adjacency, inv_count[:, None], weight_two, back_two
+    )
+    grad_part = gradient_part(both, exchange(grad_one, "x"))
+    quarter = grad_part.shape[1]
+    grad_recv = exchange(grad_part.reshape(groups // XS, -1, quarter), "z")
+    grads = (
+        exchange(spread(grad_recv, groups), NODE)
+        .reshape(XS, grad_part.shape[0], quarter)
+        .transpose(1, 0, 2)
+        .reshape(grad_part.shape[0], XS * quarter)
+    )
     logits = dot(second_hidden, weight_three).astype(jnp.bfloat16)
     return (grads[:width], grads[width:], logits)
 

time: 172 us -> 168 us (0.977)
  starting transfers between devices: 33.9 us -> 38.7 us
  blocking collectives: 51.8 us -> 47.2 us
  waiting for transfers between devices: 64.1 us -> 60.8 us
  Pallas kernels: 9.31 us -> 12.5 us
    all_to_all x1, blocking collectives: 35.1 us -> 12.7 us  [exchange(): return lax.all_to_all(pieces, axis, split_axis=0, concat_axis=0, tiled=True)]
    all_gather x1 -> x2, blocking collectives: 16.7 us -> 34.5 us  [the longest x1 18 us: body(): both = lax.all_gather(both, 'x', axis=0, tiled=True)]
    all_to_all x3 -> x4, starting transfers between devices: 23.1 us -> 27.9 us  [exchange(): return lax.all_to_all(pieces, axis, split_axis=0, concat_axis=0, tiled=True)]
    all_to_all x3 -> x4, waiting for transfers between devices: 57.2 us -> 54.5 us  [exchange(): return lax.all_to_all(pieces, axis, split_axis=0, concat_axis=0, tiled=True)]
    pallas_call x1, Pallas kernels: 0.09 us -> 2.13 us  [make_payloads(): pl.pallas_call(payload_kernel, in_specs=[pl.BlockSpec(memory_space=pltpu....]
    unnamed x30 -> x29, local copies, waits for them, and re-layouts: 4.94 us -> 3.26 us
  transfers between devices with their start and end apart: 6 -> 7, of which waited for: 4 -> 4; matrix products, arithmetic and copies ran while one was open for 2% -> 1% of each run, Pallas kernels for 1% -> 2%
where the time goes in v3:
time: 168 us; the launch traced here: 167 us
  waiting for transfers between devices  60.8 us (36%)
  blocking collectives  47.2 us (28%)
  starting transfers between devices  38.7 us (23%)
  Pallas kernels  12.5 us (7%)
  local copies, waits for them, and re-layouts  5.21 us (3%)
    all_to_all x4, waiting for transfers between devices, exchange(): return lax.all_to_all(pieces, axis, split_axis=0, concat_axis=0, tiled=True)  54.5 us
    all_to_all x4, starting transfers between devices, exchange(): return lax.all_to_all(pieces, axis, split_axis=0, concat_axis=0, tiled=True)  27.9 us
    all_gather x1, blocking collectives, body(): both = lax.all_gather(both, 'x', axis=0, tiled=True)  18 us
    all_gather x1, blocking collectives, body(): pre = lax.all_gather(pre_piece, FEAT, axis=0, tiled=True)  16.5 us
    all_to_all x1, blocking collectives, exchange(): return lax.all_to_all(pieces, axis, split_axis=0, concat_axis=0, tiled=True)  12.7 us
    ppermute x3, starting transfers between devices, body(): lax.ppermute(payloads[s], 'x', [(i, (i + s) % XS) for i in range(XS)])  10.8 us
    ppermute x3, waiting for transfers between devices, body(): lax.ppermute(payloads[s], 'x', [(i, (i + s) % XS) for i in range(XS)])  6.23 us
    pallas_call x3, Pallas kernels, gather_sum(): pl.pallas_call(functools.partial(gather_kernel, slots, int(carried is not...  4.47 us
  transfers between devices with their start and end apart: 7, of which 4 were waited for; matrix products, arithmetic and copies ran while one was open for 1% of the time, Pallas kernels for 2%

profile of v3, /device:TPU:64, one launch (start us, length us, event | category | flops | bytes accessed | tf_op | source)
XLA Modules:
  0.0 167.3 jit_solution(4869494604876129479)
XLA Ops:
  0.6 0.0 copy-start
  0.7 2.1 %payloads.1 = (bf16[544,256]{1,0:T(8,128)(2,1)}, bf16[544,256]{1,0:T(8,128)(2,1)}, bf16[544,256]{1,0:T(8,128)(2,1)}, bf16[544,256]{1,0:T(8,128)(2,1)}) custom-call(s32[1]{0:T(128)} %bitcast.place_ref, s32[4,6144]{1,0:T(4,128)} %bitcast.25, s32[1,6144]{1,0:T(1,128)} %count_hbm.1, bf16[512,256]{1,0:T(8,128)(2,1)} %table_hbm.1), custom_call_target="tpu_custom_call" | custom-call | tf_op jit(solution)/shard_map/payloads/pallas_call | solution.py:74
  2.8 3.4 %collective-permute-start = (bf16[544,256]{1,0:T(8,128)(2,1)}, bf16[544,256]{1,0:T(8,128)(2,1)S(1)}, u32[]{:S(2)}, u32[]{:S(2)}) collective-permute-start(bf16[544,256]{1,0:T(8,128)(2,1)} %get-tuple-element.12), channel_id=1, source_target_pairs={{0,128},{128,256},{256,384},{384,0},{1,129},{129,257},{257,385},{3... | collective-permute-start | bytes 835592 | tf_op jit(solution)/shard_map/ppermute | solution.py:282
  6.2 3.7 %collective-permute-start.1 = (bf16[544,256]{1,0:T(8,128)(2,1)}, bf16[544,256]{1,0:T(8,128)(2,1)S(1)}, u32[]{:S(2)}, u32[]{:S(2)}) collective-permute-start(bf16[544,256]{1,0:T(8,128)(2,1)} %get-tuple-element.13), channel_id=1, source_target_pairs={{0,384},{128,0},{256,128},{384,256},{1,385},{129,1},{257,129},{385... | collective-permute-start | bytes 835592 | tf_op jit(solution)/shard_map/ppermute | solution.py:282
  9.9 3.7 %collective-permute-start.2 = (bf16[544,256]{1,0:T(8,128)(2,1)}, bf16[544,256]{1,0:T(8,128)(2,1)S(1)}, u32[]{:S(2)}, u32[]{:S(2)}) collective-permute-start(bf16[544,256]{1,0:T(8,128)(2,1)} %get-tuple-element.14), channel_id=1, source_target_pairs={{0,256},{128,384},{256,0},{384,128},{1,257},{129,385},{257,1},{385... | collective-permute-start | bytes 835592 | tf_op jit(solution)/shard_map/ppermute | solution.py:282
  13.6 0.0 copy-start.7
  13.6 0.9 copy-done.7
  14.5 1.0 gather_sum.3.refs_0_
  15.5 0.0 collective-permute-done.refs_1_
  15.6 6.2 %collective-permute-done.1.refs_2_ = bf16[544,256]{1,0:T(8,128)(2,1)S(1)} collective-permute-done((bf16[544,256]{1,0:T(8,128)(2,1)}, bf16[544,256]{1,0:T(8,128)(2,1)S(1)}, u32[]{:S(2)}, u32[]{:S(2)}) %collective-permute-start.1) | collective-permute-done | bytes 278560 | tf_op jit(solution)/shard_map/ppermute | solution.py:282
  21.8 1.6 gather_sum.4.refs_0_
  23.4 0.0 copy-start.13
  23.4 0.0 copy-start.12
  23.4 0.0 copy-start.2
  23.4 0.0 copy-start.3
  23.4 0.0 copy-start.9
  23.4 0.0 collective-permute-done.2.refs_1_
  23.4 1.9 %gather_sum.5 = bf16[1536,256]{1,0:T(8,128)(2,1)} custom-call(f32[1536,256]{1,0:T(8,128)S(1)} %gather_sum.4.refs_0_, bf16[544,256]{1,0:T(8,128)(2,1)S(1)} %collective-permute-done.2.refs_1_), custom_call_target="tpu_custom_call" | custom-call | tf_op jit(solution)/shard_map/gather_sum/pallas_call | solution.py:119
  25.3 0.0 copy-start.11
  25.3 10.1 %all-to-all-start = ((bf16[8,192,256]{2,1,0:T(8,128)(2,1)}), bf16[8,192,256]{2,1,0:T(8,128)(2,1)S(1)}, u32[]{:S(2)}, u32[]{:S(2)}) async-start(bf16[8,192,256]{2,1,0:T(8,128)(2,1)} %bitcast.3), calls=%async_computation | async-start | bytes 1572864 | tf_op jit(solution)/shard_map/all_to_all | solution.py:256
  35.4 0.0 copy-done.13
  35.4 0.0 copy-start.10
  35.5 0.1 copy.28.degree_ref
  35.6 0.0 copy-done.12
  35.6 18.2 %all-to-all-done.recv_ref = bf16[8,192,256]{2,1,0:T(8,128)(2,1)S(1)} async-done(((bf16[8,192,256]{2,1,0:T(8,128)(2,1)}), bf16[8,192,256]{2,1,0:T(8,128)(2,1)S(1)}, u32[]{:S(2)}, u32[]{:S(2)}) %all-to-all-start) | async-done | bytes 786464 | tf_op jit(solution)/shard_map/all_to_all | solution.py:256
  53.8 0.0 copy-done.2
  53.8 0.0 copy-done.3
  53.8 0.0 copy-done.9
  53.8 1.2 first_layer.1
  55.0 0.0 copy-start.8
  55.0 0.7 copy-done.8
  55.7 0.0 copy-start.1
  55.7 7.4 %all-to-all-start.1 = ((bf16[16,96,128]{2,1,0:T(8,128)(2,1)}), bf16[16,96,128]{2,1,0:T(8,128)(2,1)}, u32[]{:S(2)}, u32[]{:S(2)}) async-start(bf16[16,96,128]{2,1,0:T(8,128)(2,1)} %get-tuple-element.16), calls=%async_computation.1 | async-start | bytes 786432 | tf_op jit(solution)/shard_map/all_to_all | solution.py:256
  63.1 0.1 copy.29.inv_ref
  63.2 0.0 copy-done.11
  63.2 0.8 convert_reduce_fusion
  64.1 0.0 copy-done
  64.1 0.0 copy-done.10
  64.1 0.3 fusion.1.back_ref
  64.4 12.5 %all-to-all-done.1.recv_ref = bf16[16,96,128]{2,1,0:T(8,128)(2,1)} async-done(((bf16[16,96,128]{2,1,0:T(8,128)(2,1)}), bf16[16,96,128]{2,1,0:T(8,128)(2,1)}, u32[]{:S(2)}, u32[]{:S(2)}) %all-to-all-start.1) | async-done | bytes 393248 | tf_op jit(solution)/shard_map/all_to_all | solution.py:256
  76.8 1.1 sum_and_spread.2
  77.9 16.5 %all_gather.7.pre_ref = bf16[16,96,128]{2,1,0:T(8,128)(2,1)S(1)} all-gather(bf16[1,96,128]{2,1,0:T(8,128)(2,1)S(1)} %sum_and_spread.2), channel_id=1, replica_groups=mesh['x'=4,'z'=8,'y'=8,'c'=2] {'y','c'}, dimensions={0}, use_global_device_ids=true | all-gather | bytes 417792 | tf_op jit(solution)/shard_map/all_gather | solution.py:298
  94.4 0.0 copy-done.1
  94.4 2.0 %second_layer.1 = (bf16[192,1024]{1,0:T(8,128)(2,1)S(1)}, bf16[4,192,256]{2,1,0:T(8,128)(2,1)S(1)}) custom-call(bf16[16,96,128]{2,1,0:T(8,128)(2,1)S(1)} %all_gather.7.pre_ref, bf16[192,192]{1,0:T(8,128)(2,1)S(1)} %add_convert_fusion.adj_ref, f32[192,1]{1,0:T(8,128)S(1)} %copy.29.inv_ref, bf16[1024,1024]{1,0:T(8,128)(2,1)S(1)} %copy-done.1, ...), custom_call_target="tpu_custom_call" | custom-call | tf_op jit(solution)/shard_map/second_layer/pallas_call | solution.py:200
  96.4 0.0 copy-start.4
  96.4 0.7 copy-done.4
  97.1 0.0 copy-start.6
  97.1 0.7 copy-done.6
  97.9 5.1 %all-to-all-start.2 = ((bf16[4,192,256]{2,1,0:T(8,128)(2,1)}), bf16[4,192,256]{2,1,0:T(8,128)(2,1)S(1)}, u32[]{:S(2)}, u32[]{:S(2)}) async-start(bf16[4,192,256]{2,1,0:T(8,128)(2,1)} %copy-done.6), calls=%async_computation.2 | async-start | bytes 786432 | tf_op jit(solution)/shard_map/all_to_all | solution.py:256
  102.9 18.0 %all_gather.6.both_ref = bf16[768,512]{1,0:T(8,128)(2,1)S(1)} all-gather(bf16[192,512]{1,0:T(8,128)(2,1)} %copy-done.8), channel_id=1, replica_groups=mesh['x'=4,'z'=8,'y'=8,'c'=2] {'x'}, dimensions={0}, use_global_device_ids=true | all-gather | bytes 983040 | tf_op jit(solution)/shard_map/all_gather | solution.py:296
  121.0 0.0 all-to-all-done.2.grad_ref
  121.0 0.5 gradient_part.1
  121.5 0.0 copy-start.5
  121.5 12.7 %all_to_all.25.recv_ref = bf16[8,64,256]{2,1,0:T(8,128)(2,1)S(1)} all-to-all(bf16[8,64,256]{2,1,0:T(8,128)(2,1)S(1)} %bitcast.21), channel_id=1, replica_groups=mesh['x'=4,'z'=8,'y'=8,'c'=2] {'z'}, dimensions={0} | all-to-all | bytes 524288 | tf_op jit(solution)/shard_map/all_to_all | solution.py:256
  134.2 1.1 sum_and_spread.3
  135.3 5.4 %all-to-all-start.4 = ((bf16[32,64,256]{2,1,0:T(8,128)(2,1)}), bf16[32,64,256]{2,1,0:T(8,128)(2,1)S(1)}, u32[]{:S(2)}, u32[]{:S(2)}) async-start(bf16[32,64,256]{2,1,0:T(8,128)(2,1)} %sum_and_spread.3), calls=%async_computation.4 | async-start | bytes 2097152 | tf_op jit(solution)/shard_map/all_to_all | solution.py:256
  140.7 0.0 copy-done.5
  140.7 0.9 convolution_convert_fusion
  141.7 23.8 %all-to-all-done.4 = bf16[32,64,256]{2,1,0:T(8,128)(2,1)S(1)} async-done(((bf16[32,64,256]{2,1,0:T(8,128)(2,1)}), bf16[32,64,256]{2,1,0:T(8,128)(2,1)S(1)}, u32[]{:S(2)}, u32[]{:S(2)}) %all-to-all-start.4) | async-done | bytes 1048608 | tf_op jit(solution)/shard_map/all_to_all | solution.py:256
  165.5 0.1 slice_bitcast_fusion
  165.6 0.9 copy.32
  166.4 0.9 copy.33
  (4 shorter events, 0.0 us)
Async XLA Ops:
  0.6 63.4 %copy-start = (bf16[1024,172]{0,1:T(8,128)(2,1)S(1)}, bf16[1024,172]{0,1:T(8,128)(2,1)}, u32[]{:S(2)}) copy-start(bf16[1024,172]{0,1:T(8,128)(2,1)} %param.22) | copy-start | bytes 1056772
  2.8 12.8 %collective-permute-start = (bf16[544,256]{1,0:T(8,128)(2,1)}, bf16[544,256]{1,0:T(8,128)(2,1)S(1)}, u32[]{:S(2)}, u32[]{:S(2)}) collective-permute-start(bf16[544,256]{1,0:T(8,128)(2,1)} %get-tuple-element.12), channel_id=1, source_target_pairs={{0,128},{128,256},{256,384},{384,0},{1,129},{129,257},{257,385},{3... | collective-permute-start | bytes 835592 | tf_op jit(solution)/shard_map/ppermute | solution.py:282
  6.2 15.6 %collective-permute-start.1 = (bf16[544,256]{1,0:T(8,128)(2,1)}, bf16[544,256]{1,0:T(8,128)(2,1)S(1)}, u32[]{:S(2)}, u32[]{:S(2)}) collective-permute-start(bf16[544,256]{1,0:T(8,128)(2,1)} %get-tuple-element.13), channel_id=1, source_target_pairs={{0,384},{128,0},{256,128},{384,256},{1,385},{129,1},{257,129},{385... | collective-permute-start | bytes 835592 | tf_op jit(solution)/shard_map/ppermute | solution.py:282
  9.9 13.6 %collective-permute-start.2 = (bf16[544,256]{1,0:T(8,128)(2,1)}, bf16[544,256]{1,0:T(8,128)(2,1)S(1)}, u32[]{:S(2)}, u32[]{:S(2)}) collective-permute-start(bf16[544,256]{1,0:T(8,128)(2,1)} %get-tuple-element.14), channel_id=1, source_target_pairs={{0,256},{128,384},{256,0},{384,128},{1,257},{129,385},{257,1},{385... | collective-permute-start | bytes 835592 | tf_op jit(solution)/shard_map/ppermute | solution.py:282
  13.6 1.0 copy-start.7
  23.4 12.1 %copy-start.13 = (s32[192]{0:T(256)S(1)}, s32[192]{0:T(256)}, u32[]{:S(2)}) copy-start(s32[192]{0:T(256)} %param.16) | copy-start | bytes 2308
  23.4 12.2 %copy-start.12 = (s32[192]{0:T(256)S(1)}, s32[192]{0:T(256)}, u32[]{:S(2)}) copy-start(s32[192]{0:T(256)} %param.18) | copy-start | bytes 2308
  23.4 30.4 %copy-start.2 = (bf16[256,1024]{1,0:T(8,128)(2,1)S(1)}, bf16[256,1024]{1,0:T(8,128)(2,1)}, u32[]{:S(2)}) copy-start(bf16[256,1024]{1,0:T(8,128)(2,1)} %self_ref.1) | copy-start | bytes 1572868
  23.4 30.4 %copy-start.3 = (bf16[256,1024]{1,0:T(8,128)(2,1)S(1)}, bf16[256,1024]{1,0:T(8,128)(2,1)}, u32[]{:S(2)}) copy-start(bf16[256,1024]{1,0:T(8,128)(2,1)} %neigh_ref.1) | copy-start | bytes 1572868
  23.4 30.4 %copy-start.9 = (bf16[192,256]{1,0:T(8,128)(2,1)S(1)}, bf16[192,256]{1,0:T(8,128)(2,1)}, u32[]{:S(2)}) copy-start(bf16[192,256]{1,0:T(8,128)(2,1)} %own_ref.1) | copy-start | bytes 294916
  25.3 37.9 %copy-start.11 = (s32[192,10]{0,1:T(8,128)S(1)}, s32[192,10]{0,1:T(8,128)}, u32[]{:S(2)}) copy-start(s32[192,10]{0,1:T(8,128)} %param.17) | copy-start | bytes 23044
  25.3 28.5 %all-to-all-start = ((bf16[8,192,256]{2,1,0:T(8,128)(2,1)}), bf16[8,192,256]{2,1,0:T(8,128)(2,1)S(1)}, u32[]{:S(2)}, u32[]{:S(2)}) async-start(bf16[8,192,256]{2,1,0:T(8,128)(2,1)} %bitcast.3), calls=%async_computation | async-start | bytes 1572864 | tf_op jit(solution)/shard_map/all_to_all | solution.py:256
  35.4 28.6 %copy-start.10 = (bf16[192,172]{0,1:T(8,128)(2,1)S(1)}, bf16[192,172]{0,1:T(8,128)(2,1)}, u32[]{:S(2)}) copy-start(bf16[192,172]{0,1:T(8,128)(2,1)} %param.23) | copy-start | bytes 198148
  55.0 0.7 copy-start.8
  55.7 38.7 %copy-start.1 = (bf16[1024,1024]{1,0:T(8,128)(2,1)S(1)}, bf16[1024,1024]{1,0:T(8,128)(2,1)}, u32[]{:S(2)}) copy-start(bf16[1024,1024]{1,0:T(8,128)(2,1)} %two_ref.1) | copy-start | bytes 6291460
  55.7 21.1 %all-to-all-start.1 = ((bf16[16,96,128]{2,1,0:T(8,128)(2,1)}), bf16[16,96,128]{2,1,0:T(8,128)(2,1)}, u32[]{:S(2)}, u32[]{:S(2)}) async-start(bf16[16,96,128]{2,1,0:T(8,128)(2,1)} %get-tuple-element.16), calls=%async_computation.1 | async-start | bytes 786432 | tf_op jit(solution)/shard_map/all_to_all | solution.py:256
  96.4 0.7 copy-start.4
  97.1 0.7 copy-start.6
  97.9 23.1 %all-to-all-start.2 = ((bf16[4,192,256]{2,1,0:T(8,128)(2,1)}), bf16[4,192,256]{2,1,0:T(8,128)(2,1)S(1)}, u32[]{:S(2)}, u32[]{:S(2)}) async-start(bf16[4,192,256]{2,1,0:T(8,128)(2,1)} %copy-done.6), calls=%async_computation.2 | async-start | bytes 786432 | tf_op jit(solution)/shard_map/all_to_all | solution.py:256
  121.5 19.3 %copy-start.5 = (bf16[192,1024]{1,0:T(8,128)(2,1)S(1)}, bf16[192,1024]{1,0:T(8,128)(2,1)}, u32[]{:S(2)}) copy-start(bf16[192,1024]{1,0:T(8,128)(2,1)} %copy-done.4) | copy-start | bytes 1179652
  135.3 30.2 %all-to-all-start.4 = ((bf16[32,64,256]{2,1,0:T(8,128)(2,1)}), bf16[32,64,256]{2,1,0:T(8,128)(2,1)S(1)}, u32[]{:S(2)}, u32[]{:S(2)}) async-start(bf16[32,64,256]{2,1,0:T(8,128)(2,1)} %sum_and_spread.3), calls=%async_computation.4 | async-start | bytes 2097152 | tf_op jit(solution)/shard_map/all_to_all | solution.py:256

commit v4 on v3

--- a/solution.py
+++ b/solution.py
@@ -12,6 +12,7 @@
 ROW_BLOCK = 256
 DEAD = 512.0
 MIB = 1024 * 1024
+GATHER_ROWS = 256
 NODE = ("x", "z")
 FEAT = ("y", "c")
 
@@ -70,7 +71,7 @@
     used = slots * (total // XS // ROW_BLOCK)
     extra = -(-used // 16) * 16
     vmem = pl.BlockSpec(memory_space=pltpu.VMEM)
-    hbm = pl.BlockSpec(memory_space=pl.ANY)
+    hbm = pl.BlockSpec(memory_space=pltpu.HBM)
     return pl.pallas_call(
         payload_kernel,
         in_specs=[pl.BlockSpec(memory_space=pltpu.SMEM), hbm, hbm, hbm],
@@ -83,7 +84,7 @@
             pltpu.VMEM((XS, extra, ROW_BLOCK), jnp.bfloat16),
             pltpu.SemaphoreType.DMA((3,)),
         ],
-        compiler_params=params(60),
+        compiler_params=params(16),
         name="payloads",
     )(place, index, count, table)
 
@@ -126,40 +127,76 @@
     )(*operands)
 
 
-def first_kernel(recv_ref, degree_ref, own_ref, self_ref, neigh_ref, both_ref, out_ref):
+def first_kernel(
+    recv_ref, degree_ref, own_ref, self_ref, neigh_ref, both_hbm, out_ref, both_ref, sem
+):
     sums = recv_ref[0].astype(jnp.float32)
     for i in range(1, recv_ref.shape[0]):
         sums = sums + recv_ref[i].astype(jnp.float32)
     mean = (sums / degree_ref[...]).astype(jnp.bfloat16)
-    width_in = own_ref.shape[1]
-    both_ref[:, 0:width_in] = own_ref[...]
-    both_ref[:, width_in:] = mean
+    rows, width_in = own_ref.shape
+    both_ref[0:rows, 0:width_in] = own_ref[...]
+    both_ref[0:rows, width_in:] = mean
+    both_ref[rows:, :] = jnp.zeros((both_ref.shape[0] - rows, 2 * width_in), jnp.bfloat16)
+    copy = pltpu.make_async_copy(both_ref, both_hbm, sem)
+    copy.start()
     pre = (dot(own_ref[...], self_ref[...]) + dot(mean, neigh_ref[...])).astype(jnp.bfloat16)
     count, height, width = out_ref.shape
-    halves = pre.shape[0] // height
+    halves = rows // height
     for i in range(count):
         t, h = i // halves, i % halves
         out_ref[i] = pre[h * height : (h + 1) * height, t * width : (t + 1) * width]
+    copy.wait()
 
 
 def first_layer(recv, degree, own, self_weight, neigh_weight, pieces):
     rows, width = own.shape
     hidden = self_weight.shape[1]
     vmem = pl.BlockSpec(memory_space=pltpu.VMEM)
+    padded = max(rows, GATHER_ROWS)
     return pl.pallas_call(
         first_kernel,
         in_specs=[vmem] * 5,
-        out_specs=[vmem] * 2,
+        out_specs=[pl.BlockSpec(memory_space=pltpu.HBM), vmem],
         out_shape=[
-            jax.ShapeDtypeStruct((rows, 2 * width), jnp.bfloat16),
+            jax.ShapeDtypeStruct((padded, 2 * width), jnp.bfloat16),
             jax.ShapeDtypeStruct((pieces, rows // 2, 2 * hidden // pieces), jnp.bfloat16),
+        ],
+        scratch_shapes=[
+            pltpu.VMEM((padded, 2 * width), jnp.bfloat16),
+            pltpu.SemaphoreType.DMA(()),
         ],
         compiler_params=params(16),
         name="first_layer",
     )(recv, degree, own, self_weight, neigh_weight)
 
 
-def second_kernel(pre_ref, adj_ref, inv_ref, two_ref, back_ref, hidden_ref, grad_ref):
+def pair_kernel(core_ref, pieces_ref, out_ref):
+    count = out_ref.shape[0]
+    first = core_ref[0] * count
+    for i in range(count):
+        total = pieces_ref[0, first + i].astype(jnp.float32)
+        for source in range(1, pieces_ref.shape[0]):
+            total = total + pieces_ref[source, first + i].astype(jnp.float32)
+        out_ref[i] = total.astype(jnp.bfloat16)
+
+
+def pair_sum(core, pieces):
+    cores, count, height, width = pieces.shape
+    vmem = pl.BlockSpec(memory_space=pltpu.VMEM)
+    return pl.pallas_call(
+        pair_kernel,
+        in_specs=[pl.BlockSpec(memory_space=pltpu.SMEM), vmem],
+        out_specs=vmem,
+        out_shape=jax.ShapeDtypeStruct((count // cores, height, width), jnp.bfloat16),
+        compiler_params=params(8),
+        name="pair_sum",
+    )(core, pieces)
+
+
+def second_kernel(
+    pre_ref, adj_ref, inv_ref, two_ref, three_ref, back_ref, logits_ref, grad_hbm, grad_ref, sem
+):
     count, height, width = pre_ref.shape
     halves = inv_ref.shape[0] // height
     strips = [
@@ -175,10 +212,12 @@
     mixed = (dot(adjacency, first_hidden) * inv).astype(jnp.bfloat16)
     pre_two = dot(mixed, two_ref[...])
     gate_two = jax.nn.sigmoid(pre_two)
-    hidden_ref[...] = (pre_two * gate_two).astype(jnp.bfloat16)
+    second_hidden = (pre_two * gate_two).astype(jnp.bfloat16)
+    across = ((1,), (1,))
+    logits_ref[...] = dot(three_ref[...], second_hidden, across).astype(jnp.bfloat16)
     slope_two = gate_two + pre_two * gate_two * (1.0 - gate_two)
     grad_two = (back_ref[...] * slope_two).astype(jnp.bfloat16)
-    grad_mixed = dot(grad_two, two_ref[...], ((1,), (1,))) * inv
+    grad_mixed = dot(grad_two, two_ref[...], across) * inv
     high = grad_mixed.astype(jnp.bfloat16)
     rest = grad_mixed - high.astype(jnp.float32)
     middle = rest.astype(jnp.bfloat16)
@@ -191,30 +230,38 @@
     quarter = grad_ref.shape[2]
     for x in range(grad_ref.shape[0]):
         grad_ref[x] = grad_one[:, x * quarter : (x + 1) * quarter]
-
-
-def second_layer(pre, adjacency, inv_count, weight_two, back_two):
+    copy = pltpu.make_async_copy(grad_ref, grad_hbm, sem)
+    copy.start()
+    copy.wait()
+
+
+def second_layer(pre, adjacency, inv_count, weight_two, weight_three, back_two):
     rows = adjacency.shape[0]
     hidden = weight_two.shape[0]
     vmem = pl.BlockSpec(memory_space=pltpu.VMEM)
     return pl.pallas_call(
         second_kernel,
-        in_specs=[vmem] * 5,
-        out_specs=[vmem] * 2,
+        in_specs=[vmem] * 6,
+        out_specs=[vmem, pl.BlockSpec(memory_space=pltpu.HBM)],
         out_shape=[
-            jax.ShapeDtypeStruct((rows, hidden), jnp.bfloat16),
+            jax.ShapeDtypeStruct((weight_three.shape[0], rows), jnp.bfloat16),
             jax.ShapeDtypeStruct((XS, rows, hidden // XS), jnp.bfloat16),
+        ],
+        scratch_shapes=[
+            pltpu.VMEM((XS, rows, hidden // XS), jnp.bfloat16),
+            pltpu.SemaphoreType.DMA(()),
         ],
         compiler_params=params(24),
         name="second_layer",
-    )(pre, adjacency, inv_count, weight_two, back_two)
+    )(pre, adjacency, inv_count, weight_two, weight_three, back_two)
 
 
 def gradient_kernel(both_ref, grad_ref, out_ref):
-    rows = grad_ref.shape[1]
+    xs, rows, _ = grad_ref.shape
+    padded = both_ref.shape[0] // xs
     total = None
-    for x in range(grad_ref.shape[0]):
-        part = dot(both_ref[x * rows : (x + 1) * rows, :], grad_ref[x], ((0,), (0,)))
+    for x in range(xs):
+        part = dot(both_ref[x * padded : x * padded + rows, :], grad_ref[x], ((0,), (0,)))
         total = part if total is None else total + part
     out_ref[...] = total.astype(jnp.bfloat16)
 
@@ -249,6 +296,37 @@
         out_shape=jax.ShapeDtypeStruct((copies,) + recv.shape[1:], recv.dtype),
         compiler_params=params(8),
         name="sum_and_spread",
+    )(recv)
+
+
+def assemble_kernel(recv_hbm, self_hbm, neigh_hbm, sem):
+    height, hidden = self_hbm.shape
+    width = recv_hbm.shape[1]
+    copies = []
+    for x in range(hidden // width):
+        for i, out in enumerate((self_hbm, neigh_hbm)):
+            source = recv_hbm.at[pl.ds((2 * x + i) * height, height), :]
+            copies.append(
+                pltpu.make_async_copy(source, out.at[:, pl.ds(x * width, width)], sem.at[2 * x + i])
+            )
+    for copy in copies:
+        copy.start()
+    for copy in copies:
+        copy.wait()
+
+
+def assemble(recv):
+    total, width = recv.shape
+    height = total // XS // 2
+    shape = jax.ShapeDtypeStruct((height, XS * width), recv.dtype)
+    return pl.pallas_call(
+        assemble_kernel,
+        in_specs=[pl.BlockSpec(memory_space=pl.ANY)],
+        out_specs=[pl.BlockSpec(memory_space=pltpu.HBM)] * 2,
+        out_shape=[shape] * 2,
+        scratch_shapes=[pltpu.SemaphoreType.DMA((2 * XS,))],
+        compiler_params=params(8),
+        name="assemble",
     )(recv)
 
 
@@ -294,8 +372,10 @@
         splits,
     )
     both = lax.all_gather(both, "x", axis=0, tiled=True)
-    pre_piece = spread(exchange(pieces, FEAT), 1)
-    pre = lax.all_gather(pre_piece, FEAT, axis=0, tiled=True)
+    core = lax.axis_index("c").reshape(1).astype(jnp.int32)
+    paired = pair_sum(core, lax.all_gather(pieces, "c", axis=0, tiled=False))
+    pre_copies = spread(exchange(paired, "y"), paired.shape[0])
+    pre = lax.all_gather(exchange(pre_copies, "y"), "c", axis=0, tiled=True)
 
     slot_ids = jnp.arange(local_index.shape[1], dtype=jnp.int32)
     live_slots = slot_ids[None, :] < local_count[:, None]
@@ -307,20 +387,15 @@
     ).astype(jnp.bfloat16)
     inv_count = 1.0 / (1.0 + local_count.astype(jnp.float32))
     back_two = dot(cotangent, weight_three, ((1,), (1,)))
-    second_hidden, grad_one = second_layer(
-        pre, adjacency, inv_count[:, None], weight_two, back_two
+    logits, grad_one = second_layer(
+        pre, adjacency, inv_count[:, None], weight_two, weight_three.T, back_two
     )
     grad_part = gradient_part(both, exchange(grad_one, "x"))
     quarter = grad_part.shape[1]
     grad_recv = exchange(grad_part.reshape(groups // XS, -1, quarter), "z")
-    grads = (
-        exchange(spread(grad_recv, groups), NODE)
-        .reshape(XS, grad_part.shape[0], quarter)
-        .transpose(1, 0, 2)
-        .reshape(grad_part.shape[0], XS * quarter)
-    )
-    logits = dot(second_hidden, weight_three).astype(jnp.bfloat16)
-    return (grads[:width], grads[width:], logits)
+    grads = exchange(spread(grad_recv, groups), NODE)
+    grad_self, grad_neigh = assemble(grads.reshape(-1, quarter))
+    return (grad_self, grad_neigh, logits.T)
 
 
 def solution(mesh):

time: 168 us -> 172 us (1.024)
  waiting for transfers between devices: 60.8 us -> 44.5 us
  blocking collectives: 47.2 us -> 62.8 us
  between operations: 0.92 us -> 14.3 us
  starting transfers between devices: 38.7 us -> 32.1 us
    all_to_all x1 -> x3, blocking collectives: 12.7 us -> 58 us  [exchange(): return lax.all_to_all(pieces, axis, split_axis=0, concat_axis=0, tiled=True)]
    all_gather x2, blocking collectives: 34.5 us -> 4.79 us  [the longest x1 2.5 us: body(): paired = pair_sum(core, lax.all_gather(pieces, 'c', axis=0, tiled=False))]
    all_to_all x4 -> x3, waiting for transfers between devices: 54.5 us -> 37.6 us  [exchange(): return lax.all_to_all(pieces, axis, split_axis=0, concat_axis=0, tiled=True)]
    all_to_all x4 -> x3, starting transfers between devices: 27.9 us -> 21.4 us  [exchange(): return lax.all_to_all(pieces, axis, split_axis=0, concat_axis=0, tiled=True)]
    pallas_call x2 -> x4, Pallas kernels: 3.19 us -> 6.22 us  [the longest x1 3.38 us: second_layer(): pl.pallas_call(second_kernel, in_specs=[vmem] * 6, out_specs=[vmem, pl.Bl...]
    pallas_call x1, Pallas kernels: 2.13 us -> 0.29 us  [make_payloads(): pl.pallas_call(payload_kernel, in_specs=[pl.BlockSpec(memory_space=pltpu....]
    unnamed x29 -> x26, local copies, waits for them, and re-layouts: 3.26 us -> 3.88 us
  transfers between devices with their start and end apart: 7 -> 7, of which waited for: 4 -> 4; matrix products, arithmetic and copies ran while one was open for 1% -> 1% of each run, Pallas kernels for 2% -> 4%
where the time goes in v4:
time: 172 us; the launch traced here: 171 us
  blocking collectives  62.8 us (37%)
  waiting for transfers between devices  44.5 us (26%)
  starting transfers between devices  32.1 us (19%)
  between operations  14.3 us (8%)
  Pallas kernels  12.3 us (7%)
  local copies, waits for them, and re-layouts  4.13 us (2%)
    all_to_all x3, blocking collectives, exchange(): return lax.all_to_all(pieces, axis, split_axis=0, concat_axis=0, tiled=True)  58 us
    all_to_all x3, waiting for transfers between devices, exchange(): return lax.all_to_all(pieces, axis, split_axis=0, concat_axis=0, tiled=True)  37.6 us
    all_to_all x3, starting transfers between devices, exchange(): return lax.all_to_all(pieces, axis, split_axis=0, concat_axis=0, tiled=True)  21.4 us
    ppermute x3, starting transfers between devices, body(): lax.ppermute(payloads[s], 'x', [(i, (i + s) % XS) for i in range(XS)])  10.8 us
    ppermute x3, waiting for transfers between devices, body(): lax.ppermute(payloads[s], 'x', [(i, (i + s) % XS) for i in range(XS)])  6.87 us
    pallas_call x3, Pallas kernels, gather_sum(): pl.pallas_call(functools.partial(gather_kernel, slots, int(carried is not...  4.51 us
    unnamed x26, local copies, waits for them, and re-layouts  3.88 us
  transfers between devices with their start and end apart: 7, of which 4 were waited for; matrix products, arithmetic and copies ran while one was open for 1% of the time, Pallas kernels for 4%

profile of v4, /device:TPU:64, one launch (start us, length us, event | category | flops | bytes accessed | tf_op | source)
XLA Modules:
  0.0 171.3 jit_solution(14080688755513727002)
XLA Ops:
  7.2 0.0 copy-start
  7.2 0.0 copy-start.6
  7.2 1.0 copy-done.6
  8.2 0.0 copy-start.8
  8.2 0.9 copy-done.8
  9.1 0.0 copy-start.9
  9.1 0.7 copy-done.9
  9.8 0.3 payloads.1
  10.1 3.4 %collective-permute-start = (bf16[544,256]{1,0:T(8,128)(2,1)S(1)}, bf16[544,256]{1,0:T(8,128)(2,1)S(1)}, u32[]{:S(2)}, u32[]{:S(2)}) collective-permute-start(bf16[544,256]{1,0:T(8,128)(2,1)S(1)} %get-tuple-element.14), channel_id=1, source_target_pairs={{0,128},{128,256},{256,384},{384,0},{1,129},{129,257},{257,385},{3... | collective-permute-start | bytes 835592 | tf_op jit(solution)/shard_map/ppermute | solution.py:360
  13.5 3.7 %collective-permute-start.1 = (bf16[544,256]{1,0:T(8,128)(2,1)S(1)}, bf16[544,256]{1,0:T(8,128)(2,1)S(1)}, u32[]{:S(2)}, u32[]{:S(2)}) collective-permute-start(bf16[544,256]{1,0:T(8,128)(2,1)S(1)} %get-tuple-element.15), channel_id=1, source_target_pairs={{0,384},{128,0},{256,128},{384,256},{1,385},{129,1},{257,129},{385... | collective-permute-start | bytes 835592 | tf_op jit(solution)/shard_map/ppermute | solution.py:360
  17.2 3.7 %collective-permute-start.2 = (bf16[544,256]{1,0:T(8,128)(2,1)S(1)}, bf16[544,256]{1,0:T(8,128)(2,1)S(1)}, u32[]{:S(2)}, u32[]{:S(2)}) collective-permute-start(bf16[544,256]{1,0:T(8,128)(2,1)S(1)} %get-tuple-element.16), channel_id=1, source_target_pairs={{0,256},{128,384},{256,0},{384,128},{1,257},{129,385},{257,1},{385... | collective-permute-start | bytes 835592 | tf_op jit(solution)/shard_map/ppermute | solution.py:360
  20.9 1.0 gather_sum.3.refs_0_
  21.9 0.0 collective-permute-done.refs_1_
  21.9 6.9 %collective-permute-done.1.refs_2_ = bf16[544,256]{1,0:T(8,128)(2,1)S(1)} collective-permute-done((bf16[544,256]{1,0:T(8,128)(2,1)S(1)}, bf16[544,256]{1,0:T(8,128)(2,1)S(1)}, u32[]{:S(2)}, u32[]{:S(2)}) %collective-permute-start.1) | collective-permute-done | bytes 278560 | tf_op jit(solution)/shard_map/ppermute | solution.py:360
  28.8 1.6 gather_sum.4.refs_0_
  30.3 0.0 copy-start.12
  30.4 0.0 copy-start.4
  30.4 0.0 copy-start.5
  30.4 0.0 copy-start.7
  30.4 0.0 collective-permute-done.2.refs_1_
  30.4 2.0 %gather_sum.5 = bf16[1536,256]{1,0:T(8,128)(2,1)} custom-call(f32[1536,256]{1,0:T(8,128)S(1)} %gather_sum.4.refs_0_, bf16[544,256]{1,0:T(8,128)(2,1)S(1)} %collective-permute-done.2.refs_1_), custom_call_target="tpu_custom_call" | custom-call | tf_op jit(solution)/shard_map/gather_sum/pallas_call | solution.py:120
  32.4 0.0 copy-start.11
  32.4 10.1 %all-to-all-start = ((bf16[8,192,256]{2,1,0:T(8,128)(2,1)}), bf16[8,192,256]{2,1,0:T(8,128)(2,1)S(1)}, u32[]{:S(2)}, u32[]{:S(2)}) async-start(bf16[8,192,256]{2,1,0:T(8,128)(2,1)} %bitcast.3), calls=%async_computation | async-start | bytes 1572864 | tf_op jit(solution)/shard_map/all_to_all | solution.py:334
  42.5 0.0 all-gather.3.cloned.1.call-start
  42.5 0.0 copy-done.12
  42.5 0.1 copy.22.degree_ref
  42.6 0.0 copy-start.10
  42.6 18.3 %all-to-all-done.recv_ref = bf16[8,192,256]{2,1,0:T(8,128)(2,1)S(1)} async-done(((bf16[8,192,256]{2,1,0:T(8,128)(2,1)}), bf16[8,192,256]{2,1,0:T(8,128)(2,1)S(1)}, u32[]{:S(2)}, u32[]{:S(2)}) %all-to-all-start) | async-done | bytes 786464 | tf_op jit(solution)/shard_map/all_to_all | solution.py:334
  60.9 0.0 copy-done.4
  60.9 0.0 copy-done.5
  60.9 0.0 copy-done.7
  60.9 1.1 first_layer.1
  62.0 0.0 all-gather.3.cloned.1.call-update
  62.1 0.0 copy-done.11
  62.1 0.0 copy-start.2
  62.1 2.5 %all-gather = bf16[32,96,128]{2,1,0:T(8,128)(2,1)S(1)} all-gather(bf16[16,96,128]{2,1,0:T(8,128)(2,1)S(1)} %get-tuple-element.18), channel_id=2, replica_groups=mesh['x'=4,'z'=8,'y'=8,'c'=2] {'c'}, dimensions={0}, use_global_device_ids=true | all-gather | bytes 1179648 | tf_op jit(solution)/shard_map/all_gather | solution.py:376
  64.6 0.7 pair_sum.1
  65.3 0.0 copy-start.1
  65.3 7.2 %all-to-all-start.1 = ((bf16[8,96,128]{2,1,0:T(8,128)(2,1)}), bf16[8,96,128]{2,1,0:T(8,128)(2,1)S(1)}, u32[]{:S(2)}, u32[]{:S(2)}) async-start(bf16[8,96,128]{2,1,0:T(8,128)(2,1)} %pair_sum.1), calls=%async_computation.1 | async-start | bytes 393216 | tf_op jit(solution)/shard_map/all_to_all | solution.py:334
  72.6 0.0 copy-done.10
  72.6 0.8 convert_reduce_fusion
  73.4 10.0 %all-to-all-done.1.recv_ref = bf16[8,96,128]{2,1,0:T(8,128)(2,1)S(1)} async-done(((bf16[8,96,128]{2,1,0:T(8,128)(2,1)}), bf16[8,96,128]{2,1,0:T(8,128)(2,1)S(1)}, u32[]{:S(2)}, u32[]{:S(2)}) %all-to-all-start.1) | async-done | bytes 196640 | tf_op jit(solution)/shard_map/all_to_all | solution.py:334
  83.3 0.7 sum_and_spread.2
  84.0 4.0 %all-to-all-start.2 = ((bf16[8,96,128]{2,1,0:T(8,128)(2,1)}), bf16[8,96,128]{2,1,0:T(8,128)(2,1)}, u32[]{:S(2)}, u32[]{:S(2)}) async-start(bf16[8,96,128]{2,1,0:T(8,128)(2,1)} %sum_and_spread.2), calls=%async_computation.2 | async-start | bytes 393216 | tf_op jit(solution)/shard_map/all_to_all | solution.py:334
  88.1 0.1 copy.23.inv_ref
  88.2 0.0 copy-done
  88.2 0.0 copy-done.2
  88.2 0.3 fusion.1.back_ref
  88.5 9.3 %all-to-all-done.2 = bf16[8,96,128]{2,1,0:T(8,128)(2,1)} async-done(((bf16[8,96,128]{2,1,0:T(8,128)(2,1)}), bf16[8,96,128]{2,1,0:T(8,128)(2,1)}, u32[]{:S(2)}, u32[]{:S(2)}) %all-to-all-start.2) | async-done | bytes 196640 | tf_op jit(solution)/shard_map/all_to_all | solution.py:334
  97.9 2.3 %all_gather.15.pre_ref = bf16[16,96,128]{2,1,0:T(8,128)(2,1)S(1)} all-gather(bf16[8,96,128]{2,1,0:T(8,128)(2,1)} %all-to-all-done.2), channel_id=1, replica_groups=mesh['x'=4,'z'=8,'y'=8,'c'=2] {'c'}, dimensions={0}, use_global_device_ids=true | all-gather | bytes 589824 | tf_op jit(solution)/shard_map/all_gather | solution.py:378
  100.1 0.0 copy-done.1
  100.1 3.4 %second_layer.1 = (bf16[172,192]{1,0:T(8,128)(2,1)}, bf16[4,192,256]{2,1,0:T(8,128)(2,1)S(1)}) custom-call(bf16[16,96,128]{2,1,0:T(8,128)(2,1)S(1)} %all_gather.15.pre_ref, bf16[192,192]{1,0:T(8,128)(2,1)S(1)} %add_convert_fusion.adj_ref, f32[192,1]{1,0:T(8,128)S(1)} %copy.23.inv_ref, bf16[1024,1024]{1,0:T(8,128)(2,1)S(1)} %copy-done.1, ...), custom_call_target="tpu_custom_call" | custom-call | tf_op jit(solution)/shard_map/second_layer/pallas_call | solution.py:242
  103.5 13.2 %all_to_all.30.grad_ref = bf16[4,192,256]{2,1,0:T(8,128)(2,1)S(1)} all-to-all(bf16[4,192,256]{2,1,0:T(8,128)(2,1)S(1)} %get-tuple-element.19), channel_id=1, replica_groups=mesh['x'=4,'z'=8,'y'=8,'c'=2] {'x'}, dimensions={0} | all-to-all | bytes 786432 | tf_op jit(solution)/shard_map/all_to_all | solution.py:334
  116.8 0.0 all-gather.3.cloned.1.call-done.both_ref
  116.8 0.0 copy-start.3
  116.8 1.2 copy-done.3
  118.0 0.5 gradient_part.1
  118.5 13.5 %all_to_all.31.recv_ref = bf16[8,64,256]{2,1,0:T(8,128)(2,1)S(1)} all-to-all(bf16[8,64,256]{2,1,0:T(8,128)(2,1)S(1)} %bitcast.18), channel_id=1, replica_groups=mesh['x'=4,'z'=8,'y'=8,'c'=2] {'z'}, dimensions={0} | all-to-all | bytes 524288 | tf_op jit(solution)/shard_map/all_to_all | solution.py:334
  131.9 0.1 sum_and_spread.3
  132.1 31.4 %all_to_all.32 = bf16[32,64,256]{2,1,0:T(8,128)(2,1)S(1)} all-to-all(bf16[32,64,256]{2,1,0:T(8,128)(2,1)S(1)} %sum_and_spread.3), channel_id=1, replica_groups=mesh['x'=4,'z'=8,'y'=8,'c'=2] {'x','z'}, dimensions={0} | all-to-all | bytes 2097152 | tf_op jit(solution)/shard_map/all_to_all | solution.py:334
  163.4 1.0 assemble.1
  (4 shorter events, 0.0 us)
Async XLA Ops:
  7.2 81.1 %copy-start = (bf16[192,172]{0,1:T(8,128)(2,1)S(1)}, bf16[192,172]{0,1:T(8,128)(2,1)}, u32[]{:S(2)}) copy-start(bf16[192,172]{0,1:T(8,128)(2,1)} %param.23) | copy-start | bytes 198148
  7.2 1.0 copy-start.6
  8.2 0.9 copy-start.8
  9.1 0.7 copy-start.9
  10.1 11.8 %collective-permute-start = (bf16[544,256]{1,0:T(8,128)(2,1)S(1)}, bf16[544,256]{1,0:T(8,128)(2,1)S(1)}, u32[]{:S(2)}, u32[]{:S(2)}) collective-permute-start(bf16[544,256]{1,0:T(8,128)(2,1)S(1)} %get-tuple-element.14), channel_id=1, source_target_pairs={{0,128},{128,256},{256,384},{384,0},{1,129},{129,257},{257,385},{3... | collective-permute-start | bytes 835592 | tf_op jit(solution)/shard_map/ppermute | solution.py:360
  13.5 15.3 %collective-permute-start.1 = (bf16[544,256]{1,0:T(8,128)(2,1)S(1)}, bf16[544,256]{1,0:T(8,128)(2,1)S(1)}, u32[]{:S(2)}, u32[]{:S(2)}) collective-permute-start(bf16[544,256]{1,0:T(8,128)(2,1)S(1)} %get-tuple-element.15), channel_id=1, source_target_pairs={{0,384},{128,0},{256,128},{384,256},{1,385},{129,1},{257,129},{385... | collective-permute-start | bytes 835592 | tf_op jit(solution)/shard_map/ppermute | solution.py:360
  17.2 13.2 %collective-permute-start.2 = (bf16[544,256]{1,0:T(8,128)(2,1)S(1)}, bf16[544,256]{1,0:T(8,128)(2,1)S(1)}, u32[]{:S(2)}, u32[]{:S(2)}) collective-permute-start(bf16[544,256]{1,0:T(8,128)(2,1)S(1)} %get-tuple-element.16), channel_id=1, source_target_pairs={{0,256},{128,384},{256,0},{384,128},{1,257},{129,385},{257,1},{385... | collective-permute-start | bytes 835592 | tf_op jit(solution)/shard_map/ppermute | solution.py:360
  30.3 12.1 %copy-start.12 = (s32[192]{0:T(256)S(1)}, s32[192]{0:T(256)}, u32[]{:S(2)}) copy-start(s32[192]{0:T(256)} %param.16) | copy-start | bytes 2308
  30.4 30.6 %copy-start.4 = (bf16[256,1024]{1,0:T(8,128)(2,1)S(1)}, bf16[256,1024]{1,0:T(8,128)(2,1)}, u32[]{:S(2)}) copy-start(bf16[256,1024]{1,0:T(8,128)(2,1)} %self_ref.1) | copy-start | bytes 1572868
  30.4 30.6 %copy-start.5 = (bf16[256,1024]{1,0:T(8,128)(2,1)S(1)}, bf16[256,1024]{1,0:T(8,128)(2,1)}, u32[]{:S(2)}) copy-start(bf16[256,1024]{1,0:T(8,128)(2,1)} %neigh_ref.1) | copy-start | bytes 1572868
  30.4 30.6 %copy-start.7 = (bf16[192,256]{1,0:T(8,128)(2,1)S(1)}, bf16[192,256]{1,0:T(8,128)(2,1)}, u32[]{:S(2)}) copy-start(bf16[192,256]{1,0:T(8,128)(2,1)} %own_ref.1) | copy-start | bytes 294916
  32.4 29.7 %copy-start.11 = (s32[192]{0:T(256)S(1)}, s32[192]{0:T(256)}, u32[]{:S(2)}) copy-start(s32[192]{0:T(256)} %param.18) | copy-start | bytes 2308
  32.4 28.6 %all-to-all-start = ((bf16[8,192,256]{2,1,0:T(8,128)(2,1)}), bf16[8,192,256]{2,1,0:T(8,128)(2,1)S(1)}, u32[]{:S(2)}, u32[]{:S(2)}) async-start(bf16[8,192,256]{2,1,0:T(8,128)(2,1)} %bitcast.3), calls=%async_computation | async-start | bytes 1572864 | tf_op jit(solution)/shard_map/all_to_all | solution.py:334
  42.5 74.3 %all-gather.3.cloned.1.call-start = ((), (), s32[]{:S(2)}) async-start(), calls=%async_computation.6 | async-start | bytes 1310720 | tf_op jit(solution)/shard_map/all_gather | solution.py:374
  42.6 30.0 %copy-start.10 = (s32[192,10]{0,1:T(8,128)S(1)}, s32[192,10]{0,1:T(8,128)}, u32[]{:S(2)}) copy-start(s32[192,10]{0,1:T(8,128)} %param.17) | copy-start | bytes 23044
  62.1 26.1 %copy-start.2 = (bf16[1024,172]{0,1:T(8,128)(2,1)S(1)}, bf16[1024,172]{0,1:T(8,128)(2,1)}, u32[]{:S(2)}) copy-start(bf16[1024,172]{0,1:T(8,128)(2,1)} %param.22) | copy-start | bytes 1056772
  65.3 34.8 %copy-start.1 = (bf16[1024,1024]{1,0:T(8,128)(2,1)S(1)}, bf16[1024,1024]{1,0:T(8,128)(2,1)}, u32[]{:S(2)}) copy-start(bf16[1024,1024]{1,0:T(8,128)(2,1)} %two_ref.1) | copy-start | bytes 6291460
  65.3 18.0 %all-to-all-start.1 = ((bf16[8,96,128]{2,1,0:T(8,128)(2,1)}), bf16[8,96,128]{2,1,0:T(8,128)(2,1)S(1)}, u32[]{:S(2)}, u32[]{:S(2)}) async-start(bf16[8,96,128]{2,1,0:T(8,128)(2,1)} %pair_sum.1), calls=%async_computation.1 | async-start | bytes 393216 | tf_op jit(solution)/shard_map/all_to_all | solution.py:334
  84.0 13.8 %all-to-all-start.2 = ((bf16[8,96,128]{2,1,0:T(8,128)(2,1)}), bf16[8,96,128]{2,1,0:T(8,128)(2,1)}, u32[]{:S(2)}, u32[]{:S(2)}) async-start(bf16[8,96,128]{2,1,0:T(8,128)(2,1)} %sum_and_spread.2), calls=%async_computation.2 | async-start | bytes 393216 | tf_op jit(solution)/shard_map/all_to_all | solution.py:334
  116.8 1.2 copy-start.3
Sparse Core Ops, SparseCore 0:
  62.2 27.3 all-gather.2

commit v5 on v4

--- a/solution.py
+++ b/solution.py
@@ -12,7 +12,6 @@
 ROW_BLOCK = 256
 DEAD = 512.0
 MIB = 1024 * 1024
-GATHER_ROWS = 256
 NODE = ("x", "z")
 FEAT = ("y", "c")
 
@@ -33,36 +32,41 @@
 def payload_kernel(place_ref, index_hbm, count_hbm, table_hbm, *refs):
     outs = refs[:XS]
     index_ref, count_ref, table_ref, coded, sems = refs[XS:]
-    copies = [
-        pltpu.make_async_copy(source, target, sems.at[i])
-        for i, (source, target) in enumerate(
-            [(index_hbm, index_ref), (count_hbm, count_ref), (table_hbm, table_ref)]
-        )
-    ]
-    for copy in copies:
-        copy.start()
+    nodes = table_hbm.shape[0]
+    first = pltpu.make_async_copy(index_hbm, index_ref, sems.at[0])
+    second = pltpu.make_async_copy(count_hbm, count_ref, sems.at[1])
+    third = pltpu.make_async_copy(table_hbm, table_ref, sems.at[2 + 2 * XS])
+    first.start()
+    second.start()
+    third.start()
     slots, total = index_ref.shape
-    nodes = table_ref.shape[0]
-    per_x = total // XS
-    blocks = per_x // ROW_BLOCK
-    copies[0].wait()
-    copies[1].wait()
+    blocks = total // XS // ROW_BLOCK
+    extra = coded.shape[1] - slots * blocks
+    first.wait()
+    second.wait()
     index = index_ref[...]
     slot = lax.broadcasted_iota(jnp.int32, (slots, total), 0)
     code = jnp.where(index < 256, index, 255 - index).astype(jnp.float32)
     code = jnp.where(slot < count_ref[...], code, DEAD)
-    extra = coded.shape[1] - slots * blocks
     for x in range(XS):
         pieces = [
             code[:, (x * blocks + c) * ROW_BLOCK : (x * blocks + c + 1) * ROW_BLOCK]
             for c in range(blocks)
         ] + [jnp.full((extra, ROW_BLOCK), DEAD, jnp.float32)]
         coded[x] = jnp.concatenate(pieces, axis=0).astype(jnp.bfloat16)
-    copies[2].wait()
+    third.wait()
+    copies = []
     for shift in range(XS):
-        out = outs[shift]
-        out[0:nodes, :] = table_ref[...]
-        out[nodes:, :] = coded[lax.rem(place_ref[0] + shift, XS)]
+        target = outs[shift].at[pl.ds(0, nodes), :]
+        copies.append(pltpu.make_async_copy(table_ref, target, sems.at[2 + shift]))
+        copies[shift].start()
+    for shift in range(XS):
+        source = coded.at[lax.rem(place_ref[0] + shift, XS)]
+        target = outs[shift].at[pl.ds(nodes, coded.shape[1]), :]
+        copies.append(pltpu.make_async_copy(source, target, sems.at[2 + XS + shift]))
+        copies[XS + shift].start()
+    for copy in copies:
+        copy.wait()
 
 
 def make_payloads(place, index, count, table):
@@ -70,21 +74,20 @@
     nodes, width = table.shape
     used = slots * (total // XS // ROW_BLOCK)
     extra = -(-used // 16) * 16
-    vmem = pl.BlockSpec(memory_space=pltpu.VMEM)
     hbm = pl.BlockSpec(memory_space=pltpu.HBM)
     return pl.pallas_call(
         payload_kernel,
         in_specs=[pl.BlockSpec(memory_space=pltpu.SMEM), hbm, hbm, hbm],
-        out_specs=[vmem] * XS,
+        out_specs=[hbm] * XS,
         out_shape=[jax.ShapeDtypeStruct((nodes + extra, width), jnp.bfloat16)] * XS,
         scratch_shapes=[
             pltpu.VMEM(index.shape, index.dtype),
             pltpu.VMEM(count.shape, count.dtype),
             pltpu.VMEM(table.shape, table.dtype),
             pltpu.VMEM((XS, extra, ROW_BLOCK), jnp.bfloat16),
-            pltpu.SemaphoreType.DMA((3,)),
+            pltpu.SemaphoreType.DMA((3 + 2 * XS,)),
         ],
-        compiler_params=params(16),
+        compiler_params=params(60),
         name="payloads",
     )(place, index, count, table)
 
@@ -127,44 +130,31 @@
     )(*operands)
 
 
-def first_kernel(
-    recv_ref, degree_ref, own_ref, self_ref, neigh_ref, both_hbm, out_ref, both_ref, sem
-):
+def first_kernel(recv_ref, degree_ref, own_ref, self_ref, neigh_ref, mean_ref, out_ref):
     sums = recv_ref[0].astype(jnp.float32)
     for i in range(1, recv_ref.shape[0]):
         sums = sums + recv_ref[i].astype(jnp.float32)
     mean = (sums / degree_ref[...]).astype(jnp.bfloat16)
-    rows, width_in = own_ref.shape
-    both_ref[0:rows, 0:width_in] = own_ref[...]
-    both_ref[0:rows, width_in:] = mean
-    both_ref[rows:, :] = jnp.zeros((both_ref.shape[0] - rows, 2 * width_in), jnp.bfloat16)
-    copy = pltpu.make_async_copy(both_ref, both_hbm, sem)
-    copy.start()
+    mean_ref[...] = mean
     pre = (dot(own_ref[...], self_ref[...]) + dot(mean, neigh_ref[...])).astype(jnp.bfloat16)
     count, height, width = out_ref.shape
-    halves = rows // height
+    halves = pre.shape[0] // height
     for i in range(count):
         t, h = i // halves, i % halves
         out_ref[i] = pre[h * height : (h + 1) * height, t * width : (t + 1) * width]
-    copy.wait()
 
 
 def first_layer(recv, degree, own, self_weight, neigh_weight, pieces):
     rows, width = own.shape
     hidden = self_weight.shape[1]
     vmem = pl.BlockSpec(memory_space=pltpu.VMEM)
-    padded = max(rows, GATHER_ROWS)
     return pl.pallas_call(
         first_kernel,
         in_specs=[vmem] * 5,
-        out_specs=[pl.BlockSpec(memory_space=pltpu.HBM), vmem],
+        out_specs=[vmem] * 2,
         out_shape=[
-            jax.ShapeDtypeStruct((padded, 2 * width), jnp.bfloat16),
+            jax.ShapeDtypeStruct((rows, width), jnp.bfloat16),
             jax.ShapeDtypeStruct((pieces, rows // 2, 2 * hidden // pieces), jnp.bfloat16),
-        ],
-        scratch_shapes=[
-            pltpu.VMEM((padded, 2 * width), jnp.bfloat16),
-            pltpu.SemaphoreType.DMA(()),
         ],
         compiler_params=params(16),
         name="first_layer",
@@ -256,26 +246,29 @@
     )(pre, adjacency, inv_count, weight_two, weight_three, back_two)
 
 
-def gradient_kernel(both_ref, grad_ref, out_ref):
-    xs, rows, _ = grad_ref.shape
-    padded = both_ref.shape[0] // xs
-    total = None
-    for x in range(xs):
-        part = dot(both_ref[x * padded : x * padded + rows, :], grad_ref[x], ((0,), (0,)))
-        total = part if total is None else total + part
-    out_ref[...] = total.astype(jnp.bfloat16)
-
-
-def gradient_part(both, grad):
+def gradient_kernel(place_ref, *refs):
+    operands, grad_ref, out_ref = refs[:-2], refs[-2], refs[-1]
+    width = operands[0].shape[1]
+    for half in range(2):
+        total = None
+        for shift in range(XS):
+            source = lax.rem(place_ref[0] + (XS - shift), XS)
+            rows = operands[half * XS + shift][...]
+            part = dot(rows, grad_ref[source], ((0,), (0,)))
+            total = part if total is None else total + part
+        out_ref[half * width : (half + 1) * width, :] = total.astype(jnp.bfloat16)
+
+
+def gradient_part(place, own, mean, grad):
     vmem = pl.BlockSpec(memory_space=pltpu.VMEM)
     return pl.pallas_call(
         gradient_kernel,
-        in_specs=[vmem] * 2,
+        in_specs=[pl.BlockSpec(memory_space=pltpu.SMEM)] + [vmem] * (2 * XS + 1),
         out_specs=vmem,
-        out_shape=jax.ShapeDtypeStruct((both.shape[1], grad.shape[2]), jnp.bfloat16),
+        out_shape=jax.ShapeDtypeStruct((2 * own[0].shape[1], grad.shape[2]), jnp.bfloat16),
         compiler_params=params(16),
         name="gradient_part",
-    )(both, grad)
+    )(place, *own, *mean, grad)
 
 
 def spread_kernel(recv_ref, out_ref):
@@ -332,6 +325,10 @@
 
 def exchange(pieces, axis):
     return lax.all_to_all(pieces, axis, split_axis=0, concat_axis=0, tiled=True)
+
+
+def shift_x(array, steps):
+    return lax.ppermute(array, "x", [(i, (i + steps) % XS) for i in range(XS)])
 
 
 def body(
@@ -356,14 +353,15 @@
 
     place = lax.axis_index("x").reshape(1).astype(jnp.int32)
     payloads = make_payloads(place, neigh_index[0].T, neigh_count, features)
-    arrived = [
-        lax.ppermute(payloads[s], "x", [(i, (i + s) % XS) for i in range(XS)]) for s in (2, 1, 3)
-    ]
+    arrived = [shift_x(payloads[s], s) for s in (2, 1, 3)]
     running = gather_sum(slots, per_x, jnp.float32, None, payloads[:1])
     running = gather_sum(slots, per_x, jnp.float32, running, arrived[1:])
     parts = gather_sum(slots, per_x, jnp.bfloat16, running, arrived[:1])
+    parts, own_late = lax.optimization_barrier((parts, own_features))
+    own = [shift_x(own_late, s) for s in range(1, XS)]
     recv = exchange(parts.reshape(groups // XS, own_rows, width), "z")
-    both, pieces = first_layer(
+    recv, *own = lax.optimization_barrier((recv, *own))
+    mean_rows, pieces = first_layer(
         recv,
         degree[:, None].astype(jnp.float32),
         own_features,
@@ -371,11 +369,13 @@
         neigh_weight,
         splits,
     )
-    both = lax.all_gather(both, "x", axis=0, tiled=True)
+    mean = [shift_x(mean_rows, s) for s in range(1, XS)]
     core = lax.axis_index("c").reshape(1).astype(jnp.int32)
     paired = pair_sum(core, lax.all_gather(pieces, "c", axis=0, tiled=False))
-    pre_copies = spread(exchange(paired, "y"), paired.shape[0])
-    pre = lax.all_gather(exchange(pre_copies, "y"), "c", axis=0, tiled=True)
+    paired, mean[0], mean[2] = lax.optimization_barrier((exchange(paired, "y"), mean[0], mean[2]))
+    pre_copies = spread(paired, paired.shape[0])
+    pre, mean[1] = lax.optimization_barrier((exchange(pre_copies, "y"), mean[1]))
+    pre = lax.all_gather(pre, "c", axis=0, tiled=True)
 
     slot_ids = jnp.arange(local_index.shape[1], dtype=jnp.int32)
     live_slots = slot_ids[None, :] < local_count[:, None]
@@ -390,7 +390,7 @@
     logits, grad_one = second_layer(
         pre, adjacency, inv_count[:, None], weight_two, weight_three.T, back_two
     )
-    grad_part = gradient_part(both, exchange(grad_one, "x"))
+    grad_part = gradient_part(place, [own_features] + own, [mean_rows] + mean, exchange(grad_one, "x"))
     quarter = grad_part.shape[1]
     grad_recv = exchange(grad_part.reshape(groups // XS, -1, quarter), "z")
     grads = exchange(spread(grad_recv, groups), NODE)

time: 172 us -> 161 us (0.936)
  starting transfers between devices: 32.1 us -> 57.5 us
  waiting for transfers between devices: 44.5 us -> 22.4 us
  between operations: 14.3 us -> 0.96 us
  Pallas kernels: 12.3 us -> 14.4 us
  blocking collectives: 62.8 us -> 60.9 us
    all_to_all x3, waiting for transfers between devices: 37.6 us -> 4.66 us  [exchange(): return lax.all_to_all(pieces, axis, split_axis=0, concat_axis=0, tiled=True)]
    ppermute x3 -> x9, starting transfers between devices: 10.8 us -> 33.1 us  [shift_x(): return lax.ppermute(array, 'x', [(i, (i + steps) % XS) for i in range(XS)])]
    ppermute x3 -> x9, waiting for transfers between devices: 6.87 us -> 17.7 us  [shift_x(): return lax.ppermute(array, 'x', [(i, (i + steps) % XS) for i in range(XS)])]
    all_to_all x3, starting transfers between devices: 21.4 us -> 24.4 us  [exchange(): return lax.all_to_all(pieces, axis, split_axis=0, concat_axis=0, tiled=True)]
    pallas_call x1, Pallas kernels: 0.29 us -> 2.11 us  [make_payloads(): pl.pallas_call(payload_kernel, in_specs=[pl.BlockSpec(memory_space=pltpu....]
    unnamed x26 -> x24, local copies, waits for them, and re-layouts: 3.88 us -> 2.6 us
  transfers between devices with their start and end apart: 7 -> 12, of which waited for: 4 -> 8; matrix products, arithmetic and copies ran while one was open for 1% -> 1% of each run, Pallas kernels for 4% -> 2%
where the time goes in v5:
time: 161 us; the launch traced here: 160 us
  blocking collectives  60.9 us (38%)
  starting transfers between devices  57.5 us (36%)
  waiting for transfers between devices  22.4 us (14%)
  Pallas kernels  14.4 us (9%)
  local copies, waits for them, and re-layouts  2.83 us (2%)
    all_to_all x3, blocking collectives, exchange(): return lax.all_to_all(pieces, axis, split_axis=0, concat_axis=0, tiled=True)  56.4 us
    ppermute x9, starting transfers between devices, shift_x(): return lax.ppermute(array, 'x', [(i, (i + steps) % XS) for i in range(XS)])  33.1 us
    all_to_all x3, starting transfers between devices, exchange(): return lax.all_to_all(pieces, axis, split_axis=0, concat_axis=0, tiled=True)  24.4 us
    ppermute x9, waiting for transfers between devices, shift_x(): return lax.ppermute(array, 'x', [(i, (i + steps) % XS) for i in range(XS)])  17.7 us
    all_to_all x3, waiting for transfers between devices, exchange(): return lax.all_to_all(pieces, axis, split_axis=0, concat_axis=0, tiled=True)  4.66 us
    pallas_call x3, Pallas kernels, gather_sum(): pl.pallas_call(functools.partial(gather_kernel, slots, int(carried is not...  4.47 us
    pallas_call x1, Pallas kernels, second_layer(): pl.pallas_call(second_kernel, in_specs=[vmem] * 6, out_specs=[vmem, pl.Bl...  3.37 us
  transfers between devices with their start and end apart: 12, of which 8 were waited for; matrix products, arithmetic and copies ran while one was open for 1% of the time, Pallas kernels for 2%

profile of v5, /device:TPU:64, one launch (start us, length us, event | category | flops | bytes accessed | tf_op | source)
XLA Modules:
  0.0 160.0 jit_solution(15479140350512058412)
XLA Ops:
  0.6 0.0 copy-start
  0.7 2.1 %payloads.1 = (bf16[544,256]{1,0:T(8,128)(2,1)}, bf16[544,256]{1,0:T(8,128)(2,1)}, bf16[544,256]{1,0:T(8,128)(2,1)}, bf16[544,256]{1,0:T(8,128)(2,1)}) custom-call(s32[1]{0:T(128)} %bitcast.place_ref, s32[4,6144]{1,0:T(4,128)} %bitcast.19, s32[1,6144]{1,0:T(1,128)} %count_hbm.1, bf16[512,256]{1,0:T(8,128)(2,1)} %table_hbm.1), custom_call_target="tpu_custom_call" | custom-call | tf_op jit(solution)/shard_map/payloads/pallas_call | solution.py:78
  2.8 3.4 %collective-permute-start = (bf16[544,256]{1,0:T(8,128)(2,1)}, bf16[544,256]{1,0:T(8,128)(2,1)S(1)}, u32[]{:S(2)}, u32[]{:S(2)}) collective-permute-start(bf16[544,256]{1,0:T(8,128)(2,1)} %get-tuple-element.25), channel_id=1, source_target_pairs={{0,128},{128,256},{256,384},{384,0},{1,129},{129,257},{257,385},{3... | collective-permute-start | bytes 835592 | tf_op jit(solution)/shard_map/ppermute | solution.py:331
  6.2 3.7 %collective-permute-start.1 = (bf16[544,256]{1,0:T(8,128)(2,1)}, bf16[544,256]{1,0:T(8,128)(2,1)S(1)}, u32[]{:S(2)}, u32[]{:S(2)}) collective-permute-start(bf16[544,256]{1,0:T(8,128)(2,1)} %get-tuple-element.26), channel_id=1, source_target_pairs={{0,384},{128,0},{256,128},{384,256},{1,385},{129,1},{257,129},{385... | collective-permute-start | bytes 835592 | tf_op jit(solution)/shard_map/ppermute | solution.py:331
  9.8 3.7 %collective-permute-start.2 = (bf16[544,256]{1,0:T(8,128)(2,1)}, bf16[544,256]{1,0:T(8,128)(2,1)S(1)}, u32[]{:S(2)}, u32[]{:S(2)}) collective-permute-start(bf16[544,256]{1,0:T(8,128)(2,1)} %get-tuple-element.27), channel_id=1, source_target_pairs={{0,256},{128,384},{256,0},{384,128},{1,257},{129,385},{257,1},{385... | collective-permute-start | bytes 835592 | tf_op jit(solution)/shard_map/ppermute | solution.py:331
  13.6 0.0 copy-start.6
  13.6 0.9 copy-done.6
  14.5 1.0 gather_sum.3.refs_0_
  15.5 0.0 collective-permute-done.refs_1_
  15.5 6.2 %collective-permute-done.1.refs_2_ = bf16[544,256]{1,0:T(8,128)(2,1)S(1)} collective-permute-done((bf16[544,256]{1,0:T(8,128)(2,1)}, bf16[544,256]{1,0:T(8,128)(2,1)S(1)}, u32[]{:S(2)}, u32[]{:S(2)}) %collective-permute-start.1) | collective-permute-done | bytes 278560 | tf_op jit(solution)/shard_map/ppermute | solution.py:331
  21.8 1.6 gather_sum.4.refs_0_
  23.3 0.0 copy-start.5
  23.3 0.0 copy-start.2
  23.4 0.0 collective-permute-done.2.refs_1_
  23.4 1.9 %gather_sum.5 = bf16[1536,256]{1,0:T(8,128)(2,1)} custom-call(f32[1536,256]{1,0:T(8,128)S(1)} %gather_sum.4.refs_0_, bf16[544,256]{1,0:T(8,128)(2,1)S(1)} %collective-permute-done.2.refs_1_), custom_call_target="tpu_custom_call" | custom-call | tf_op jit(solution)/shard_map/gather_sum/pallas_call | solution.py:123
  25.3 0.0 copy-start.11
  25.3 10.1 %all-to-all-start = ((bf16[8,192,256]{2,1,0:T(8,128)(2,1)}), bf16[8,192,256]{2,1,0:T(8,128)(2,1)S(1)}, u32[]{:S(2)}, u32[]{:S(2)}) async-start(bf16[8,192,256]{2,1,0:T(8,128)(2,1)} %bitcast.3), calls=%async_computation | async-start | bytes 1572864 | tf_op jit(solution)/shard_map/all_to_all | solution.py:327
  35.4 0.0 copy-done.5
  35.4 3.0 %collective-permute-start.3 = (bf16[192,256]{1,0:T(8,128)(2,1)S(1)}, bf16[192,256]{1,0:T(8,128)(2,1)S(1)}, u32[]{:S(2)}, u32[]{:S(2)}) collective-permute-start(bf16[192,256]{1,0:T(8,128)(2,1)S(1)} %copy-done.5), channel_id=1, source_target_pairs={{0,128},{128,256},{256,384},{384,0},{1,129},{129,257},{257,385},{3... | collective-permute-start | bytes 294920 | tf_op jit(solution)/shard_map/ppermute | solution.py:331
  38.4 5.8 %collective-permute-start.4 = (bf16[192,256]{1,0:T(8,128)(2,1)S(1)}, bf16[192,256]{1,0:T(8,128)(2,1)S(1)}, u32[]{:S(2)}, u32[]{:S(2)}) collective-permute-start(bf16[192,256]{1,0:T(8,128)(2,1)S(1)} %copy-done.5), channel_id=1, source_target_pairs={{0,256},{128,384},{256,0},{384,128},{1,257},{129,385},{257,1},{385... | collective-permute-start | bytes 294920 | tf_op jit(solution)/shard_map/ppermute | solution.py:331
  44.2 1.9 %collective-permute-start.5 = (bf16[192,256]{1,0:T(8,128)(2,1)S(1)}, bf16[192,256]{1,0:T(8,128)(2,1)}, u32[]{:S(2)}, u32[]{:S(2)}) collective-permute-start(bf16[192,256]{1,0:T(8,128)(2,1)S(1)} %copy-done.5), channel_id=1, source_target_pairs={{0,384},{128,0},{256,128},{384,256},{1,385},{129,1},{257,129},{385... | collective-permute-start | bytes 294920 | tf_op jit(solution)/shard_map/ppermute | solution.py:331
  46.2 0.0 copy-done
  46.2 0.0 copy-done.2
  46.2 0.3 fusion.1.back_ref
  46.5 0.0 copy-done.11
  46.5 0.1 copy.22.degree_ref
  46.6 0.0 copy-start.10
  46.6 0.0 copy-start.9
  46.7 0.0 collective-permute-done.3.refs_1_
  46.7 0.2 collective-permute-done.4.refs_2_
  46.8 4.0 %collective-permute-done.5.refs_3_ = bf16[192,256]{1,0:T(8,128)(2,1)} collective-permute-done((bf16[192,256]{1,0:T(8,128)(2,1)S(1)}, bf16[192,256]{1,0:T(8,128)(2,1)}, u32[]{:S(2)}, u32[]{:S(2)}) %collective-permute-start.5) | collective-permute-done | bytes 98336 | tf_op jit(solution)/shard_map/ppermute | solution.py:331
  50.9 2.9 %all-to-all-done.recv_ref = bf16[8,192,256]{2,1,0:T(8,128)(2,1)S(1)} async-done(((bf16[8,192,256]{2,1,0:T(8,128)(2,1)}), bf16[8,192,256]{2,1,0:T(8,128)(2,1)S(1)}, u32[]{:S(2)}, u32[]{:S(2)}) %all-to-all-start) | async-done | bytes 786464 | tf_op jit(solution)/shard_map/all_to_all | solution.py:327
  53.8 0.0 copy-done.3
  53.8 0.0 copy-done.4
  53.8 0.4 first_layer.1
  54.2 0.0 copy-start.7
  54.3 2.4 %all-gather = bf16[32,96,128]{2,1,0:T(8,128)(2,1)S(1)} all-gather(bf16[16,96,128]{2,1,0:T(8,128)(2,1)S(1)} %get-tuple-element.35), channel_id=2, replica_groups=mesh['x'=4,'z'=8,'y'=8,'c'=2] {'c'}, dimensions={0}, use_global_device_ids=true | all-gather | bytes 1179648 | tf_op jit(solution)/shard_map/all_gather | solution.py:374
  56.6 0.0 copy-done.7
  56.6 0.7 pair_sum.1
  57.4 7.1 %all-to-all-start.1 = ((bf16[8,96,128]{2,1,0:T(8,128)(2,1)}), bf16[8,96,128]{2,1,0:T(8,128)(2,1)S(1)}, u32[]{:S(2)}, u32[]{:S(2)}) async-start(bf16[8,96,128]{2,1,0:T(8,128)(2,1)} %pair_sum.1), calls=%async_computation.1 | async-start | bytes 393216 | tf_op jit(solution)/shard_map/all_to_all | solution.py:327
  64.5 0.0 copy-done.10
  64.5 5.1 %collective-permute-start.6 = (bf16[192,256]{1,0:T(8,128)(2,1)}, bf16[192,256]{1,0:T(8,128)(2,1)S(1)}, u32[]{:S(2)}, u32[]{:S(2)}) collective-permute-start(bf16[192,256]{1,0:T(8,128)(2,1)} %copy-done.7), channel_id=1, source_target_pairs={{0,128},{128,256},{256,384},{384,0},{1,129},{129,257},{257,385},{3... | collective-permute-start | bytes 294920 | tf_op jit(solution)/shard_map/ppermute | solution.py:331
  69.6 2.5 %collective-permute-start.7 = (bf16[192,256]{1,0:T(8,128)(2,1)}, bf16[192,256]{1,0:T(8,128)(2,1)S(1)}, u32[]{:S(2)}, u32[]{:S(2)}) collective-permute-start(bf16[192,256]{1,0:T(8,128)(2,1)} %copy-done.7), channel_id=1, source_target_pairs={{0,384},{128,0},{256,128},{384,256},{1,385},{129,1},{257,129},{385... | collective-permute-start | bytes 294920 | tf_op jit(solution)/shard_map/ppermute | solution.py:331
  72.1 0.0 copy-done.9
  72.1 0.8 convert_reduce_fusion
  72.9 0.3 collective-permute-done.6.refs_5_
  73.2 3.1 %collective-permute-done.7.refs_7_ = bf16[192,256]{1,0:T(8,128)(2,1)S(1)} collective-permute-done((bf16[192,256]{1,0:T(8,128)(2,1)}, bf16[192,256]{1,0:T(8,128)(2,1)S(1)}, u32[]{:S(2)}, u32[]{:S(2)}) %collective-permute-start.7) | collective-permute-done | bytes 98336 | tf_op jit(solution)/shard_map/ppermute | solution.py:331
  76.3 0.0 all-to-all-done.1.recv_ref
  76.3 0.7 sum_and_spread.2
  77.0 7.2 %all-to-all-start.2 = ((bf16[8,96,128]{2,1,0:T(8,128)(2,1)}), bf16[8,96,128]{2,1,0:T(8,128)(2,1)S(1)}, u32[]{:S(2)}, u32[]{:S(2)}) async-start(bf16[8,96,128]{2,1,0:T(8,128)(2,1)} %sum_and_spread.2), calls=%async_computation.2 | async-start | bytes 393216 | tf_op jit(solution)/shard_map/all_to_all | solution.py:327
  84.3 0.0 copy-done.8
  84.3 4.0 %collective-permute-start.8 = (bf16[192,256]{1,0:T(8,128)(2,1)S(1)}, bf16[192,256]{1,0:T(8,128)(2,1)S(1)}, u32[]{:S(2)}, u32[]{:S(2)}) collective-permute-start(bf16[192,256]{1,0:T(8,128)(2,1)S(1)} %copy-done.8), channel_id=1, source_target_pairs={{0,256},{128,384},{256,0},{384,128},{1,257},{129,385},{257,1},{385... | collective-permute-start | bytes 294920 | tf_op jit(solution)/shard_map/ppermute | solution.py:331
  88.2 0.1 copy.23.inv_ref
  88.4 3.9 %collective-permute-done.8.refs_6_ = bf16[192,256]{1,0:T(8,128)(2,1)S(1)} collective-permute-done((bf16[192,256]{1,0:T(8,128)(2,1)S(1)}, bf16[192,256]{1,0:T(8,128)(2,1)S(1)}, u32[]{:S(2)}, u32[]{:S(2)}) %collective-permute-start.8) | collective-permute-done | bytes 98336 | tf_op jit(solution)/shard_map/ppermute | solution.py:331
  92.3 1.7 %all-to-all-done.2 = bf16[8,96,128]{2,1,0:T(8,128)(2,1)S(1)} async-done(((bf16[8,96,128]{2,1,0:T(8,128)(2,1)}), bf16[8,96,128]{2,1,0:T(8,128)(2,1)S(1)}, u32[]{:S(2)}, u32[]{:S(2)}) %all-to-all-start.2) | async-done | bytes 196640 | tf_op jit(solution)/shard_map/all_to_all | solution.py:327
  94.0 2.1 %all_gather.11.pre_ref = bf16[16,96,128]{2,1,0:T(8,128)(2,1)S(1)} all-gather(bf16[8,96,128]{2,1,0:T(8,128)(2,1)S(1)} %all-to-all-done.2), channel_id=1, replica_groups=mesh['x'=4,'z'=8,'y'=8,'c'=2] {'c'}, dimensions={0}, use_global_device_ids=true | all-gather | bytes 589824 | tf_op jit(solution)/shard_map/all_gather | solution.py:378
  96.1 1.6 copy-done.1
  97.7 3.4 %second_layer.1 = (bf16[172,192]{1,0:T(8,128)(2,1)}, bf16[4,192,256]{2,1,0:T(8,128)(2,1)S(1)}) custom-call(bf16[16,96,128]{2,1,0:T(8,128)(2,1)S(1)} %all_gather.11.pre_ref, bf16[192,192]{1,0:T(8,128)(2,1)S(1)} %add_convert_fusion.adj_ref, f32[192,1]{1,0:T(8,128)S(1)} %copy.23.inv_ref, bf16[1024,1024]{1,0:T(8,128)(2,1)S(1)} %copy-done.1, ...), custom_call_target="tpu_custom_call" | custom-call | tf_op jit(solution)/shard_map/second_layer/pallas_call | solution.py:232
  101.1 11.5 %all_to_all.30.refs_8_ = bf16[4,192,256]{2,1,0:T(8,128)(2,1)S(1)} all-to-all(bf16[4,192,256]{2,1,0:T(8,128)(2,1)S(1)} %get-tuple-element.41), channel_id=1, replica_groups=mesh['x'=4,'z'=8,'y'=8,'c'=2] {'x'}, dimensions={0} | all-to-all | bytes 786432 | tf_op jit(solution)/shard_map/all_to_all | solution.py:327
  112.6 1.4 gradient_part.1
  114.0 13.5 %all_to_all.31.recv_ref = bf16[8,64,256]{2,1,0:T(8,128)(2,1)S(1)} all-to-all(bf16[8,64,256]{2,1,0:T(8,128)(2,1)S(1)} %bitcast.18), channel_id=1, replica_groups=mesh['x'=4,'z'=8,'y'=8,'c'=2] {'z'}, dimensions={0} | all-to-all | bytes 524288 | tf_op jit(solution)/shard_map/all_to_all | solution.py:327
  127.4 0.1 sum_and_spread.3
  127.6 31.4 %all_to_all.32 = bf16[32,64,256]{2,1,0:T(8,128)(2,1)S(1)} all-to-all(bf16[32,64,256]{2,1,0:T(8,128)(2,1)S(1)} %sum_and_spread.3), channel_id=1, replica_groups=mesh['x'=4,'z'=8,'y'=8,'c'=2] {'x','z'}, dimensions={0} | all-to-all | bytes 2097152 | tf_op jit(solution)/shard_map/all_to_all | solution.py:327
  159.0 1.0 assemble.1
  (8 shorter events, 0.0 us)
Async XLA Ops:
  0.6 45.5 %copy-start = (bf16[192,172]{0,1:T(8,128)(2,1)S(1)}, bf16[192,172]{0,1:T(8,128)(2,1)}, u32[]{:S(2)}) copy-start(bf16[192,172]{0,1:T(8,128)(2,1)} %param.23) | copy-start | bytes 198148
  2.8 12.8 %collective-permute-start = (bf16[544,256]{1,0:T(8,128)(2,1)}, bf16[544,256]{1,0:T(8,128)(2,1)S(1)}, u32[]{:S(2)}, u32[]{:S(2)}) collective-permute-start(bf16[544,256]{1,0:T(8,128)(2,1)} %get-tuple-element.25), channel_id=1, source_target_pairs={{0,128},{128,256},{256,384},{384,0},{1,129},{129,257},{257,385},{3... | collective-permute-start | bytes 835592 | tf_op jit(solution)/shard_map/ppermute | solution.py:331
  6.2 15.6 %collective-permute-start.1 = (bf16[544,256]{1,0:T(8,128)(2,1)}, bf16[544,256]{1,0:T(8,128)(2,1)S(1)}, u32[]{:S(2)}, u32[]{:S(2)}) collective-permute-start(bf16[544,256]{1,0:T(8,128)(2,1)} %get-tuple-element.26), channel_id=1, source_target_pairs={{0,384},{128,0},{256,128},{384,256},{1,385},{129,1},{257,129},{385... | collective-permute-start | bytes 835592 | tf_op jit(solution)/shard_map/ppermute | solution.py:331
  9.8 13.5 %collective-permute-start.2 = (bf16[544,256]{1,0:T(8,128)(2,1)}, bf16[544,256]{1,0:T(8,128)(2,1)S(1)}, u32[]{:S(2)}, u32[]{:S(2)}) collective-permute-start(bf16[544,256]{1,0:T(8,128)(2,1)} %get-tuple-element.27), channel_id=1, source_target_pairs={{0,256},{128,384},{256,0},{384,128},{1,257},{129,385},{257,1},{385... | collective-permute-start | bytes 835592 | tf_op jit(solution)/shard_map/ppermute | solution.py:331
  13.6 1.0 copy-start.6
  23.3 12.1 %copy-start.5 = (bf16[192,256]{1,0:T(8,128)(2,1)S(1)}, bf16[192,256]{1,0:T(8,128)(2,1)}, u32[]{:S(2)}) copy-start(bf16[192,256]{1,0:T(8,128)(2,1)} %refs_0_.1) | copy-start | bytes 294916
  23.3 22.8 %copy-start.2 = (bf16[1024,172]{0,1:T(8,128)(2,1)S(1)}, bf16[1024,172]{0,1:T(8,128)(2,1)}, u32[]{:S(2)}) copy-start(bf16[1024,172]{0,1:T(8,128)(2,1)} %param.22) | copy-start | bytes 1056772
  25.3 21.2 %copy-start.11 = (s32[192]{0:T(256)S(1)}, s32[192]{0:T(256)}, u32[]{:S(2)}) copy-start(s32[192]{0:T(256)} %param.16) | copy-start | bytes 2308
  25.3 28.5 %copy-start.3 = (bf16[256,1024]{1,0:T(8,128)(2,1)S(1)}, bf16[256,1024]{1,0:T(8,128)(2,1)}, u32[]{:S(2)}) copy-start(bf16[256,1024]{1,0:T(8,128)(2,1)} %self_ref.1) | copy-start | bytes 1572868
  25.3 28.5 %copy-start.4 = (bf16[256,1024]{1,0:T(8,128)(2,1)S(1)}, bf16[256,1024]{1,0:T(8,128)(2,1)}, u32[]{:S(2)}) copy-start(bf16[256,1024]{1,0:T(8,128)(2,1)} %neigh_ref.1) | copy-start | bytes 1572868
  25.3 28.5 %all-to-all-start = ((bf16[8,192,256]{2,1,0:T(8,128)(2,1)}), bf16[8,192,256]{2,1,0:T(8,128)(2,1)S(1)}, u32[]{:S(2)}, u32[]{:S(2)}) async-start(bf16[8,192,256]{2,1,0:T(8,128)(2,1)} %bitcast.3), calls=%async_computation | async-start | bytes 1572864 | tf_op jit(solution)/shard_map/all_to_all | solution.py:327
  35.4 11.3 %collective-permute-start.3 = (bf16[192,256]{1,0:T(8,128)(2,1)S(1)}, bf16[192,256]{1,0:T(8,128)(2,1)S(1)}, u32[]{:S(2)}, u32[]{:S(2)}) collective-permute-start(bf16[192,256]{1,0:T(8,128)(2,1)S(1)} %copy-done.5), channel_id=1, source_target_pairs={{0,128},{128,256},{256,384},{384,0},{1,129},{129,257},{257,385},{3... | collective-permute-start | bytes 294920 | tf_op jit(solution)/shard_map/ppermute | solution.py:331
  38.4 8.4 %collective-permute-start.4 = (bf16[192,256]{1,0:T(8,128)(2,1)S(1)}, bf16[192,256]{1,0:T(8,128)(2,1)S(1)}, u32[]{:S(2)}, u32[]{:S(2)}) collective-permute-start(bf16[192,256]{1,0:T(8,128)(2,1)S(1)} %copy-done.5), channel_id=1, source_target_pairs={{0,256},{128,384},{256,0},{384,128},{1,257},{129,385},{257,1},{385... | collective-permute-start | bytes 294920 | tf_op jit(solution)/shard_map/ppermute | solution.py:331
  44.2 6.6 %collective-permute-start.5 = (bf16[192,256]{1,0:T(8,128)(2,1)S(1)}, bf16[192,256]{1,0:T(8,128)(2,1)}, u32[]{:S(2)}, u32[]{:S(2)}) collective-permute-start(bf16[192,256]{1,0:T(8,128)(2,1)S(1)} %copy-done.5), channel_id=1, source_target_pairs={{0,384},{128,0},{256,128},{384,256},{1,385},{129,1},{257,129},{385... | collective-permute-start | bytes 294920 | tf_op jit(solution)/shard_map/ppermute | solution.py:331
  46.6 17.8 %copy-start.10 = (s32[192]{0:T(256)S(1)}, s32[192]{0:T(256)}, u32[]{:S(2)}) copy-start(s32[192]{0:T(256)} %param.18) | copy-start | bytes 2308
  46.6 25.5 %copy-start.9 = (s32[192,10]{0,1:T(8,128)S(1)}, s32[192,10]{0,1:T(8,128)}, u32[]{:S(2)}) copy-start(s32[192,10]{0,1:T(8,128)} %param.17) | copy-start | bytes 23044
  54.2 2.4 %copy-start.7 = (bf16[192,256]{1,0:T(8,128)(2,1)}, bf16[192,256]{1,0:T(8,128)(2,1)S(1)}, u32[]{:S(2)}) copy-start(bf16[192,256]{1,0:T(8,128)(2,1)S(1)} %get-tuple-element.34.refs_4_) | copy-start | bytes 294916
  56.6 27.6 %copy-start.8 = (bf16[192,256]{1,0:T(8,128)(2,1)S(1)}, bf16[192,256]{1,0:T(8,128)(2,1)}, u32[]{:S(2)}) copy-start(bf16[192,256]{1,0:T(8,128)(2,1)} %copy-done.7) | copy-start | bytes 294916
  57.4 19.0 %all-to-all-start.1 = ((bf16[8,96,128]{2,1,0:T(8,128)(2,1)}), bf16[8,96,128]{2,1,0:T(8,128)(2,1)S(1)}, u32[]{:S(2)}, u32[]{:S(2)}) async-start(bf16[8,96,128]{2,1,0:T(8,128)(2,1)} %pair_sum.1), calls=%async_computation.1 | async-start | bytes 393216 | tf_op jit(solution)/shard_map/all_to_all | solution.py:327
  64.5 8.7 %collective-permute-start.6 = (bf16[192,256]{1,0:T(8,128)(2,1)}, bf16[192,256]{1,0:T(8,128)(2,1)S(1)}, u32[]{:S(2)}, u32[]{:S(2)}) collective-permute-start(bf16[192,256]{1,0:T(8,128)(2,1)} %copy-done.7), channel_id=1, source_target_pairs={{0,128},{128,256},{256,384},{384,0},{1,129},{129,257},{257,385},{3... | collective-permute-start | bytes 294920 | tf_op jit(solution)/shard_map/ppermute | solution.py:331
  69.6 6.7 %collective-permute-start.7 = (bf16[192,256]{1,0:T(8,128)(2,1)}, bf16[192,256]{1,0:T(8,128)(2,1)S(1)}, u32[]{:S(2)}, u32[]{:S(2)}) collective-permute-start(bf16[192,256]{1,0:T(8,128)(2,1)} %copy-done.7), channel_id=1, source_target_pairs={{0,384},{128,0},{256,128},{384,256},{1,385},{129,1},{257,129},{385... | collective-permute-start | bytes 294920 | tf_op jit(solution)/shard_map/ppermute | solution.py:331
  77.0 17.0 %all-to-all-start.2 = ((bf16[8,96,128]{2,1,0:T(8,128)(2,1)}), bf16[8,96,128]{2,1,0:T(8,128)(2,1)S(1)}, u32[]{:S(2)}, u32[]{:S(2)}) async-start(bf16[8,96,128]{2,1,0:T(8,128)(2,1)} %sum_and_spread.2), calls=%async_computation.2 | async-start | bytes 393216 | tf_op jit(solution)/shard_map/all_to_all | solution.py:327
  84.3 8.0 %collective-permute-start.8 = (bf16[192,256]{1,0:T(8,128)(2,1)S(1)}, bf16[192,256]{1,0:T(8,128)(2,1)S(1)}, u32[]{:S(2)}, u32[]{:S(2)}) collective-permute-start(bf16[192,256]{1,0:T(8,128)(2,1)S(1)} %copy-done.8), channel_id=1, source_target_pairs={{0,256},{128,384},{256,0},{384,128},{1,257},{129,385},{257,1},{385... | collective-permute-start | bytes 294920 | tf_op jit(solution)/shard_map/ppermute | solution.py:331
  96.1 1.6 copy-start.1

commit v6 on v5

--- a/solution.py
+++ b/solution.py
@@ -87,13 +87,18 @@
             pltpu.VMEM((XS, extra, ROW_BLOCK), jnp.bfloat16),
             pltpu.SemaphoreType.DMA((3 + 2 * XS,)),
         ],
-        compiler_params=params(60),
+        compiler_params=params(16),
         name="payloads",
     )(place, index, count, table)
 
 
-def gather_kernel(slots, carried, *refs):
-    payloads, out_ref = refs[carried:-1], refs[-1]
+def gather_kernel(slots, carried, staged, *refs):
+    if staged:
+        *refs, out_hbm, out_ref, sems = refs
+        copies = []
+    else:
+        *refs, out_ref = refs
+    payloads = refs[carried:]
     blocks = out_ref.shape[0] // ROW_BLOCK
     extra = -(-slots * blocks // 16) * 16
     nodes = payloads[0].shape[0] - extra
@@ -114,17 +119,30 @@
             part = dot(hits, ref[0:nodes, :])
             total = part if total is None else total + part
         out_ref[rows, :] = total.astype(out_ref.dtype)
-
-
-def gather_sum(slots, rows, dtype, carried, payloads):
+        if staged:
+            block = pl.ds(c * ROW_BLOCK, ROW_BLOCK)
+            copies.append(pltpu.make_async_copy(out_ref.at[block], out_hbm.at[block], sems.at[c]))
+            copies[c].start()
+    if staged:
+        for copy in copies:
+            copy.wait()
+
+
+def gather_sum(slots, rows, dtype, carried, payloads, staged=False):
     width = payloads[0].shape[1]
     operands = ([carried] if carried is not None else []) + list(payloads)
     vmem = pl.BlockSpec(memory_space=pltpu.VMEM)
     return pl.pallas_call(
-        functools.partial(gather_kernel, slots, int(carried is not None)),
+        functools.partial(gather_kernel, slots, int(carried is not None), staged),
         in_specs=[vmem] * len(operands),
-        out_specs=vmem,
+        out_specs=pl.BlockSpec(memory_space=pl.ANY) if staged else vmem,
         out_shape=jax.ShapeDtypeStruct((rows, width), dtype),
+        scratch_shapes=[
+            pltpu.VMEM((rows, width), dtype),
+            pltpu.SemaphoreType.DMA((rows // ROW_BLOCK,)),
+        ]
+        if staged
+        else [],
         compiler_params=params(16),
         name="gather_sum",
     )(*operands)
@@ -185,10 +203,10 @@
 
 
 def second_kernel(
-    pre_ref, adj_ref, inv_ref, two_ref, three_ref, back_ref, logits_ref, grad_hbm, grad_ref, sem
+    pre_ref, adj_ref, two_ref, three_ref, cot_ref, logits_out, grad_ref, logits_ref, sem
 ):
     count, height, width = pre_ref.shape
-    halves = inv_ref.shape[0] // height
+    halves = adj_ref.shape[0] // height
     strips = [
         jnp.concatenate([pre_ref[t * halves + h] for h in range(halves)], axis=0)
         for t in range(count // halves)
@@ -198,15 +216,18 @@
     first_hidden = (pre * gate).astype(jnp.bfloat16)
     slope = (gate + pre * gate * (1.0 - gate)).astype(jnp.bfloat16).astype(jnp.float32)
     adjacency = adj_ref[...]
-    inv = inv_ref[...]
+    inv = 1.0 / jnp.sum(adjacency.astype(jnp.float32), axis=1, keepdims=True)
     mixed = (dot(adjacency, first_hidden) * inv).astype(jnp.bfloat16)
     pre_two = dot(mixed, two_ref[...])
     gate_two = jax.nn.sigmoid(pre_two)
     second_hidden = (pre_two * gate_two).astype(jnp.bfloat16)
     across = ((1,), (1,))
     logits_ref[...] = dot(three_ref[...], second_hidden, across).astype(jnp.bfloat16)
+    copy = pltpu.make_async_copy(logits_ref, logits_out, sem)
+    copy.start()
     slope_two = gate_two + pre_two * gate_two * (1.0 - gate_two)
-    grad_two = (back_ref[...] * slope_two).astype(jnp.bfloat16)
+    back_two = dot(cot_ref[...], three_ref[...], ((0,), (0,)))
+    grad_two = (back_two * slope_two).astype(jnp.bfloat16)
     grad_mixed = dot(grad_two, two_ref[...], across) * inv
     high = grad_mixed.astype(jnp.bfloat16)
     rest = grad_mixed - high.astype(jnp.float32)
@@ -220,30 +241,29 @@
     quarter = grad_ref.shape[2]
     for x in range(grad_ref.shape[0]):
         grad_ref[x] = grad_one[:, x * quarter : (x + 1) * quarter]
-    copy = pltpu.make_async_copy(grad_ref, grad_hbm, sem)
-    copy.start()
     copy.wait()
 
 
-def second_layer(pre, adjacency, inv_count, weight_two, weight_three, back_two):
+def second_layer(pre, adjacency, weight_two, weight_three, cotangent):
     rows = adjacency.shape[0]
     hidden = weight_two.shape[0]
+    classes = weight_three.shape[0]
     vmem = pl.BlockSpec(memory_space=pltpu.VMEM)
     return pl.pallas_call(
         second_kernel,
-        in_specs=[vmem] * 6,
-        out_specs=[vmem, pl.BlockSpec(memory_space=pltpu.HBM)],
+        in_specs=[vmem] * 5,
+        out_specs=[pl.BlockSpec(memory_space=pl.ANY), vmem],
         out_shape=[
-            jax.ShapeDtypeStruct((weight_three.shape[0], rows), jnp.bfloat16),
+            jax.ShapeDtypeStruct((classes, rows), jnp.bfloat16),
             jax.ShapeDtypeStruct((XS, rows, hidden // XS), jnp.bfloat16),
         ],
         scratch_shapes=[
-            pltpu.VMEM((XS, rows, hidden // XS), jnp.bfloat16),
+            pltpu.VMEM((classes, rows), jnp.bfloat16),
             pltpu.SemaphoreType.DMA(()),
         ],
         compiler_params=params(24),
         name="second_layer",
-    )(pre, adjacency, inv_count, weight_two, weight_three, back_two)
+    )(pre, adjacency, weight_two, weight_three, cotangent)
 
 
 def gradient_kernel(place_ref, *refs):
@@ -356,7 +376,7 @@
     arrived = [shift_x(payloads[s], s) for s in (2, 1, 3)]
     running = gather_sum(slots, per_x, jnp.float32, None, payloads[:1])
     running = gather_sum(slots, per_x, jnp.float32, running, arrived[1:])
-    parts = gather_sum(slots, per_x, jnp.bfloat16, running, arrived[:1])
+    parts = gather_sum(slots, per_x, jnp.bfloat16, running, arrived[:1], staged=True)
     parts, own_late = lax.optimization_barrier((parts, own_features))
     own = [shift_x(own_late, s) for s in range(1, XS)]
     recv = exchange(parts.reshape(groups // XS, own_rows, width), "z")
@@ -385,10 +405,8 @@
     adjacency = (
         jnp.sum(slot_hits.astype(jnp.float32), axis=1) + jnp.eye(own_rows, dtype=jnp.float32)
     ).astype(jnp.bfloat16)
-    inv_count = 1.0 / (1.0 + local_count.astype(jnp.float32))
-    back_two = dot(cotangent, weight_three, ((1,), (1,)))
     logits, grad_one = second_layer(
-        pre, adjacency, inv_count[:, None], weight_two, weight_three.T, back_two
+        pre, adjacency, weight_two, weight_three.T, cotangent.T
     )
     grad_part = gradient_part(place, [own_features] + own, [mean_rows] + mean, exchange(grad_one, "x"))
     quarter = grad_part.shape[1]

time: 161 us -> 158 us (0.981)
  Pallas kernels: 14.4 us -> 10.4 us
    pallas_call x1, Pallas kernels: 2.11 us -> 0.48 us  [make_payloads(): pl.pallas_call(payload_kernel, in_specs=[pl.BlockSpec(memory_space=pltpu....]
where the time goes in v6:
time: 158 us; the launch traced here: 157 us
  blocking collectives  61.2 us (39%)
  starting transfers between devices  57.5 us (36%)
  waiting for transfers between devices  23.4 us (15%)
  Pallas kernels  10.4 us (7%)
  local copies, waits for them, and re-layouts  2.75 us (2%)
    all_to_all x3, blocking collectives, exchange(): return lax.all_to_all(pieces, axis, split_axis=0, concat_axis=0, tiled=True)  56.5 us
    ppermute x9, starting transfers between devices, shift_x(): return lax.ppermute(array, 'x', [(i, (i + steps) % XS) for i in range(XS)])  33.2 us
    all_to_all x3, starting transfers between devices, exchange(): return lax.all_to_all(pieces, axis, split_axis=0, concat_axis=0, tiled=True)  24.3 us
    ppermute x9, waiting for transfers between devices, shift_x(): return lax.ppermute(array, 'x', [(i, (i + steps) % XS) for i in range(XS)])  19.3 us
    pallas_call x3, Pallas kernels, gather_sum(): pl.pallas_call(functools.partial(gather_kernel, slots, int(carried is not...  4.35 us
    all_to_all x3, waiting for transfers between devices, exchange(): return lax.all_to_all(pieces, axis, split_axis=0, concat_axis=0, tiled=True)  4.1 us
  transfers between devices with their start and end apart: 12, of which 8 were waited for; matrix products, arithmetic and copies ran while one was open for 1% of the time, Pallas kernels for 2%

profile of v6, /device:TPU:64, one launch (start us, length us, event | category | flops | bytes accessed | tf_op | source)
XLA Modules:
  0.0 157.0 jit_solution(11334737100829930223)
XLA Ops:
  0.6 0.0 copy-start.5
  0.6 0.9 copy-done.5
  1.6 0.9 copy-done.6
  2.5 0.7 copy-done.8
  3.2 0.5 payloads.1
  3.7 3.4 %collective-permute-start = (bf16[544,256]{1,0:T(8,128)(2,1)S(1)}, bf16[544,256]{1,0:T(8,128)(2,1)S(1)}, u32[]{:S(2)}, u32[]{:S(2)}) collective-permute-start(bf16[544,256]{1,0:T(8,128)(2,1)S(1)} %get-tuple-element.25), channel_id=1, source_target_pairs={{0,128},{128,256},{256,384},{384,0},{1,129},{129,257},{257,385},{3... | collective-permute-start | bytes 835592 | tf_op jit(solution)/shard_map/ppermute | solution.py:351
  7.1 3.7 %collective-permute-start.1 = (bf16[544,256]{1,0:T(8,128)(2,1)S(1)}, bf16[544,256]{1,0:T(8,128)(2,1)S(1)}, u32[]{:S(2)}, u32[]{:S(2)}) collective-permute-start(bf16[544,256]{1,0:T(8,128)(2,1)S(1)} %get-tuple-element.26), channel_id=1, source_target_pairs={{0,384},{128,0},{256,128},{384,256},{1,385},{129,1},{257,129},{385... | collective-permute-start | bytes 835592 | tf_op jit(solution)/shard_map/ppermute | solution.py:351
  10.8 3.7 %collective-permute-start.2 = (bf16[544,256]{1,0:T(8,128)(2,1)S(1)}, bf16[544,256]{1,0:T(8,128)(2,1)S(1)}, u32[]{:S(2)}, u32[]{:S(2)}) collective-permute-start(bf16[544,256]{1,0:T(8,128)(2,1)S(1)} %get-tuple-element.27), channel_id=1, source_target_pairs={{0,256},{128,384},{256,0},{384,128},{1,257},{129,385},{257,1},{385... | collective-permute-start | bytes 835592 | tf_op jit(solution)/shard_map/ppermute | solution.py:351
  14.5 1.0 gather_sum.3.refs_0_
  15.5 0.0 collective-permute-done.refs_1_
  15.5 6.9 %collective-permute-done.1.refs_2_ = bf16[544,256]{1,0:T(8,128)(2,1)S(1)} collective-permute-done((bf16[544,256]{1,0:T(8,128)(2,1)S(1)}, bf16[544,256]{1,0:T(8,128)(2,1)S(1)}, u32[]{:S(2)}, u32[]{:S(2)}) %collective-permute-start.1) | collective-permute-done | bytes 278560 | tf_op jit(solution)/shard_map/ppermute | solution.py:351
  22.4 1.6 gather_sum.4.refs_0_
  24.0 0.0 copy-start.3
  24.0 0.0 copy-start.11
  24.0 0.0 copy-start.1
  24.0 0.0 copy-start.2
  24.0 0.0 collective-permute-done.2.refs_1_
  24.0 1.8 %gather_sum.5 = bf16[1536,256]{1,0:T(8,128)(2,1)} custom-call(f32[1536,256]{1,0:T(8,128)S(1)} %gather_sum.4.refs_0_, bf16[544,256]{1,0:T(8,128)(2,1)S(1)} %collective-permute-done.2.refs_1_), custom_call_target="tpu_custom_call" | custom-call | tf_op jit(solution)/shard_map/gather_sum/pallas_call | solution.py:135
  25.8 10.0 %all-to-all-start = ((bf16[8,192,256]{2,1,0:T(8,128)(2,1)}), bf16[8,192,256]{2,1,0:T(8,128)(2,1)S(1)}, u32[]{:S(2)}, u32[]{:S(2)}) async-start(bf16[8,192,256]{2,1,0:T(8,128)(2,1)} %bitcast.3), calls=%async_computation | async-start | bytes 1572864 | tf_op jit(solution)/shard_map/all_to_all | solution.py:347
  35.8 0.0 copy-done.3
  35.8 3.1 %collective-permute-start.3 = (bf16[192,256]{1,0:T(8,128)(2,1)S(1)}, bf16[192,256]{1,0:T(8,128)(2,1)S(1)}, u32[]{:S(2)}, u32[]{:S(2)}) collective-permute-start(bf16[192,256]{1,0:T(8,128)(2,1)S(1)} %copy-done.3), channel_id=1, source_target_pairs={{0,128},{128,256},{256,384},{384,0},{1,129},{129,257},{257,385},{3... | collective-permute-start | bytes 294920 | tf_op jit(solution)/shard_map/ppermute | solution.py:351
  38.9 5.8 %collective-permute-start.4 = (bf16[192,256]{1,0:T(8,128)(2,1)S(1)}, bf16[192,256]{1,0:T(8,128)(2,1)S(1)}, u32[]{:S(2)}, u32[]{:S(2)}) collective-permute-start(bf16[192,256]{1,0:T(8,128)(2,1)S(1)} %copy-done.3), channel_id=1, source_target_pairs={{0,256},{128,384},{256,0},{384,128},{1,257},{129,385},{257,1},{385... | collective-permute-start | bytes 294920 | tf_op jit(solution)/shard_map/ppermute | solution.py:351
  44.7 1.9 %collective-permute-start.5 = (bf16[192,256]{1,0:T(8,128)(2,1)S(1)}, bf16[192,256]{1,0:T(8,128)(2,1)S(1)}, u32[]{:S(2)}, u32[]{:S(2)}) collective-permute-start(bf16[192,256]{1,0:T(8,128)(2,1)S(1)} %copy-done.3), channel_id=1, source_target_pairs={{0,384},{128,0},{256,128},{384,256},{1,385},{129,1},{257,129},{385... | collective-permute-start | bytes 294920 | tf_op jit(solution)/shard_map/ppermute | solution.py:351
  46.7 0.0 copy-done.11
  46.7 0.1 copy.20.degree_ref
  46.8 0.0 copy-start.10
  46.8 0.0 collective-permute-done.3.refs_1_
  46.8 0.5 collective-permute-done.4.refs_2_
  47.3 3.9 %collective-permute-done.5.refs_3_ = bf16[192,256]{1,0:T(8,128)(2,1)S(1)} collective-permute-done((bf16[192,256]{1,0:T(8,128)(2,1)S(1)}, bf16[192,256]{1,0:T(8,128)(2,1)S(1)}, u32[]{:S(2)}, u32[]{:S(2)}) %collective-permute-start.5) | collective-permute-done | bytes 98336 | tf_op jit(solution)/shard_map/ppermute | solution.py:351
  51.2 3.0 %all-to-all-done.recv_ref = bf16[8,192,256]{2,1,0:T(8,128)(2,1)S(1)} async-done(((bf16[8,192,256]{2,1,0:T(8,128)(2,1)}), bf16[8,192,256]{2,1,0:T(8,128)(2,1)S(1)}, u32[]{:S(2)}, u32[]{:S(2)}) %all-to-all-start) | async-done | bytes 786464 | tf_op jit(solution)/shard_map/all_to_all | solution.py:347
  54.3 0.0 copy-done.1
  54.3 0.0 copy-done.2
  54.3 0.4 first_layer.1
  54.7 0.0 copy-start.9
  54.7 0.0 copy-start
  54.7 0.0 copy-start.4
  54.7 0.0 copy-start.7
  54.8 2.5 %all-gather = bf16[32,96,128]{2,1,0:T(8,128)(2,1)S(1)} all-gather(bf16[16,96,128]{2,1,0:T(8,128)(2,1)S(1)} %get-tuple-element.35), channel_id=2, replica_groups=mesh['x'=4,'z'=8,'y'=8,'c'=2] {'c'}, dimensions={0}, use_global_device_ids=true | all-gather | bytes 1179648 | tf_op jit(solution)/shard_map/all_gather | solution.py:394
  57.3 0.7 pair_sum.1
  58.0 7.1 %all-to-all-start.1 = ((bf16[8,96,128]{2,1,0:T(8,128)(2,1)}), bf16[8,96,128]{2,1,0:T(8,128)(2,1)S(1)}, u32[]{:S(2)}, u32[]{:S(2)}) async-start(bf16[8,96,128]{2,1,0:T(8,128)(2,1)} %pair_sum.1), calls=%async_computation.1 | async-start | bytes 393216 | tf_op jit(solution)/shard_map/all_to_all | solution.py:347
  65.1 5.1 %collective-permute-start.6 = (bf16[192,256]{1,0:T(8,128)(2,1)S(1)}, bf16[192,256]{1,0:T(8,128)(2,1)S(1)}, u32[]{:S(2)}, u32[]{:S(2)}) collective-permute-start(bf16[192,256]{1,0:T(8,128)(2,1)S(1)} %get-tuple-element.34.refs_4_), channel_id=1, source_target_pairs={{0,128},{128,256},{256,384},{384,0},{1,129},{129,257},{257,385},{3... | collective-permute-start | bytes 294920 | tf_op jit(solution)/shard_map/ppermute | solution.py:351
  70.2 2.5 %collective-permute-start.7 = (bf16[192,256]{1,0:T(8,128)(2,1)S(1)}, bf16[192,256]{1,0:T(8,128)(2,1)S(1)}, u32[]{:S(2)}, u32[]{:S(2)}) collective-permute-start(bf16[192,256]{1,0:T(8,128)(2,1)S(1)} %get-tuple-element.34.refs_4_), channel_id=1, source_target_pairs={{0,384},{128,0},{256,128},{384,256},{1,385},{129,1},{257,129},{385... | collective-permute-start | bytes 294920 | tf_op jit(solution)/shard_map/ppermute | solution.py:351
  72.7 0.0 copy-done.10
  72.7 0.8 collective-permute-done.6.refs_5_
  73.6 3.1 %collective-permute-done.7.refs_7_ = bf16[192,256]{1,0:T(8,128)(2,1)S(1)} collective-permute-done((bf16[192,256]{1,0:T(8,128)(2,1)S(1)}, bf16[192,256]{1,0:T(8,128)(2,1)S(1)}, u32[]{:S(2)}, u32[]{:S(2)}) %collective-permute-start.7) | collective-permute-done | bytes 98336 | tf_op jit(solution)/shard_map/ppermute | solution.py:351
  76.7 0.0 all-to-all-done.1.recv_ref
  76.7 0.7 sum_and_spread.2
  77.4 7.2 %all-to-all-start.2 = ((bf16[8,96,128]{2,1,0:T(8,128)(2,1)}), bf16[8,96,128]{2,1,0:T(8,128)(2,1)}, u32[]{:S(2)}, u32[]{:S(2)}) async-start(bf16[8,96,128]{2,1,0:T(8,128)(2,1)} %sum_and_spread.2), calls=%async_computation.2 | async-start | bytes 393216 | tf_op jit(solution)/shard_map/all_to_all | solution.py:347
  84.6 0.0 copy-done.9
  84.6 0.8 convert_reduce_fusion
  85.4 4.0 %collective-permute-start.8 = (bf16[192,256]{1,0:T(8,128)(2,1)S(1)}, bf16[192,256]{1,0:T(8,128)(2,1)S(1)}, u32[]{:S(2)}, u32[]{:S(2)}) collective-permute-start(bf16[192,256]{1,0:T(8,128)(2,1)S(1)} %get-tuple-element.34.refs_4_), channel_id=1, source_target_pairs={{0,256},{128,384},{256,0},{384,128},{1,257},{129,385},{257,1},{385... | collective-permute-start | bytes 294920 | tf_op jit(solution)/shard_map/ppermute | solution.py:351
  89.4 4.0 %collective-permute-done.8.refs_6_ = bf16[192,256]{1,0:T(8,128)(2,1)S(1)} collective-permute-done((bf16[192,256]{1,0:T(8,128)(2,1)S(1)}, bf16[192,256]{1,0:T(8,128)(2,1)S(1)}, u32[]{:S(2)}, u32[]{:S(2)}) %collective-permute-start.8) | collective-permute-done | bytes 98336 | tf_op jit(solution)/shard_map/ppermute | solution.py:351
  93.4 1.1 all-to-all-done.2
  94.5 2.3 %all_gather.11.pre_ref = bf16[16,96,128]{2,1,0:T(8,128)(2,1)S(1)} all-gather(bf16[8,96,128]{2,1,0:T(8,128)(2,1)} %all-to-all-done.2), channel_id=1, replica_groups=mesh['x'=4,'z'=8,'y'=8,'c'=2] {'c'}, dimensions={0}, use_global_device_ids=true | all-gather | bytes 589824 | tf_op jit(solution)/shard_map/all_gather | solution.py:398
  96.8 0.0 copy-done
  96.8 0.0 copy-done.4
  96.8 0.0 copy-done.7
  96.8 2.1 %second_layer.1 = (bf16[172,192]{1,0:T(8,128)(2,1)}, bf16[4,192,256]{2,1,0:T(8,128)(2,1)S(1)}) custom-call(bf16[16,96,128]{2,1,0:T(8,128)(2,1)S(1)} %all_gather.11.pre_ref, bf16[192,192]{1,0:T(8,128)(2,1)S(1)} %add_convert_fusion.adj_ref, bf16[1024,1024]{1,0:T(8,128)(2,1)S(1)} %copy-done, bf16[172,1024]{1,0:T(8,128)(2,1)S(1)} %bitcast.16, ...), custom_call_target="tpu_custom_call" | custom-call | tf_op jit(solution)/shard_map/second_layer/pallas_call | solution.py:252
  98.9 11.5 %all_to_all.30.refs_8_ = bf16[4,192,256]{2,1,0:T(8,128)(2,1)S(1)} all-to-all(bf16[4,192,256]{2,1,0:T(8,128)(2,1)S(1)} %get-tuple-element.41), channel_id=1, replica_groups=mesh['x'=4,'z'=8,'y'=8,'c'=2] {'x'}, dimensions={0} | all-to-all | bytes 786432 | tf_op jit(solution)/shard_map/all_to_all | solution.py:347
  110.4 0.5 gradient_part.1
  110.9 13.5 %all_to_all.31.recv_ref = bf16[8,64,256]{2,1,0:T(8,128)(2,1)S(1)} all-to-all(bf16[8,64,256]{2,1,0:T(8,128)(2,1)S(1)} %bitcast.15), channel_id=1, replica_groups=mesh['x'=4,'z'=8,'y'=8,'c'=2] {'z'}, dimensions={0} | all-to-all | bytes 524288 | tf_op jit(solution)/shard_map/all_to_all | solution.py:347
  124.4 0.1 sum_and_spread.3
  124.5 31.5 %all_to_all.32 = bf16[32,64,256]{2,1,0:T(8,128)(2,1)S(1)} all-to-all(bf16[32,64,256]{2,1,0:T(8,128)(2,1)S(1)} %sum_and_spread.3), channel_id=1, replica_groups=mesh['x'=4,'z'=8,'y'=8,'c'=2] {'x','z'}, dimensions={0} | all-to-all | bytes 2097152 | tf_op jit(solution)/shard_map/all_to_all | solution.py:347
  156.0 1.0 assemble.1
  (5 shorter events, 0.0 us)
Async XLA Ops:
  0.6 1.0 copy-start.5
  1.6 0.9 copy-start.6
  2.5 0.7 copy-start.8
  3.7 11.8 %collective-permute-start = (bf16[544,256]{1,0:T(8,128)(2,1)S(1)}, bf16[544,256]{1,0:T(8,128)(2,1)S(1)}, u32[]{:S(2)}, u32[]{:S(2)}) collective-permute-start(bf16[544,256]{1,0:T(8,128)(2,1)S(1)} %get-tuple-element.25), channel_id=1, source_target_pairs={{0,128},{128,256},{256,384},{384,0},{1,129},{129,257},{257,385},{3... | collective-permute-start | bytes 835592 | tf_op jit(solution)/shard_map/ppermute | solution.py:351
  7.1 15.3 %collective-permute-start.1 = (bf16[544,256]{1,0:T(8,128)(2,1)S(1)}, bf16[544,256]{1,0:T(8,128)(2,1)S(1)}, u32[]{:S(2)}, u32[]{:S(2)}) collective-permute-start(bf16[544,256]{1,0:T(8,128)(2,1)S(1)} %get-tuple-element.26), channel_id=1, source_target_pairs={{0,384},{128,0},{256,128},{384,256},{1,385},{129,1},{257,129},{385... | collective-permute-start | bytes 835592 | tf_op jit(solution)/shard_map/ppermute | solution.py:351
  10.8 13.2 %collective-permute-start.2 = (bf16[544,256]{1,0:T(8,128)(2,1)S(1)}, bf16[544,256]{1,0:T(8,128)(2,1)S(1)}, u32[]{:S(2)}, u32[]{:S(2)}) collective-permute-start(bf16[544,256]{1,0:T(8,128)(2,1)S(1)} %get-tuple-element.27), channel_id=1, source_target_pairs={{0,256},{128,384},{256,0},{384,128},{1,257},{129,385},{257,1},{385... | collective-permute-start | bytes 835592 | tf_op jit(solution)/shard_map/ppermute | solution.py:351
  24.0 11.8 %copy-start.3 = (bf16[192,256]{1,0:T(8,128)(2,1)S(1)}, bf16[192,256]{1,0:T(8,128)(2,1)}, u32[]{:S(2)}) copy-start(bf16[192,256]{1,0:T(8,128)(2,1)} %refs_0_.1) | copy-start | bytes 294916
  24.0 22.7 %copy-start.11 = (s32[192]{0:T(256)S(1)}, s32[192]{0:T(256)}, u32[]{:S(2)}) copy-start(s32[192]{0:T(256)} %param.16) | copy-start | bytes 2308
  24.0 30.3 %copy-start.1 = (bf16[256,1024]{1,0:T(8,128)(2,1)S(1)}, bf16[256,1024]{1,0:T(8,128)(2,1)}, u32[]{:S(2)}) copy-start(bf16[256,1024]{1,0:T(8,128)(2,1)} %self_ref.1) | copy-start | bytes 1572868
  24.0 30.3 %copy-start.2 = (bf16[256,1024]{1,0:T(8,128)(2,1)S(1)}, bf16[256,1024]{1,0:T(8,128)(2,1)}, u32[]{:S(2)}) copy-start(bf16[256,1024]{1,0:T(8,128)(2,1)} %neigh_ref.1) | copy-start | bytes 1572868
  25.8 28.4 %all-to-all-start = ((bf16[8,192,256]{2,1,0:T(8,128)(2,1)}), bf16[8,192,256]{2,1,0:T(8,128)(2,1)S(1)}, u32[]{:S(2)}, u32[]{:S(2)}) async-start(bf16[8,192,256]{2,1,0:T(8,128)(2,1)} %bitcast.3), calls=%async_computation | async-start | bytes 1572864 | tf_op jit(solution)/shard_map/all_to_all | solution.py:347
  35.8 11.0 %collective-permute-start.3 = (bf16[192,256]{1,0:T(8,128)(2,1)S(1)}, bf16[192,256]{1,0:T(8,128)(2,1)S(1)}, u32[]{:S(2)}, u32[]{:S(2)}) collective-permute-start(bf16[192,256]{1,0:T(8,128)(2,1)S(1)} %copy-done.3), channel_id=1, source_target_pairs={{0,128},{128,256},{256,384},{384,0},{1,129},{129,257},{257,385},{3... | collective-permute-start | bytes 294920 | tf_op jit(solution)/shard_map/ppermute | solution.py:351
  38.9 8.4 %collective-permute-start.4 = (bf16[192,256]{1,0:T(8,128)(2,1)S(1)}, bf16[192,256]{1,0:T(8,128)(2,1)S(1)}, u32[]{:S(2)}, u32[]{:S(2)}) collective-permute-start(bf16[192,256]{1,0:T(8,128)(2,1)S(1)} %copy-done.3), channel_id=1, source_target_pairs={{0,256},{128,384},{256,0},{384,128},{1,257},{129,385},{257,1},{385... | collective-permute-start | bytes 294920 | tf_op jit(solution)/shard_map/ppermute | solution.py:351
  44.7 6.5 %collective-permute-start.5 = (bf16[192,256]{1,0:T(8,128)(2,1)S(1)}, bf16[192,256]{1,0:T(8,128)(2,1)S(1)}, u32[]{:S(2)}, u32[]{:S(2)}) collective-permute-start(bf16[192,256]{1,0:T(8,128)(2,1)S(1)} %copy-done.3), channel_id=1, source_target_pairs={{0,384},{128,0},{256,128},{384,256},{1,385},{129,1},{257,129},{385... | collective-permute-start | bytes 294920 | tf_op jit(solution)/shard_map/ppermute | solution.py:351
  46.8 25.9 %copy-start.10 = (s32[192]{0:T(256)S(1)}, s32[192]{0:T(256)}, u32[]{:S(2)}) copy-start(s32[192]{0:T(256)} %param.18) | copy-start | bytes 2308
  54.7 29.9 %copy-start.9 = (s32[192,10]{0,1:T(8,128)S(1)}, s32[192,10]{0,1:T(8,128)}, u32[]{:S(2)}) copy-start(s32[192,10]{0,1:T(8,128)} %param.17) | copy-start | bytes 23044
  54.7 42.1 %copy-start = (bf16[1024,1024]{1,0:T(8,128)(2,1)S(1)}, bf16[1024,1024]{1,0:T(8,128)(2,1)}, u32[]{:S(2)}) copy-start(bf16[1024,1024]{1,0:T(8,128)(2,1)} %two_ref.1) | copy-start | bytes 6291460
  54.7 42.1 %copy-start.4 = (bf16[1024,172]{0,1:T(8,128)(2,1)S(1)}, bf16[1024,172]{0,1:T(8,128)(2,1)}, u32[]{:S(2)}) copy-start(bf16[1024,172]{0,1:T(8,128)(2,1)} %param.22) | copy-start | bytes 1056772
  54.7 42.1 %copy-start.7 = (bf16[192,172]{0,1:T(8,128)(2,1)S(1)}, bf16[192,172]{0,1:T(8,128)(2,1)}, u32[]{:S(2)}) copy-start(bf16[192,172]{0,1:T(8,128)(2,1)} %param.23) | copy-start | bytes 198148
  58.0 18.7 %all-to-all-start.1 = ((bf16[8,96,128]{2,1,0:T(8,128)(2,1)}), bf16[8,96,128]{2,1,0:T(8,128)(2,1)S(1)}, u32[]{:S(2)}, u32[]{:S(2)}) async-start(bf16[8,96,128]{2,1,0:T(8,128)(2,1)} %pair_sum.1), calls=%async_computation.1 | async-start | bytes 393216 | tf_op jit(solution)/shard_map/all_to_all | solution.py:347
  65.1 8.5 %collective-permute-start.6 = (bf16[192,256]{1,0:T(8,128)(2,1)S(1)}, bf16[192,256]{1,0:T(8,128)(2,1)S(1)}, u32[]{:S(2)}, u32[]{:S(2)}) collective-permute-start(bf16[192,256]{1,0:T(8,128)(2,1)S(1)} %get-tuple-element.34.refs_4_), channel_id=1, source_target_pairs={{0,128},{128,256},{256,384},{384,0},{1,129},{129,257},{257,385},{3... | collective-permute-start | bytes 294920 | tf_op jit(solution)/shard_map/ppermute | solution.py:351
  70.2 6.5 %collective-permute-start.7 = (bf16[192,256]{1,0:T(8,128)(2,1)S(1)}, bf16[192,256]{1,0:T(8,128)(2,1)S(1)}, u32[]{:S(2)}, u32[]{:S(2)}) collective-permute-start(bf16[192,256]{1,0:T(8,128)(2,1)S(1)} %get-tuple-element.34.refs_4_), channel_id=1, source_target_pairs={{0,384},{128,0},{256,128},{384,256},{1,385},{129,1},{257,129},{385... | collective-permute-start | bytes 294920 | tf_op jit(solution)/shard_map/ppermute | solution.py:351
  77.4 17.1 %all-to-all-start.2 = ((bf16[8,96,128]{2,1,0:T(8,128)(2,1)}), bf16[8,96,128]{2,1,0:T(8,128)(2,1)}, u32[]{:S(2)}, u32[]{:S(2)}) async-start(bf16[8,96,128]{2,1,0:T(8,128)(2,1)} %sum_and_spread.2), calls=%async_computation.2 | async-start | bytes 393216 | tf_op jit(solution)/shard_map/all_to_all | solution.py:347
  85.4 8.0 %collective-permute-start.8 = (bf16[192,256]{1,0:T(8,128)(2,1)S(1)}, bf16[192,256]{1,0:T(8,128)(2,1)S(1)}, u32[]{:S(2)}, u32[]{:S(2)}) collective-permute-start(bf16[192,256]{1,0:T(8,128)(2,1)S(1)} %get-tuple-element.34.refs_4_), channel_id=1, source_target_pairs={{0,256},{128,384},{256,0},{384,128},{1,257},{129,385},{257,1},{385... | collective-permute-start | bytes 294920 | tf_op jit(solution)/shard_map/ppermute | solution.py:351

commit v7 on v6

--- a/solution.py
+++ b/solution.py
@@ -39,6 +39,12 @@
     first.start()
     second.start()
     third.start()
+    third.wait()
+    copies = []
+    for shift in range(XS):
+        target = outs[shift].at[pl.ds(0, nodes), :]
+        copies.append(pltpu.make_async_copy(table_ref, target, sems.at[2 + shift]))
+        copies[shift].start()
     slots, total = index_ref.shape
     blocks = total // XS // ROW_BLOCK
     extra = coded.shape[1] - slots * blocks
@@ -54,12 +60,6 @@
             for c in range(blocks)
         ] + [jnp.full((extra, ROW_BLOCK), DEAD, jnp.float32)]
         coded[x] = jnp.concatenate(pieces, axis=0).astype(jnp.bfloat16)
-    third.wait()
-    copies = []
-    for shift in range(XS):
-        target = outs[shift].at[pl.ds(0, nodes), :]
-        copies.append(pltpu.make_async_copy(table_ref, target, sems.at[2 + shift]))
-        copies[shift].start()
     for shift in range(XS):
         source = coded.at[lax.rem(place_ref[0] + shift, XS)]
         target = outs[shift].at[pl.ds(nodes, coded.shape[1]), :]
@@ -87,7 +87,7 @@
             pltpu.VMEM((XS, extra, ROW_BLOCK), jnp.bfloat16),
             pltpu.SemaphoreType.DMA((3 + 2 * XS,)),
         ],
-        compiler_params=params(16),
+        compiler_params=params(60),
         name="payloads",
     )(place, index, count, table)
 
@@ -392,10 +392,10 @@
     mean = [shift_x(mean_rows, s) for s in range(1, XS)]
     core = lax.axis_index("c").reshape(1).astype(jnp.int32)
     paired = pair_sum(core, lax.all_gather(pieces, "c", axis=0, tiled=False))
-    paired, mean[0], mean[2] = lax.optimization_barrier((exchange(paired, "y"), mean[0], mean[2]))
+    paired, mean[0] = lax.optimization_barrier((exchange(paired, "y"), mean[0]))
     pre_copies = spread(paired, paired.shape[0])
-    pre, mean[1] = lax.optimization_barrier((exchange(pre_copies, "y"), mean[1]))
-    pre = lax.all_gather(pre, "c", axis=0, tiled=True)
+    pre = lax.all_gather(exchange(pre_copies, "y"), "c", axis=0, tiled=True)
+    pre, mean[1], mean[2] = lax.optimization_barrier((pre, mean[1], mean[2]))
 
     slot_ids = jnp.arange(local_index.shape[1], dtype=jnp.int32)
     live_slots = slot_ids[None, :] < local_count[:, None]

time: 158 us -> 154 us (0.975)
  waiting for transfers between devices: 23.4 us -> 19.4 us
  local copies, waits for them, and re-layouts: 2.75 us -> 1.12 us
  Pallas kernels: 10.4 us -> 12 us
    ppermute x9, waiting for transfers between devices: 19.3 us -> 14 us  [shift_x(): return lax.ppermute(array, 'x', [(i, (i + steps) % XS) for i in range(XS)])]
    all_to_all x3, starting transfers between devices: 24.3 us -> 21.8 us  [exchange(): return lax.all_to_all(pieces, axis, split_axis=0, concat_axis=0, tiled=True)]
    ppermute x9, starting transfers between devices: 33.2 us -> 35.6 us  [shift_x(): return lax.ppermute(array, 'x', [(i, (i + steps) % XS) for i in range(XS)])]
    unnamed x24 -> x20, local copies, waits for them, and re-layouts: 2.63 us -> 1.01 us
    pallas_call x1, Pallas kernels: 0.48 us -> 2.08 us  [make_payloads(): pl.pallas_call(payload_kernel, in_specs=[pl.BlockSpec(memory_space=pltpu....]
  transfers between devices with their start and end apart: 12 -> 12, of which waited for: 8 -> 6; matrix products, arithmetic and copies ran while one was open for 1% -> 1% of each run, Pallas kernels for 2% -> 2%
where the time goes in v7:
time: 154 us; the launch traced here: 153 us
  blocking collectives  61.4 us (40%)
  starting transfers between devices  57.4 us (37%)
  waiting for transfers between devices  19.4 us (13%)
  Pallas kernels  12 us (8%)
    all_to_all x3, blocking collectives, exchange(): return lax.all_to_all(pieces, axis, split_axis=0, concat_axis=0, tiled=True)  56.6 us
    ppermute x9, starting transfers between devices, shift_x(): return lax.ppermute(array, 'x', [(i, (i + steps) % XS) for i in range(XS)])  35.6 us
    all_to_all x3, starting transfers between devices, exchange(): return lax.all_to_all(pieces, axis, split_axis=0, concat_axis=0, tiled=True)  21.8 us
    ppermute x9, waiting for transfers between devices, shift_x(): return lax.ppermute(array, 'x', [(i, (i + steps) % XS) for i in range(XS)])  14 us
    all_to_all x3, waiting for transfers between devices, exchange(): return lax.all_to_all(pieces, axis, split_axis=0, concat_axis=0, tiled=True)  5.33 us
    pallas_call x3, Pallas kernels, gather_sum(): pl.pallas_call(functools.partial(gather_kernel, slots, int(carried is not...  4.32 us
  transfers between devices with their start and end apart: 12, of which 6 were waited for; matrix products, arithmetic and copies ran while one was open for 1% of the time, Pallas kernels for 2%

profile of v7, /device:TPU:64, one launch (start us, length us, event | category | flops | bytes accessed | tf_op | source)
XLA Modules:
  0.0 153.0 jit_solution(5399776696433259293)
XLA Ops:
  0.6 2.1 %payloads.1 = (bf16[544,256]{1,0:T(8,128)(2,1)}, bf16[544,256]{1,0:T(8,128)(2,1)}, bf16[544,256]{1,0:T(8,128)(2,1)}, bf16[544,256]{1,0:T(8,128)(2,1)}) custom-call(s32[1]{0:T(128)} %bitcast.place_ref, s32[4,6144]{1,0:T(4,128)} %bitcast.18, s32[1,6144]{1,0:T(1,128)} %count_hbm.1, bf16[512,256]{1,0:T(8,128)(2,1)} %table_hbm.1), custom_call_target="tpu_custom_call" | custom-call | tf_op jit(solution)/shard_map/payloads/pallas_call | solution.py:78
  2.7 3.4 %collective-permute-start = (bf16[544,256]{1,0:T(8,128)(2,1)}, bf16[544,256]{1,0:T(8,128)(2,1)S(1)}, u32[]{:S(2)}, u32[]{:S(2)}) collective-permute-start(bf16[544,256]{1,0:T(8,128)(2,1)} %get-tuple-element.25), channel_id=1, source_target_pairs={{0,128},{128,256},{256,384},{384,0},{1,129},{129,257},{257,385},{3... | collective-permute-start | bytes 835592 | tf_op jit(solution)/shard_map/ppermute | solution.py:351
  6.1 3.7 %collective-permute-start.1 = (bf16[544,256]{1,0:T(8,128)(2,1)}, bf16[544,256]{1,0:T(8,128)(2,1)S(1)}, u32[]{:S(2)}, u32[]{:S(2)}) collective-permute-start(bf16[544,256]{1,0:T(8,128)(2,1)} %get-tuple-element.26), channel_id=1, source_target_pairs={{0,384},{128,0},{256,128},{384,256},{1,385},{129,1},{257,129},{385... | collective-permute-start | bytes 835592 | tf_op jit(solution)/shard_map/ppermute | solution.py:351
  9.8 3.7 %collective-permute-start.2 = (bf16[544,256]{1,0:T(8,128)(2,1)}, bf16[544,256]{1,0:T(8,128)(2,1)S(1)}, u32[]{:S(2)}, u32[]{:S(2)}) collective-permute-start(bf16[544,256]{1,0:T(8,128)(2,1)} %get-tuple-element.27), channel_id=1, source_target_pairs={{0,256},{128,384},{256,0},{384,128},{1,257},{129,385},{257,1},{385... | collective-permute-start | bytes 835592 | tf_op jit(solution)/shard_map/ppermute | solution.py:351
  13.5 0.0 copy-start.5
  13.5 0.9 copy-done.5
  14.5 1.0 gather_sum.3.refs_0_
  15.5 0.0 collective-permute-done.refs_1_
  15.5 6.2 %collective-permute-done.1.refs_2_ = bf16[544,256]{1,0:T(8,128)(2,1)S(1)} collective-permute-done((bf16[544,256]{1,0:T(8,128)(2,1)}, bf16[544,256]{1,0:T(8,128)(2,1)S(1)}, u32[]{:S(2)}, u32[]{:S(2)}) %collective-permute-start.1) | collective-permute-done | bytes 278560 | tf_op jit(solution)/shard_map/ppermute | solution.py:351
  21.7 1.6 %gather_sum.4.refs_0_ = f32[1536,256]{1,0:T(8,128)S(1)} custom-call(f32[1536,256]{1,0:T(8,128)S(1)} %gather_sum.3.refs_0_, bf16[544,256]{1,0:T(8,128)(2,1)S(1)} %collective-permute-done.refs_1_, bf16[544,256]{1,0:T(8,128)(2,1)S(1)} %collective-permute-done.1.refs_2_), custom_call_target="tpu_custom_call" | custom-call | tf_op jit(solution)/shard_map/gather_sum/pallas_call | solution.py:135
  23.3 0.0 copy-start.3
  23.3 0.0 copy-start.9
  23.3 0.0 copy-start.1
  23.3 0.0 copy-start.2
  23.3 0.0 collective-permute-done.2.refs_1_
  23.3 1.8 %gather_sum.5 = bf16[1536,256]{1,0:T(8,128)(2,1)} custom-call(f32[1536,256]{1,0:T(8,128)S(1)} %gather_sum.4.refs_0_, bf16[544,256]{1,0:T(8,128)(2,1)S(1)} %collective-permute-done.2.refs_1_), custom_call_target="tpu_custom_call" | custom-call | tf_op jit(solution)/shard_map/gather_sum/pallas_call | solution.py:135
  25.1 10.0 %all-to-all-start = ((bf16[8,192,256]{2,1,0:T(8,128)(2,1)}), bf16[8,192,256]{2,1,0:T(8,128)(2,1)S(1)}, u32[]{:S(2)}, u32[]{:S(2)}) async-start(bf16[8,192,256]{2,1,0:T(8,128)(2,1)} %bitcast.3), calls=%async_computation | async-start | bytes 1572864 | tf_op jit(solution)/shard_map/all_to_all | solution.py:347
  35.1 0.0 copy-done.3
  35.1 3.0 %collective-permute-start.3 = (bf16[192,256]{1,0:T(8,128)(2,1)S(1)}, bf16[192,256]{1,0:T(8,128)(2,1)S(1)}, u32[]{:S(2)}, u32[]{:S(2)}) collective-permute-start(bf16[192,256]{1,0:T(8,128)(2,1)S(1)} %copy-done.3), channel_id=1, source_target_pairs={{0,128},{128,256},{256,384},{384,0},{1,129},{129,257},{257,385},{3... | collective-permute-start | bytes 294920 | tf_op jit(solution)/shard_map/ppermute | solution.py:351
  38.1 5.8 %collective-permute-start.4 = (bf16[192,256]{1,0:T(8,128)(2,1)S(1)}, bf16[192,256]{1,0:T(8,128)(2,1)S(1)}, u32[]{:S(2)}, u32[]{:S(2)}) collective-permute-start(bf16[192,256]{1,0:T(8,128)(2,1)S(1)} %copy-done.3), channel_id=1, source_target_pairs={{0,256},{128,384},{256,0},{384,128},{1,257},{129,385},{257,1},{385... | collective-permute-start | bytes 294920 | tf_op jit(solution)/shard_map/ppermute | solution.py:351
  44.0 1.9 %collective-permute-start.5 = (bf16[192,256]{1,0:T(8,128)(2,1)S(1)}, bf16[192,256]{1,0:T(8,128)(2,1)S(1)}, u32[]{:S(2)}, u32[]{:S(2)}) collective-permute-start(bf16[192,256]{1,0:T(8,128)(2,1)S(1)} %copy-done.3), channel_id=1, source_target_pairs={{0,384},{128,0},{256,128},{384,256},{1,385},{129,1},{257,129},{385... | collective-permute-start | bytes 294920 | tf_op jit(solution)/shard_map/ppermute | solution.py:351
  45.9 0.0 copy-done.9
  45.9 0.1 copy.20.degree_ref
  46.0 0.0 copy-start.8
  46.0 0.0 collective-permute-done.3.refs_1_
  46.0 0.5 collective-permute-done.4.refs_2_
  46.5 3.9 %collective-permute-done.5.refs_3_ = bf16[192,256]{1,0:T(8,128)(2,1)S(1)} collective-permute-done((bf16[192,256]{1,0:T(8,128)(2,1)S(1)}, bf16[192,256]{1,0:T(8,128)(2,1)S(1)}, u32[]{:S(2)}, u32[]{:S(2)}) %collective-permute-start.5) | collective-permute-done | bytes 98336 | tf_op jit(solution)/shard_map/ppermute | solution.py:351
  50.5 3.0 %all-to-all-done.recv_ref = bf16[8,192,256]{2,1,0:T(8,128)(2,1)S(1)} async-done(((bf16[8,192,256]{2,1,0:T(8,128)(2,1)}), bf16[8,192,256]{2,1,0:T(8,128)(2,1)S(1)}, u32[]{:S(2)}, u32[]{:S(2)}) %all-to-all-start) | async-done | bytes 786464 | tf_op jit(solution)/shard_map/all_to_all | solution.py:347
  53.5 0.0 copy-done.1
  53.5 0.0 copy-done.2
  53.5 0.4 first_layer.1
  53.9 0.0 copy-start.7
  53.9 0.0 copy-start
  54.0 0.0 copy-start.4
  54.0 0.0 copy-start.6
  54.0 2.5 %all-gather = bf16[32,96,128]{2,1,0:T(8,128)(2,1)S(1)} all-gather(bf16[16,96,128]{2,1,0:T(8,128)(2,1)S(1)} %get-tuple-element.35), channel_id=2, replica_groups=mesh['x'=4,'z'=8,'y'=8,'c'=2] {'c'}, dimensions={0}, use_global_device_ids=true | all-gather | bytes 1179648 | tf_op jit(solution)/shard_map/all_gather | solution.py:394
  56.5 0.7 pair_sum.1
  57.2 7.1 %all-to-all-start.1 = ((bf16[8,96,128]{2,1,0:T(8,128)(2,1)}), bf16[8,96,128]{2,1,0:T(8,128)(2,1)S(1)}, u32[]{:S(2)}, u32[]{:S(2)}) async-start(bf16[8,96,128]{2,1,0:T(8,128)(2,1)} %pair_sum.1), calls=%async_computation.1 | async-start | bytes 393216 | tf_op jit(solution)/shard_map/all_to_all | solution.py:347
  64.3 5.1 %collective-permute-start.6 = (bf16[192,256]{1,0:T(8,128)(2,1)S(1)}, bf16[192,256]{1,0:T(8,128)(2,1)S(1)}, u32[]{:S(2)}, u32[]{:S(2)}) collective-permute-start(bf16[192,256]{1,0:T(8,128)(2,1)S(1)} %get-tuple-element.34.refs_4_), channel_id=1, source_target_pairs={{0,128},{128,256},{256,384},{384,0},{1,129},{129,257},{257,385},{3... | collective-permute-start | bytes 294920 | tf_op jit(solution)/shard_map/ppermute | solution.py:351
  69.4 0.0 copy-done.8
  69.4 3.4 %collective-permute-done.6.refs_5_ = bf16[192,256]{1,0:T(8,128)(2,1)S(1)} collective-permute-done((bf16[192,256]{1,0:T(8,128)(2,1)S(1)}, bf16[192,256]{1,0:T(8,128)(2,1)S(1)}, u32[]{:S(2)}, u32[]{:S(2)}) %collective-permute-start.6) | collective-permute-done | bytes 98336 | tf_op jit(solution)/shard_map/ppermute | solution.py:351
  72.8 2.3 %all-to-all-done.1.recv_ref = bf16[8,96,128]{2,1,0:T(8,128)(2,1)S(1)} async-done(((bf16[8,96,128]{2,1,0:T(8,128)(2,1)}), bf16[8,96,128]{2,1,0:T(8,128)(2,1)S(1)}, u32[]{:S(2)}, u32[]{:S(2)}) %all-to-all-start.1) | async-done | bytes 196640 | tf_op jit(solution)/shard_map/all_to_all | solution.py:347
  75.1 0.7 sum_and_spread.2
  75.8 4.7 %all-to-all-start.2 = ((bf16[8,96,128]{2,1,0:T(8,128)(2,1)}), bf16[8,96,128]{2,1,0:T(8,128)(2,1)}, u32[]{:S(2)}, u32[]{:S(2)}) async-start(bf16[8,96,128]{2,1,0:T(8,128)(2,1)} %sum_and_spread.2), calls=%async_computation.2 | async-start | bytes 393216 | tf_op jit(solution)/shard_map/all_to_all | solution.py:347
  80.5 0.0 copy-done.7
  80.5 0.8 convert_reduce_fusion
  81.3 3.4 %collective-permute-start.7 = (bf16[192,256]{1,0:T(8,128)(2,1)S(1)}, bf16[192,256]{1,0:T(8,128)(2,1)S(1)}, u32[]{:S(2)}, u32[]{:S(2)}) collective-permute-start(bf16[192,256]{1,0:T(8,128)(2,1)S(1)} %get-tuple-element.34.refs_4_), channel_id=1, source_target_pairs={{0,256},{128,384},{256,0},{384,128},{1,257},{129,385},{257,1},{385... | collective-permute-start | bytes 294920 | tf_op jit(solution)/shard_map/ppermute | solution.py:351
  84.7 5.6 %collective-permute-start.8 = (bf16[192,256]{1,0:T(8,128)(2,1)S(1)}, bf16[192,256]{1,0:T(8,128)(2,1)S(1)}, u32[]{:S(2)}, u32[]{:S(2)}) collective-permute-start(bf16[192,256]{1,0:T(8,128)(2,1)S(1)} %get-tuple-element.34.refs_4_), channel_id=1, source_target_pairs={{0,384},{128,0},{256,128},{384,256},{1,385},{129,1},{257,129},{385... | collective-permute-start | bytes 294920 | tf_op jit(solution)/shard_map/ppermute | solution.py:351
  90.3 0.0 all-to-all-done.2
  90.4 2.3 %all_gather.11.pre_ref = bf16[16,96,128]{2,1,0:T(8,128)(2,1)S(1)} all-gather(bf16[8,96,128]{2,1,0:T(8,128)(2,1)} %all-to-all-done.2), channel_id=1, replica_groups=mesh['x'=4,'z'=8,'y'=8,'c'=2] {'c'}, dimensions={0}, use_global_device_ids=true | all-gather | bytes 589824 | tf_op jit(solution)/shard_map/all_gather | solution.py:397
  92.7 0.0 collective-permute-done.7.refs_6_
  92.7 0.0 collective-permute-done.8.refs_7_
  92.7 0.0 copy-done
  92.7 0.0 copy-done.4
  92.7 0.0 copy-done.6
  92.7 2.1 %second_layer.1 = (bf16[172,192]{1,0:T(8,128)(2,1)}, bf16[4,192,256]{2,1,0:T(8,128)(2,1)S(1)}) custom-call(bf16[16,96,128]{2,1,0:T(8,128)(2,1)S(1)} %all_gather.11.pre_ref, bf16[192,192]{1,0:T(8,128)(2,1)S(1)} %add_convert_fusion.adj_ref, bf16[1024,1024]{1,0:T(8,128)(2,1)S(1)} %copy-done, bf16[172,1024]{1,0:T(8,128)(2,1)S(1)} %bitcast.16, ...), custom_call_target="tpu_custom_call" | custom-call | tf_op jit(solution)/shard_map/second_layer/pallas_call | solution.py:252
  94.8 12.4 %all_to_all.30.refs_8_ = bf16[4,192,256]{2,1,0:T(8,128)(2,1)S(1)} all-to-all(bf16[4,192,256]{2,1,0:T(8,128)(2,1)S(1)} %get-tuple-element.41), channel_id=1, replica_groups=mesh['x'=4,'z'=8,'y'=8,'c'=2] {'x'}, dimensions={0} | all-to-all | bytes 786432 | tf_op jit(solution)/shard_map/all_to_all | solution.py:347
  107.2 0.5 gradient_part.1
  107.7 13.3 %all_to_all.31.recv_ref = bf16[8,64,256]{2,1,0:T(8,128)(2,1)S(1)} all-to-all(bf16[8,64,256]{2,1,0:T(8,128)(2,1)S(1)} %bitcast.15), channel_id=1, replica_groups=mesh['x'=4,'z'=8,'y'=8,'c'=2] {'z'}, dimensions={0} | all-to-all | bytes 524288 | tf_op jit(solution)/shard_map/all_to_all | solution.py:347
  121.0 0.1 sum_and_spread.3
  121.1 30.9 %all_to_all.32 = bf16[32,64,256]{2,1,0:T(8,128)(2,1)S(1)} all-to-all(bf16[32,64,256]{2,1,0:T(8,128)(2,1)S(1)} %sum_and_spread.3), channel_id=1, replica_groups=mesh['x'=4,'z'=8,'y'=8,'c'=2] {'x','z'}, dimensions={0} | all-to-all | bytes 2097152 | tf_op jit(solution)/shard_map/all_to_all | solution.py:347
  152.0 1.0 assemble.1
  (3 shorter events, 0.0 us)
Async XLA Ops:
  2.7 12.8 %collective-permute-start = (bf16[544,256]{1,0:T(8,128)(2,1)}, bf16[544,256]{1,0:T(8,128)(2,1)S(1)}, u32[]{:S(2)}, u32[]{:S(2)}) collective-permute-start(bf16[544,256]{1,0:T(8,128)(2,1)} %get-tuple-element.25), channel_id=1, source_target_pairs={{0,128},{128,256},{256,384},{384,0},{1,129},{129,257},{257,385},{3... | collective-permute-start | bytes 835592 | tf_op jit(solution)/shard_map/ppermute | solution.py:351
  6.1 15.6 %collective-permute-start.1 = (bf16[544,256]{1,0:T(8,128)(2,1)}, bf16[544,256]{1,0:T(8,128)(2,1)S(1)}, u32[]{:S(2)}, u32[]{:S(2)}) collective-permute-start(bf16[544,256]{1,0:T(8,128)(2,1)} %get-tuple-element.26), channel_id=1, source_target_pairs={{0,384},{128,0},{256,128},{384,256},{1,385},{129,1},{257,129},{385... | collective-permute-start | bytes 835592 | tf_op jit(solution)/shard_map/ppermute | solution.py:351
  9.8 13.5 %collective-permute-start.2 = (bf16[544,256]{1,0:T(8,128)(2,1)}, bf16[544,256]{1,0:T(8,128)(2,1)S(1)}, u32[]{:S(2)}, u32[]{:S(2)}) collective-permute-start(bf16[544,256]{1,0:T(8,128)(2,1)} %get-tuple-element.27), channel_id=1, source_target_pairs={{0,256},{128,384},{256,0},{384,128},{1,257},{129,385},{257,1},{385... | collective-permute-start | bytes 835592 | tf_op jit(solution)/shard_map/ppermute | solution.py:351
  13.5 1.0 copy-start.5
  23.3 11.8 %copy-start.3 = (bf16[192,256]{1,0:T(8,128)(2,1)S(1)}, bf16[192,256]{1,0:T(8,128)(2,1)}, u32[]{:S(2)}) copy-start(bf16[192,256]{1,0:T(8,128)(2,1)} %refs_0_.1) | copy-start | bytes 294916
  23.3 22.6 %copy-start.9 = (s32[192]{0:T(256)S(1)}, s32[192]{0:T(256)}, u32[]{:S(2)}) copy-start(s32[192]{0:T(256)} %param.16) | copy-start | bytes 2308
  23.3 30.2 %copy-start.1 = (bf16[256,1024]{1,0:T(8,128)(2,1)S(1)}, bf16[256,1024]{1,0:T(8,128)(2,1)}, u32[]{:S(2)}) copy-start(bf16[256,1024]{1,0:T(8,128)(2,1)} %self_ref.1) | copy-start | bytes 1572868
  23.3 30.2 %copy-start.2 = (bf16[256,1024]{1,0:T(8,128)(2,1)S(1)}, bf16[256,1024]{1,0:T(8,128)(2,1)}, u32[]{:S(2)}) copy-start(bf16[256,1024]{1,0:T(8,128)(2,1)} %neigh_ref.1) | copy-start | bytes 1572868
  25.1 28.3 %all-to-all-start = ((bf16[8,192,256]{2,1,0:T(8,128)(2,1)}), bf16[8,192,256]{2,1,0:T(8,128)(2,1)S(1)}, u32[]{:S(2)}, u32[]{:S(2)}) async-start(bf16[8,192,256]{2,1,0:T(8,128)(2,1)} %bitcast.3), calls=%async_computation | async-start | bytes 1572864 | tf_op jit(solution)/shard_map/all_to_all | solution.py:347
  35.1 10.9 %collective-permute-start.3 = (bf16[192,256]{1,0:T(8,128)(2,1)S(1)}, bf16[192,256]{1,0:T(8,128)(2,1)S(1)}, u32[]{:S(2)}, u32[]{:S(2)}) collective-permute-start(bf16[192,256]{1,0:T(8,128)(2,1)S(1)} %copy-done.3), channel_id=1, source_target_pairs={{0,128},{128,256},{256,384},{384,0},{1,129},{129,257},{257,385},{3... | collective-permute-start | bytes 294920 | tf_op jit(solution)/shard_map/ppermute | solution.py:351
  38.1 8.4 %collective-permute-start.4 = (bf16[192,256]{1,0:T(8,128)(2,1)S(1)}, bf16[192,256]{1,0:T(8,128)(2,1)S(1)}, u32[]{:S(2)}, u32[]{:S(2)}) collective-permute-start(bf16[192,256]{1,0:T(8,128)(2,1)S(1)} %copy-done.3), channel_id=1, source_target_pairs={{0,256},{128,384},{256,0},{384,128},{1,257},{129,385},{257,1},{385... | collective-permute-start | bytes 294920 | tf_op jit(solution)/shard_map/ppermute | solution.py:351
  44.0 6.5 %collective-permute-start.5 = (bf16[192,256]{1,0:T(8,128)(2,1)S(1)}, bf16[192,256]{1,0:T(8,128)(2,1)S(1)}, u32[]{:S(2)}, u32[]{:S(2)}) collective-permute-start(bf16[192,256]{1,0:T(8,128)(2,1)S(1)} %copy-done.3), channel_id=1, source_target_pairs={{0,384},{128,0},{256,128},{384,256},{1,385},{129,1},{257,129},{385... | collective-permute-start | bytes 294920 | tf_op jit(solution)/shard_map/ppermute | solution.py:351
  46.0 23.4 %copy-start.8 = (s32[192]{0:T(256)S(1)}, s32[192]{0:T(256)}, u32[]{:S(2)}) copy-start(s32[192]{0:T(256)} %param.18) | copy-start | bytes 2308
  53.9 26.6 %copy-start.7 = (s32[192,10]{0,1:T(8,128)S(1)}, s32[192,10]{0,1:T(8,128)}, u32[]{:S(2)}) copy-start(s32[192,10]{0,1:T(8,128)} %param.17) | copy-start | bytes 23044
  53.9 38.7 %copy-start = (bf16[1024,1024]{1,0:T(8,128)(2,1)S(1)}, bf16[1024,1024]{1,0:T(8,128)(2,1)}, u32[]{:S(2)}) copy-start(bf16[1024,1024]{1,0:T(8,128)(2,1)} %two_ref.1) | copy-start | bytes 6291460
  54.0 38.7 %copy-start.4 = (bf16[1024,172]{0,1:T(8,128)(2,1)S(1)}, bf16[1024,172]{0,1:T(8,128)(2,1)}, u32[]{:S(2)}) copy-start(bf16[1024,172]{0,1:T(8,128)(2,1)} %param.22) | copy-start | bytes 1056772
  54.0 38.7 %copy-start.6 = (bf16[192,172]{0,1:T(8,128)(2,1)S(1)}, bf16[192,172]{0,1:T(8,128)(2,1)}, u32[]{:S(2)}) copy-start(bf16[192,172]{0,1:T(8,128)(2,1)} %param.23) | copy-start | bytes 198148
  57.2 17.9 %all-to-all-start.1 = ((bf16[8,96,128]{2,1,0:T(8,128)(2,1)}), bf16[8,96,128]{2,1,0:T(8,128)(2,1)S(1)}, u32[]{:S(2)}, u32[]{:S(2)}) async-start(bf16[8,96,128]{2,1,0:T(8,128)(2,1)} %pair_sum.1), calls=%async_computation.1 | async-start | bytes 393216 | tf_op jit(solution)/shard_map/all_to_all | solution.py:347
  64.3 8.5 %collective-permute-start.6 = (bf16[192,256]{1,0:T(8,128)(2,1)S(1)}, bf16[192,256]{1,0:T(8,128)(2,1)S(1)}, u32[]{:S(2)}, u32[]{:S(2)}) collective-permute-start(bf16[192,256]{1,0:T(8,128)(2,1)S(1)} %get-tuple-element.34.refs_4_), channel_id=1, source_target_pairs={{0,128},{128,256},{256,384},{384,0},{1,129},{129,257},{257,385},{3... | collective-permute-start | bytes 294920 | tf_op jit(solution)/shard_map/ppermute | solution.py:351
  75.8 14.6 %all-to-all-start.2 = ((bf16[8,96,128]{2,1,0:T(8,128)(2,1)}), bf16[8,96,128]{2,1,0:T(8,128)(2,1)}, u32[]{:S(2)}, u32[]{:S(2)}) async-start(bf16[8,96,128]{2,1,0:T(8,128)(2,1)} %sum_and_spread.2), calls=%async_computation.2 | async-start | bytes 393216 | tf_op jit(solution)/shard_map/all_to_all | solution.py:347
  81.3 11.4 %collective-permute-start.7 = (bf16[192,256]{1,0:T(8,128)(2,1)S(1)}, bf16[192,256]{1,0:T(8,128)(2,1)S(1)}, u32[]{:S(2)}, u32[]{:S(2)}) collective-permute-start(bf16[192,256]{1,0:T(8,128)(2,1)S(1)} %get-tuple-element.34.refs_4_), channel_id=1, source_target_pairs={{0,256},{128,384},{256,0},{384,128},{1,257},{129,385},{257,1},{385... | collective-permute-start | bytes 294920 | tf_op jit(solution)/shard_map/ppermute | solution.py:351
  84.7 8.0 %collective-permute-start.8 = (bf16[192,256]{1,0:T(8,128)(2,1)S(1)}, bf16[192,256]{1,0:T(8,128)(2,1)S(1)}, u32[]{:S(2)}, u32[]{:S(2)}) collective-permute-start(bf16[192,256]{1,0:T(8,128)(2,1)S(1)} %get-tuple-element.34.refs_4_), channel_id=1, source_target_pairs={{0,384},{128,0},{256,128},{384,256},{1,385},{129,1},{257,129},{385... | collective-permute-start | bytes 294920 | tf_op jit(solution)/shard_map/ppermute | solution.py:351

commit v8 on v7

--- a/solution.py
+++ b/solution.py
@@ -203,7 +203,7 @@
 
 
 def second_kernel(
-    pre_ref, adj_ref, two_ref, three_ref, cot_ref, logits_out, grad_ref, logits_ref, sem
+    pre_ref, adj_ref, two_ref, three_ref, cot_ref, logits_ref, grad_ref
 ):
     count, height, width = pre_ref.shape
     halves = adj_ref.shape[0] // height
@@ -223,8 +223,6 @@
     second_hidden = (pre_two * gate_two).astype(jnp.bfloat16)
     across = ((1,), (1,))
     logits_ref[...] = dot(three_ref[...], second_hidden, across).astype(jnp.bfloat16)
-    copy = pltpu.make_async_copy(logits_ref, logits_out, sem)
-    copy.start()
     slope_two = gate_two + pre_two * gate_two * (1.0 - gate_two)
     back_two = dot(cot_ref[...], three_ref[...], ((0,), (0,)))
     grad_two = (back_two * slope_two).astype(jnp.bfloat16)
@@ -241,7 +239,6 @@
     quarter = grad_ref.shape[2]
     for x in range(grad_ref.shape[0]):
         grad_ref[x] = grad_one[:, x * quarter : (x + 1) * quarter]
-    copy.wait()
 
 
 def second_layer(pre, adjacency, weight_two, weight_three, cotangent):
@@ -252,14 +249,10 @@
     return pl.pallas_call(
         second_kernel,
         in_specs=[vmem] * 5,
-        out_specs=[pl.BlockSpec(memory_space=pl.ANY), vmem],
+        out_specs=[vmem] * 2,
         out_shape=[
             jax.ShapeDtypeStruct((classes, rows), jnp.bfloat16),
             jax.ShapeDtypeStruct((XS, rows, hidden // XS), jnp.bfloat16),
-        ],
-        scratch_shapes=[
-            pltpu.VMEM((classes, rows), jnp.bfloat16),
-            pltpu.SemaphoreType.DMA(()),
         ],
         compiler_params=params(24),
         name="second_layer",

time: 154 us -> 154 us (level)
  no operation moved by 1% of the time
where the time goes in v8:
time: 154 us; the launch traced here: 153 us
  blocking collectives  61.4 us (40%)
  starting transfers between devices  57.4 us (37%)
  waiting for transfers between devices  19.4 us (13%)
  Pallas kernels  12 us (8%)
    all_to_all x3, blocking collectives, exchange(): return lax.all_to_all(pieces, axis, split_axis=0, concat_axis=0, tiled=True)  56.6 us
    ppermute x9, starting transfers between devices, shift_x(): return lax.ppermute(array, 'x', [(i, (i + steps) % XS) for i in range(XS)])  35.6 us
    all_to_all x3, starting transfers between devices, exchange(): return lax.all_to_all(pieces, axis, split_axis=0, concat_axis=0, tiled=True)  21.8 us
    ppermute x9, waiting for transfers between devices, shift_x(): return lax.ppermute(array, 'x', [(i, (i + steps) % XS) for i in range(XS)])  14 us
    all_to_all x3, waiting for transfers between devices, exchange(): return lax.all_to_all(pieces, axis, split_axis=0, concat_axis=0, tiled=True)  5.33 us
    pallas_call x3, Pallas kernels, gather_sum(): pl.pallas_call(functools.partial(gather_kernel, slots, int(carried is not...  4.32 us
  transfers between devices with their start and end apart: 12, of which 6 were waited for; matrix products, arithmetic and copies ran while one was open for 1% of the time, Pallas kernels for 2%

profile of v8, /device:TPU:64, one launch (start us, length us, event | category | flops | bytes accessed | tf_op | source)
XLA Modules:
  0.0 153.0 jit_solution(7311391879172334710)
XLA Ops:
  0.6 2.1 %payloads.1 = (bf16[544,256]{1,0:T(8,128)(2,1)}, bf16[544,256]{1,0:T(8,128)(2,1)}, bf16[544,256]{1,0:T(8,128)(2,1)}, bf16[544,256]{1,0:T(8,128)(2,1)}) custom-call(s32[1]{0:T(128)} %bitcast.place_ref, s32[4,6144]{1,0:T(4,128)} %bitcast.18, s32[1,6144]{1,0:T(1,128)} %count_hbm.1, bf16[512,256]{1,0:T(8,128)(2,1)} %table_hbm.1), custom_call_target="tpu_custom_call" | custom-call | tf_op jit(solution)/shard_map/payloads/pallas_call | solution.py:78
  2.7 3.4 %collective-permute-start = (bf16[544,256]{1,0:T(8,128)(2,1)}, bf16[544,256]{1,0:T(8,128)(2,1)S(1)}, u32[]{:S(2)}, u32[]{:S(2)}) collective-permute-start(bf16[544,256]{1,0:T(8,128)(2,1)} %get-tuple-element.25), channel_id=1, source_target_pairs={{0,128},{128,256},{256,384},{384,0},{1,129},{129,257},{257,385},{3... | collective-permute-start | bytes 835592 | tf_op jit(solution)/shard_map/ppermute | solution.py:344
  6.1 3.7 %collective-permute-start.1 = (bf16[544,256]{1,0:T(8,128)(2,1)}, bf16[544,256]{1,0:T(8,128)(2,1)S(1)}, u32[]{:S(2)}, u32[]{:S(2)}) collective-permute-start(bf16[544,256]{1,0:T(8,128)(2,1)} %get-tuple-element.26), channel_id=1, source_target_pairs={{0,384},{128,0},{256,128},{384,256},{1,385},{129,1},{257,129},{385... | collective-permute-start | bytes 835592 | tf_op jit(solution)/shard_map/ppermute | solution.py:344
  9.8 3.7 %collective-permute-start.2 = (bf16[544,256]{1,0:T(8,128)(2,1)}, bf16[544,256]{1,0:T(8,128)(2,1)S(1)}, u32[]{:S(2)}, u32[]{:S(2)}) collective-permute-start(bf16[544,256]{1,0:T(8,128)(2,1)} %get-tuple-element.27), channel_id=1, source_target_pairs={{0,256},{128,384},{256,0},{384,128},{1,257},{129,385},{257,1},{385... | collective-permute-start | bytes 835592 | tf_op jit(solution)/shard_map/ppermute | solution.py:344
  13.5 0.0 copy-start.5
  13.5 0.9 copy-done.5
  14.5 1.0 gather_sum.3.refs_0_
  15.5 0.0 collective-permute-done.refs_1_
  15.5 6.2 %collective-permute-done.1.refs_2_ = bf16[544,256]{1,0:T(8,128)(2,1)S(1)} collective-permute-done((bf16[544,256]{1,0:T(8,128)(2,1)}, bf16[544,256]{1,0:T(8,128)(2,1)S(1)}, u32[]{:S(2)}, u32[]{:S(2)}) %collective-permute-start.1) | collective-permute-done | bytes 278560 | tf_op jit(solution)/shard_map/ppermute | solution.py:344
  21.7 1.6 %gather_sum.4.refs_0_ = f32[1536,256]{1,0:T(8,128)S(1)} custom-call(f32[1536,256]{1,0:T(8,128)S(1)} %gather_sum.3.refs_0_, bf16[544,256]{1,0:T(8,128)(2,1)S(1)} %collective-permute-done.refs_1_, bf16[544,256]{1,0:T(8,128)(2,1)S(1)} %collective-permute-done.1.refs_2_), custom_call_target="tpu_custom_call" | custom-call | tf_op jit(solution)/shard_map/gather_sum/pallas_call | solution.py:135
  23.3 0.0 copy-start.3
  23.3 0.0 copy-start.9
  23.3 0.0 copy-start.1
  23.3 0.0 copy-start.2
  23.3 0.0 collective-permute-done.2.refs_1_
  23.3 1.8 %gather_sum.5 = bf16[1536,256]{1,0:T(8,128)(2,1)} custom-call(f32[1536,256]{1,0:T(8,128)S(1)} %gather_sum.4.refs_0_, bf16[544,256]{1,0:T(8,128)(2,1)S(1)} %collective-permute-done.2.refs_1_), custom_call_target="tpu_custom_call" | custom-call | tf_op jit(solution)/shard_map/gather_sum/pallas_call | solution.py:135
  25.1 10.0 %all-to-all-start = ((bf16[8,192,256]{2,1,0:T(8,128)(2,1)}), bf16[8,192,256]{2,1,0:T(8,128)(2,1)S(1)}, u32[]{:S(2)}, u32[]{:S(2)}) async-start(bf16[8,192,256]{2,1,0:T(8,128)(2,1)} %bitcast.3), calls=%async_computation | async-start | bytes 1572864 | tf_op jit(solution)/shard_map/all_to_all | solution.py:340
  35.1 0.0 copy-done.3
  35.1 3.0 %collective-permute-start.3 = (bf16[192,256]{1,0:T(8,128)(2,1)S(1)}, bf16[192,256]{1,0:T(8,128)(2,1)S(1)}, u32[]{:S(2)}, u32[]{:S(2)}) collective-permute-start(bf16[192,256]{1,0:T(8,128)(2,1)S(1)} %copy-done.3), channel_id=1, source_target_pairs={{0,128},{128,256},{256,384},{384,0},{1,129},{129,257},{257,385},{3... | collective-permute-start | bytes 294920 | tf_op jit(solution)/shard_map/ppermute | solution.py:344
  38.1 5.8 %collective-permute-start.4 = (bf16[192,256]{1,0:T(8,128)(2,1)S(1)}, bf16[192,256]{1,0:T(8,128)(2,1)S(1)}, u32[]{:S(2)}, u32[]{:S(2)}) collective-permute-start(bf16[192,256]{1,0:T(8,128)(2,1)S(1)} %copy-done.3), channel_id=1, source_target_pairs={{0,256},{128,384},{256,0},{384,128},{1,257},{129,385},{257,1},{385... | collective-permute-start | bytes 294920 | tf_op jit(solution)/shard_map/ppermute | solution.py:344
  44.0 1.9 %collective-permute-start.5 = (bf16[192,256]{1,0:T(8,128)(2,1)S(1)}, bf16[192,256]{1,0:T(8,128)(2,1)S(1)}, u32[]{:S(2)}, u32[]{:S(2)}) collective-permute-start(bf16[192,256]{1,0:T(8,128)(2,1)S(1)} %copy-done.3), channel_id=1, source_target_pairs={{0,384},{128,0},{256,128},{384,256},{1,385},{129,1},{257,129},{385... | collective-permute-start | bytes 294920 | tf_op jit(solution)/shard_map/ppermute | solution.py:344
  45.9 0.0 copy-done.9
  45.9 0.1 copy.20.degree_ref
  46.0 0.0 copy-start.8
  46.0 0.0 collective-permute-done.3.refs_1_
  46.0 0.5 collective-permute-done.4.refs_2_
  46.5 3.9 %collective-permute-done.5.refs_3_ = bf16[192,256]{1,0:T(8,128)(2,1)S(1)} collective-permute-done((bf16[192,256]{1,0:T(8,128)(2,1)S(1)}, bf16[192,256]{1,0:T(8,128)(2,1)S(1)}, u32[]{:S(2)}, u32[]{:S(2)}) %collective-permute-start.5) | collective-permute-done | bytes 98336 | tf_op jit(solution)/shard_map/ppermute | solution.py:344
  50.5 3.0 %all-to-all-done.recv_ref = bf16[8,192,256]{2,1,0:T(8,128)(2,1)S(1)} async-done(((bf16[8,192,256]{2,1,0:T(8,128)(2,1)}), bf16[8,192,256]{2,1,0:T(8,128)(2,1)S(1)}, u32[]{:S(2)}, u32[]{:S(2)}) %all-to-all-start) | async-done | bytes 786464 | tf_op jit(solution)/shard_map/all_to_all | solution.py:340
  53.5 0.0 copy-done.1
  53.5 0.0 copy-done.2
  53.5 0.4 first_layer.1
  53.9 0.0 copy-start.7
  53.9 0.0 copy-start
  54.0 0.0 copy-start.4
  54.0 0.0 copy-start.6
  54.0 2.5 %all-gather = bf16[32,96,128]{2,1,0:T(8,128)(2,1)S(1)} all-gather(bf16[16,96,128]{2,1,0:T(8,128)(2,1)S(1)} %get-tuple-element.35), channel_id=2, replica_groups=mesh['x'=4,'z'=8,'y'=8,'c'=2] {'c'}, dimensions={0}, use_global_device_ids=true | all-gather | bytes 1179648 | tf_op jit(solution)/shard_map/all_gather | solution.py:387
  56.5 0.7 pair_sum.1
  57.2 7.1 %all-to-all-start.1 = ((bf16[8,96,128]{2,1,0:T(8,128)(2,1)}), bf16[8,96,128]{2,1,0:T(8,128)(2,1)S(1)}, u32[]{:S(2)}, u32[]{:S(2)}) async-start(bf16[8,96,128]{2,1,0:T(8,128)(2,1)} %pair_sum.1), calls=%async_computation.1 | async-start | bytes 393216 | tf_op jit(solution)/shard_map/all_to_all | solution.py:340
  64.3 5.1 %collective-permute-start.6 = (bf16[192,256]{1,0:T(8,128)(2,1)S(1)}, bf16[192,256]{1,0:T(8,128)(2,1)S(1)}, u32[]{:S(2)}, u32[]{:S(2)}) collective-permute-start(bf16[192,256]{1,0:T(8,128)(2,1)S(1)} %get-tuple-element.34.refs_4_), channel_id=1, source_target_pairs={{0,128},{128,256},{256,384},{384,0},{1,129},{129,257},{257,385},{3... | collective-permute-start | bytes 294920 | tf_op jit(solution)/shard_map/ppermute | solution.py:344
  69.4 0.0 copy-done.8
  69.4 3.4 %collective-permute-done.6.refs_5_ = bf16[192,256]{1,0:T(8,128)(2,1)S(1)} collective-permute-done((bf16[192,256]{1,0:T(8,128)(2,1)S(1)}, bf16[192,256]{1,0:T(8,128)(2,1)S(1)}, u32[]{:S(2)}, u32[]{:S(2)}) %collective-permute-start.6) | collective-permute-done | bytes 98336 | tf_op jit(solution)/shard_map/ppermute | solution.py:344
  72.8 2.3 %all-to-all-done.1.recv_ref = bf16[8,96,128]{2,1,0:T(8,128)(2,1)S(1)} async-done(((bf16[8,96,128]{2,1,0:T(8,128)(2,1)}), bf16[8,96,128]{2,1,0:T(8,128)(2,1)S(1)}, u32[]{:S(2)}, u32[]{:S(2)}) %all-to-all-start.1) | async-done | bytes 196640 | tf_op jit(solution)/shard_map/all_to_all | solution.py:340
  75.1 0.7 sum_and_spread.2
  75.8 4.7 %all-to-all-start.2 = ((bf16[8,96,128]{2,1,0:T(8,128)(2,1)}), bf16[8,96,128]{2,1,0:T(8,128)(2,1)}, u32[]{:S(2)}, u32[]{:S(2)}) async-start(bf16[8,96,128]{2,1,0:T(8,128)(2,1)} %sum_and_spread.2), calls=%async_computation.2 | async-start | bytes 393216 | tf_op jit(solution)/shard_map/all_to_all | solution.py:340
  80.5 0.0 copy-done.7
  80.5 0.8 convert_reduce_fusion
  81.3 3.4 %collective-permute-start.7 = (bf16[192,256]{1,0:T(8,128)(2,1)S(1)}, bf16[192,256]{1,0:T(8,128)(2,1)S(1)}, u32[]{:S(2)}, u32[]{:S(2)}) collective-permute-start(bf16[192,256]{1,0:T(8,128)(2,1)S(1)} %get-tuple-element.34.refs_4_), channel_id=1, source_target_pairs={{0,256},{128,384},{256,0},{384,128},{1,257},{129,385},{257,1},{385... | collective-permute-start | bytes 294920 | tf_op jit(solution)/shard_map/ppermute | solution.py:344
  84.7 5.6 %collective-permute-start.8 = (bf16[192,256]{1,0:T(8,128)(2,1)S(1)}, bf16[192,256]{1,0:T(8,128)(2,1)S(1)}, u32[]{:S(2)}, u32[]{:S(2)}) collective-permute-start(bf16[192,256]{1,0:T(8,128)(2,1)S(1)} %get-tuple-element.34.refs_4_), channel_id=1, source_target_pairs={{0,384},{128,0},{256,128},{384,256},{1,385},{129,1},{257,129},{385... | collective-permute-start | bytes 294920 | tf_op jit(solution)/shard_map/ppermute | solution.py:344
  90.3 0.0 all-to-all-done.2
  90.4 2.3 %all_gather.11.pre_ref = bf16[16,96,128]{2,1,0:T(8,128)(2,1)S(1)} all-gather(bf16[8,96,128]{2,1,0:T(8,128)(2,1)} %all-to-all-done.2), channel_id=1, replica_groups=mesh['x'=4,'z'=8,'y'=8,'c'=2] {'c'}, dimensions={0}, use_global_device_ids=true | all-gather | bytes 589824 | tf_op jit(solution)/shard_map/all_gather | solution.py:390
  92.7 0.0 collective-permute-done.7.refs_6_
  92.7 0.0 collective-permute-done.8.refs_7_
  92.7 0.0 copy-done
  92.7 0.0 copy-done.4
  92.7 0.0 copy-done.6
  92.7 2.1 %second_layer.1 = (bf16[172,192]{1,0:T(8,128)(2,1)}, bf16[4,192,256]{2,1,0:T(8,128)(2,1)S(1)}) custom-call(bf16[16,96,128]{2,1,0:T(8,128)(2,1)S(1)} %all_gather.11.pre_ref, bf16[192,192]{1,0:T(8,128)(2,1)S(1)} %add_convert_fusion.adj_ref, bf16[1024,1024]{1,0:T(8,128)(2,1)S(1)} %copy-done, bf16[172,1024]{1,0:T(8,128)(2,1)S(1)} %bitcast.16, ...), custom_call_target="tpu_custom_call" | custom-call | tf_op jit(solution)/shard_map/second_layer/pallas_call | solution.py:249
  94.8 12.4 %all_to_all.30.refs_8_ = bf16[4,192,256]{2,1,0:T(8,128)(2,1)S(1)} all-to-all(bf16[4,192,256]{2,1,0:T(8,128)(2,1)S(1)} %get-tuple-element.41), channel_id=1, replica_groups=mesh['x'=4,'z'=8,'y'=8,'c'=2] {'x'}, dimensions={0} | all-to-all | bytes 786432 | tf_op jit(solution)/shard_map/all_to_all | solution.py:340
  107.2 0.5 gradient_part.1
  107.7 13.3 %all_to_all.31.recv_ref = bf16[8,64,256]{2,1,0:T(8,128)(2,1)S(1)} all-to-all(bf16[8,64,256]{2,1,0:T(8,128)(2,1)S(1)} %bitcast.15), channel_id=1, replica_groups=mesh['x'=4,'z'=8,'y'=8,'c'=2] {'z'}, dimensions={0} | all-to-all | bytes 524288 | tf_op jit(solution)/shard_map/all_to_all | solution.py:340
  121.0 0.1 sum_and_spread.3
  121.1 30.9 %all_to_all.32 = bf16[32,64,256]{2,1,0:T(8,128)(2,1)S(1)} all-to-all(bf16[32,64,256]{2,1,0:T(8,128)(2,1)S(1)} %sum_and_spread.3), channel_id=1, replica_groups=mesh['x'=4,'z'=8,'y'=8,'c'=2] {'x','z'}, dimensions={0} | all-to-all | bytes 2097152 | tf_op jit(solution)/shard_map/all_to_all | solution.py:340
  152.0 1.0 assemble.1
  (3 shorter events, 0.0 us)
Async XLA Ops:
  2.7 12.8 %collective-permute-start = (bf16[544,256]{1,0:T(8,128)(2,1)}, bf16[544,256]{1,0:T(8,128)(2,1)S(1)}, u32[]{:S(2)}, u32[]{:S(2)}) collective-permute-start(bf16[544,256]{1,0:T(8,128)(2,1)} %get-tuple-element.25), channel_id=1, source_target_pairs={{0,128},{128,256},{256,384},{384,0},{1,129},{129,257},{257,385},{3... | collective-permute-start | bytes 835592 | tf_op jit(solution)/shard_map/ppermute | solution.py:344
  6.1 15.6 %collective-permute-start.1 = (bf16[544,256]{1,0:T(8,128)(2,1)}, bf16[544,256]{1,0:T(8,128)(2,1)S(1)}, u32[]{:S(2)}, u32[]{:S(2)}) collective-permute-start(bf16[544,256]{1,0:T(8,128)(2,1)} %get-tuple-element.26), channel_id=1, source_target_pairs={{0,384},{128,0},{256,128},{384,256},{1,385},{129,1},{257,129},{385... | collective-permute-start | bytes 835592 | tf_op jit(solution)/shard_map/ppermute | solution.py:344
  9.8 13.5 %collective-permute-start.2 = (bf16[544,256]{1,0:T(8,128)(2,1)}, bf16[544,256]{1,0:T(8,128)(2,1)S(1)}, u32[]{:S(2)}, u32[]{:S(2)}) collective-permute-start(bf16[544,256]{1,0:T(8,128)(2,1)} %get-tuple-element.27), channel_id=1, source_target_pairs={{0,256},{128,384},{256,0},{384,128},{1,257},{129,385},{257,1},{385... | collective-permute-start | bytes 835592 | tf_op jit(solution)/shard_map/ppermute | solution.py:344
  13.5 1.0 copy-start.5
  23.3 11.8 %copy-start.3 = (bf16[192,256]{1,0:T(8,128)(2,1)S(1)}, bf16[192,256]{1,0:T(8,128)(2,1)}, u32[]{:S(2)}) copy-start(bf16[192,256]{1,0:T(8,128)(2,1)} %refs_0_.1) | copy-start | bytes 294916
  23.3 22.6 %copy-start.9 = (s32[192]{0:T(256)S(1)}, s32[192]{0:T(256)}, u32[]{:S(2)}) copy-start(s32[192]{0:T(256)} %param.16) | copy-start | bytes 2308
  23.3 30.2 %copy-start.1 = (bf16[256,1024]{1,0:T(8,128)(2,1)S(1)}, bf16[256,1024]{1,0:T(8,128)(2,1)}, u32[]{:S(2)}) copy-start(bf16[256,1024]{1,0:T(8,128)(2,1)} %self_ref.1) | copy-start | bytes 1572868
  23.3 30.2 %copy-start.2 = (bf16[256,1024]{1,0:T(8,128)(2,1)S(1)}, bf16[256,1024]{1,0:T(8,128)(2,1)}, u32[]{:S(2)}) copy-start(bf16[256,1024]{1,0:T(8,128)(2,1)} %neigh_ref.1) | copy-start | bytes 1572868
  25.1 28.3 %all-to-all-start = ((bf16[8,192,256]{2,1,0:T(8,128)(2,1)}), bf16[8,192,256]{2,1,0:T(8,128)(2,1)S(1)}, u32[]{:S(2)}, u32[]{:S(2)}) async-start(bf16[8,192,256]{2,1,0:T(8,128)(2,1)} %bitcast.3), calls=%async_computation | async-start | bytes 1572864 | tf_op jit(solution)/shard_map/all_to_all | solution.py:340
  35.1 10.9 %collective-permute-start.3 = (bf16[192,256]{1,0:T(8,128)(2,1)S(1)}, bf16[192,256]{1,0:T(8,128)(2,1)S(1)}, u32[]{:S(2)}, u32[]{:S(2)}) collective-permute-start(bf16[192,256]{1,0:T(8,128)(2,1)S(1)} %copy-done.3), channel_id=1, source_target_pairs={{0,128},{128,256},{256,384},{384,0},{1,129},{129,257},{257,385},{3... | collective-permute-start | bytes 294920 | tf_op jit(solution)/shard_map/ppermute | solution.py:344
  38.1 8.4 %collective-permute-start.4 = (bf16[192,256]{1,0:T(8,128)(2,1)S(1)}, bf16[192,256]{1,0:T(8,128)(2,1)S(1)}, u32[]{:S(2)}, u32[]{:S(2)}) collective-permute-start(bf16[192,256]{1,0:T(8,128)(2,1)S(1)} %copy-done.3), channel_id=1, source_target_pairs={{0,256},{128,384},{256,0},{384,128},{1,257},{129,385},{257,1},{385... | collective-permute-start | bytes 294920 | tf_op jit(solution)/shard_map/ppermute | solution.py:344
  44.0 6.5 %collective-permute-start.5 = (bf16[192,256]{1,0:T(8,128)(2,1)S(1)}, bf16[192,256]{1,0:T(8,128)(2,1)S(1)}, u32[]{:S(2)}, u32[]{:S(2)}) collective-permute-start(bf16[192,256]{1,0:T(8,128)(2,1)S(1)} %copy-done.3), channel_id=1, source_target_pairs={{0,384},{128,0},{256,128},{384,256},{1,385},{129,1},{257,129},{385... | collective-permute-start | bytes 294920 | tf_op jit(solution)/shard_map/ppermute | solution.py:344
  46.0 23.4 %copy-start.8 = (s32[192]{0:T(256)S(1)}, s32[192]{0:T(256)}, u32[]{:S(2)}) copy-start(s32[192]{0:T(256)} %param.18) | copy-start | bytes 2308
  53.9 26.6 %copy-start.7 = (s32[192,10]{0,1:T(8,128)S(1)}, s32[192,10]{0,1:T(8,128)}, u32[]{:S(2)}) copy-start(s32[192,10]{0,1:T(8,128)} %param.17) | copy-start | bytes 23044
  53.9 38.7 %copy-start = (bf16[1024,1024]{1,0:T(8,128)(2,1)S(1)}, bf16[1024,1024]{1,0:T(8,128)(2,1)}, u32[]{:S(2)}) copy-start(bf16[1024,1024]{1,0:T(8,128)(2,1)} %two_ref.1) | copy-start | bytes 6291460
  54.0 38.7 %copy-start.4 = (bf16[1024,172]{0,1:T(8,128)(2,1)S(1)}, bf16[1024,172]{0,1:T(8,128)(2,1)}, u32[]{:S(2)}) copy-start(bf16[1024,172]{0,1:T(8,128)(2,1)} %param.22) | copy-start | bytes 1056772
  54.0 38.7 %copy-start.6 = (bf16[192,172]{0,1:T(8,128)(2,1)S(1)}, bf16[192,172]{0,1:T(8,128)(2,1)}, u32[]{:S(2)}) copy-start(bf16[192,172]{0,1:T(8,128)(2,1)} %param.23) | copy-start | bytes 198148
  57.2 17.9 %all-to-all-start.1 = ((bf16[8,96,128]{2,1,0:T(8,128)(2,1)}), bf16[8,96,128]{2,1,0:T(8,128)(2,1)S(1)}, u32[]{:S(2)}, u32[]{:S(2)}) async-start(bf16[8,96,128]{2,1,0:T(8,128)(2,1)} %pair_sum.1), calls=%async_computation.1 | async-start | bytes 393216 | tf_op jit(solution)/shard_map/all_to_all | solution.py:340
  64.3 8.5 %collective-permute-start.6 = (bf16[192,256]{1,0:T(8,128)(2,1)S(1)}, bf16[192,256]{1,0:T(8,128)(2,1)S(1)}, u32[]{:S(2)}, u32[]{:S(2)}) collective-permute-start(bf16[192,256]{1,0:T(8,128)(2,1)S(1)} %get-tuple-element.34.refs_4_), channel_id=1, source_target_pairs={{0,128},{128,256},{256,384},{384,0},{1,129},{129,257},{257,385},{3... | collective-permute-start | bytes 294920 | tf_op jit(solution)/shard_map/ppermute | solution.py:344
  75.8 14.6 %all-to-all-start.2 = ((bf16[8,96,128]{2,1,0:T(8,128)(2,1)}), bf16[8,96,128]{2,1,0:T(8,128)(2,1)}, u32[]{:S(2)}, u32[]{:S(2)}) async-start(bf16[8,96,128]{2,1,0:T(8,128)(2,1)} %sum_and_spread.2), calls=%async_computation.2 | async-start | bytes 393216 | tf_op jit(solution)/shard_map/all_to_all | solution.py:340
  81.3 11.4 %collective-permute-start.7 = (bf16[192,256]{1,0:T(8,128)(2,1)S(1)}, bf16[192,256]{1,0:T(8,128)(2,1)S(1)}, u32[]{:S(2)}, u32[]{:S(2)}) collective-permute-start(bf16[192,256]{1,0:T(8,128)(2,1)S(1)} %get-tuple-element.34.refs_4_), channel_id=1, source_target_pairs={{0,256},{128,384},{256,0},{384,128},{1,257},{129,385},{257,1},{385... | collective-permute-start | bytes 294920 | tf_op jit(solution)/shard_map/ppermute | solution.py:344
  84.7 8.0 %collective-permute-start.8 = (bf16[192,256]{1,0:T(8,128)(2,1)S(1)}, bf16[192,256]{1,0:T(8,128)(2,1)S(1)}, u32[]{:S(2)}, u32[]{:S(2)}) collective-permute-start(bf16[192,256]{1,0:T(8,128)(2,1)S(1)} %get-tuple-element.34.refs_4_), channel_id=1, source_target_pairs={{0,384},{128,0},{256,128},{384,256},{1,385},{129,1},{257,129},{385... | collective-permute-start | bytes 294920 | tf_op jit(solution)/shard_map/ppermute | solution.py:344

commit v9 on v8

--- a/solution.py
+++ b/solution.py
@@ -404,7 +404,8 @@
     grad_part = gradient_part(place, [own_features] + own, [mean_rows] + mean, exchange(grad_one, "x"))
     quarter = grad_part.shape[1]
     grad_recv = exchange(grad_part.reshape(groups // XS, -1, quarter), "z")
-    grads = exchange(spread(grad_recv, groups), NODE)
+    part = exchange(spread(grad_recv, groups // XS), "z")
+    grads = exchange(spread(part.reshape(1, -1, quarter), XS), "x")
     grad_self, grad_neigh = assemble(grads.reshape(-1, quarter))
     return (grad_self, grad_neigh, logits.T)
 

time: 154 us -> 151 us (0.981)
  the two profiles are of different devices: /device:TPU:64 before, /device:TPU:2 now
where the time goes in v9:
time: 151 us; the launch traced here: 150 us
  blocking collectives  55.6 us (37%)
  starting transfers between devices  54 us (36%)
  waiting for transfers between devices  25.5 us (17%)
  Pallas kernels  11.9 us (8%)
    all_to_all x4, blocking collectives, exchange(): return lax.all_to_all(pieces, axis, split_axis=0, concat_axis=0, tiled=True)  50.8 us
    ppermute x9, starting transfers between devices, shift_x(): return lax.ppermute(array, 'x', [(i, (i + steps) % XS) for i in range(XS)])  32.6 us
    all_to_all x3, starting transfers between devices, exchange(): return lax.all_to_all(pieces, axis, split_axis=0, concat_axis=0, tiled=True)  21.4 us
    all_to_all x3, waiting for transfers between devices, exchange(): return lax.all_to_all(pieces, axis, split_axis=0, concat_axis=0, tiled=True)  15.9 us
    ppermute x9, waiting for transfers between devices, shift_x(): return lax.ppermute(array, 'x', [(i, (i + steps) % XS) for i in range(XS)])  9.6 us
    pallas_call x3, Pallas kernels, gather_sum(): pl.pallas_call(functools.partial(gather_kernel, slots, int(carried is not...  4.32 us
  transfers between devices with their start and end apart: 12, of which 7 were waited for; matrix products, arithmetic and copies ran while one was open for 1% of the time, Pallas kernels for 2%

profile of v9, /device:TPU:2, one launch (start us, length us, event | category | flops | bytes accessed | tf_op | source)
XLA Modules:
  0.0 150.0 jit_solution(4522934618057443520)
XLA Ops:
  0.6 2.1 %payloads.1 = (bf16[544,256]{1,0:T(8,128)(2,1)}, bf16[544,256]{1,0:T(8,128)(2,1)}, bf16[544,256]{1,0:T(8,128)(2,1)}, bf16[544,256]{1,0:T(8,128)(2,1)}) custom-call(s32[1]{0:T(128)} %bitcast.place_ref, s32[4,6144]{1,0:T(4,128)} %bitcast.20, s32[1,6144]{1,0:T(1,128)} %count_hbm.1, bf16[512,256]{1,0:T(8,128)(2,1)} %table_hbm.1), custom_call_target="tpu_custom_call" | custom-call | tf_op jit(solution)/shard_map/payloads/pallas_call | solution.py:78
  2.7 3.4 %collective-permute-start = (bf16[544,256]{1,0:T(8,128)(2,1)}, bf16[544,256]{1,0:T(8,128)(2,1)S(1)}, u32[]{:S(2)}, u32[]{:S(2)}) collective-permute-start(bf16[544,256]{1,0:T(8,128)(2,1)} %get-tuple-element.25), channel_id=1, source_target_pairs={{0,128},{128,256},{256,384},{384,0},{1,129},{129,257},{257,385},{3... | collective-permute-start | bytes 835592 | tf_op jit(solution)/shard_map/ppermute | solution.py:344
  6.1 6.3 %collective-permute-start.1 = (bf16[544,256]{1,0:T(8,128)(2,1)}, bf16[544,256]{1,0:T(8,128)(2,1)S(1)}, u32[]{:S(2)}, u32[]{:S(2)}) collective-permute-start(bf16[544,256]{1,0:T(8,128)(2,1)} %get-tuple-element.26), channel_id=1, source_target_pairs={{0,384},{128,0},{256,128},{384,256},{1,385},{129,1},{257,129},{385... | collective-permute-start | bytes 835592 | tf_op jit(solution)/shard_map/ppermute | solution.py:344
  12.5 4.0 %collective-permute-start.2 = (bf16[544,256]{1,0:T(8,128)(2,1)}, bf16[544,256]{1,0:T(8,128)(2,1)S(1)}, u32[]{:S(2)}, u32[]{:S(2)}) collective-permute-start(bf16[544,256]{1,0:T(8,128)(2,1)} %get-tuple-element.27), channel_id=1, source_target_pairs={{0,256},{128,384},{256,0},{384,128},{1,257},{129,385},{257,1},{385... | collective-permute-start | bytes 835592 | tf_op jit(solution)/shard_map/ppermute | solution.py:344
  16.5 0.0 copy-start.5
  16.5 0.9 copy-done.5
  17.4 1.0 gather_sum.3.refs_0_
  18.4 0.0 collective-permute-done.refs_1_
  18.4 0.9 collective-permute-done.1.refs_2_
  19.3 1.6 %gather_sum.4.refs_0_ = f32[1536,256]{1,0:T(8,128)S(1)} custom-call(f32[1536,256]{1,0:T(8,128)S(1)} %gather_sum.3.refs_0_, bf16[544,256]{1,0:T(8,128)(2,1)S(1)} %collective-permute-done.refs_1_, bf16[544,256]{1,0:T(8,128)(2,1)S(1)} %collective-permute-done.1.refs_2_), custom_call_target="tpu_custom_call" | custom-call | tf_op jit(solution)/shard_map/gather_sum/pallas_call | solution.py:135
  20.9 0.0 copy-start.3
  20.9 0.0 copy-start.9
  20.9 0.0 copy-start.1
  20.9 0.0 copy-start.2
  21.0 2.1 %collective-permute-done.2.refs_1_ = bf16[544,256]{1,0:T(8,128)(2,1)S(1)} collective-permute-done((bf16[544,256]{1,0:T(8,128)(2,1)}, bf16[544,256]{1,0:T(8,128)(2,1)S(1)}, u32[]{:S(2)}, u32[]{:S(2)}) %collective-permute-start.2) | collective-permute-done | bytes 278560 | tf_op jit(solution)/shard_map/ppermute | solution.py:344
  23.1 1.8 %gather_sum.5 = bf16[1536,256]{1,0:T(8,128)(2,1)} custom-call(f32[1536,256]{1,0:T(8,128)S(1)} %gather_sum.4.refs_0_, bf16[544,256]{1,0:T(8,128)(2,1)S(1)} %collective-permute-done.2.refs_1_), custom_call_target="tpu_custom_call" | custom-call | tf_op jit(solution)/shard_map/gather_sum/pallas_call | solution.py:135
  24.8 10.2 %all-to-all-start = ((bf16[8,192,256]{2,1,0:T(8,128)(2,1)}), bf16[8,192,256]{2,1,0:T(8,128)(2,1)S(1)}, u32[]{:S(2)}, u32[]{:S(2)}) async-start(bf16[8,192,256]{2,1,0:T(8,128)(2,1)} %bitcast.3), calls=%async_computation | async-start | bytes 1572864 | tf_op jit(solution)/shard_map/all_to_all | solution.py:340
  35.1 0.0 copy-done.3
  35.1 1.9 %collective-permute-start.3 = (bf16[192,256]{1,0:T(8,128)(2,1)S(1)}, bf16[192,256]{1,0:T(8,128)(2,1)S(1)}, u32[]{:S(2)}, u32[]{:S(2)}) collective-permute-start(bf16[192,256]{1,0:T(8,128)(2,1)S(1)} %copy-done.3), channel_id=1, source_target_pairs={{0,128},{128,256},{256,384},{384,0},{1,129},{129,257},{257,385},{3... | collective-permute-start | bytes 294920 | tf_op jit(solution)/shard_map/ppermute | solution.py:344
  37.0 5.2 %collective-permute-start.4 = (bf16[192,256]{1,0:T(8,128)(2,1)S(1)}, bf16[192,256]{1,0:T(8,128)(2,1)S(1)}, u32[]{:S(2)}, u32[]{:S(2)}) collective-permute-start(bf16[192,256]{1,0:T(8,128)(2,1)S(1)} %copy-done.3), channel_id=1, source_target_pairs={{0,256},{128,384},{256,0},{384,128},{1,257},{129,385},{257,1},{385... | collective-permute-start | bytes 294920 | tf_op jit(solution)/shard_map/ppermute | solution.py:344
  42.2 4.5 %collective-permute-start.5 = (bf16[192,256]{1,0:T(8,128)(2,1)S(1)}, bf16[192,256]{1,0:T(8,128)(2,1)S(1)}, u32[]{:S(2)}, u32[]{:S(2)}) collective-permute-start(bf16[192,256]{1,0:T(8,128)(2,1)S(1)} %copy-done.3), channel_id=1, source_target_pairs={{0,384},{128,0},{256,128},{384,256},{1,385},{129,1},{257,129},{385... | collective-permute-start | bytes 294920 | tf_op jit(solution)/shard_map/ppermute | solution.py:344
  46.8 0.0 copy-done.9
  46.8 0.1 copy.20.degree_ref
  46.9 0.0 copy-start.8
  46.9 0.0 collective-permute-done.3.refs_1_
  46.9 0.0 collective-permute-done.4.refs_2_
  46.9 2.0 %collective-permute-done.5.refs_3_ = bf16[192,256]{1,0:T(8,128)(2,1)S(1)} collective-permute-done((bf16[192,256]{1,0:T(8,128)(2,1)S(1)}, bf16[192,256]{1,0:T(8,128)(2,1)S(1)}, u32[]{:S(2)}, u32[]{:S(2)}) %collective-permute-start.5) | collective-permute-done | bytes 98336 | tf_op jit(solution)/shard_map/ppermute | solution.py:344
  49.0 8.0 %all-to-all-done.recv_ref = bf16[8,192,256]{2,1,0:T(8,128)(2,1)S(1)} async-done(((bf16[8,192,256]{2,1,0:T(8,128)(2,1)}), bf16[8,192,256]{2,1,0:T(8,128)(2,1)S(1)}, u32[]{:S(2)}, u32[]{:S(2)}) %all-to-all-start) | async-done | bytes 786464 | tf_op jit(solution)/shard_map/all_to_all | solution.py:340
  57.0 0.0 copy-done.1
  57.0 0.0 copy-done.2
  57.0 0.4 first_layer.1
  57.4 0.0 copy-start.7
  57.5 0.0 copy-start
  57.5 0.0 copy-start.4
  57.5 0.0 copy-start.6
  57.5 2.5 %all-gather = bf16[32,96,128]{2,1,0:T(8,128)(2,1)S(1)} all-gather(bf16[16,96,128]{2,1,0:T(8,128)(2,1)S(1)} %get-tuple-element.35), channel_id=2, replica_groups=mesh['x'=4,'z'=8,'y'=8,'c'=2] {'c'}, dimensions={0}, use_global_device_ids=true | all-gather | bytes 1179648 | tf_op jit(solution)/shard_map/all_gather | solution.py:387
  60.0 0.7 pair_sum.1
  60.7 7.1 %all-to-all-start.1 = ((bf16[8,96,128]{2,1,0:T(8,128)(2,1)}), bf16[8,96,128]{2,1,0:T(8,128)(2,1)S(1)}, u32[]{:S(2)}, u32[]{:S(2)}) async-start(bf16[8,96,128]{2,1,0:T(8,128)(2,1)} %pair_sum.1), calls=%async_computation.1 | async-start | bytes 393216 | tf_op jit(solution)/shard_map/all_to_all | solution.py:340
  67.8 1.9 %collective-permute-start.6 = (bf16[192,256]{1,0:T(8,128)(2,1)S(1)}, bf16[192,256]{1,0:T(8,128)(2,1)S(1)}, u32[]{:S(2)}, u32[]{:S(2)}) collective-permute-start(bf16[192,256]{1,0:T(8,128)(2,1)S(1)} %get-tuple-element.34.refs_4_), channel_id=1, source_target_pairs={{0,128},{128,256},{256,384},{384,0},{1,129},{129,257},{257,385},{3... | collective-permute-start | bytes 294920 | tf_op jit(solution)/shard_map/ppermute | solution.py:344
  69.7 0.0 copy-done.8
  69.8 4.6 %collective-permute-done.6.refs_5_ = bf16[192,256]{1,0:T(8,128)(2,1)S(1)} collective-permute-done((bf16[192,256]{1,0:T(8,128)(2,1)S(1)}, bf16[192,256]{1,0:T(8,128)(2,1)S(1)}, u32[]{:S(2)}, u32[]{:S(2)}) %collective-permute-start.6) | collective-permute-done | bytes 98336 | tf_op jit(solution)/shard_map/ppermute | solution.py:344
  74.3 4.3 %all-to-all-done.1.recv_ref = bf16[8,96,128]{2,1,0:T(8,128)(2,1)S(1)} async-done(((bf16[8,96,128]{2,1,0:T(8,128)(2,1)}), bf16[8,96,128]{2,1,0:T(8,128)(2,1)S(1)}, u32[]{:S(2)}, u32[]{:S(2)}) %all-to-all-start.1) | async-done | bytes 196640 | tf_op jit(solution)/shard_map/all_to_all | solution.py:340
  78.6 0.7 sum_and_spread.3
  79.3 4.0 %all-to-all-start.2 = ((bf16[8,96,128]{2,1,0:T(8,128)(2,1)}), bf16[8,96,128]{2,1,0:T(8,128)(2,1)}, u32[]{:S(2)}, u32[]{:S(2)}) async-start(bf16[8,96,128]{2,1,0:T(8,128)(2,1)} %sum_and_spread.3), calls=%async_computation.2 | async-start | bytes 393216 | tf_op jit(solution)/shard_map/all_to_all | solution.py:340
  83.3 0.0 copy-done.7
  83.3 0.8 convert_reduce_fusion
  84.2 3.4 %collective-permute-start.7 = (bf16[192,256]{1,0:T(8,128)(2,1)S(1)}, bf16[192,256]{1,0:T(8,128)(2,1)S(1)}, u32[]{:S(2)}, u32[]{:S(2)}) collective-permute-start(bf16[192,256]{1,0:T(8,128)(2,1)S(1)} %get-tuple-element.34.refs_4_), channel_id=1, source_target_pairs={{0,256},{128,384},{256,0},{384,128},{1,257},{129,385},{257,1},{385... | collective-permute-start | bytes 294920 | tf_op jit(solution)/shard_map/ppermute | solution.py:344
  87.6 1.9 %collective-permute-start.8 = (bf16[192,256]{1,0:T(8,128)(2,1)S(1)}, bf16[192,256]{1,0:T(8,128)(2,1)S(1)}, u32[]{:S(2)}, u32[]{:S(2)}) collective-permute-start(bf16[192,256]{1,0:T(8,128)(2,1)S(1)} %get-tuple-element.34.refs_4_), channel_id=1, source_target_pairs={{0,384},{128,0},{256,128},{384,256},{1,385},{129,1},{257,129},{385... | collective-permute-start | bytes 294920 | tf_op jit(solution)/shard_map/ppermute | solution.py:344
  89.5 3.6 %all-to-all-done.2 = bf16[8,96,128]{2,1,0:T(8,128)(2,1)} async-done(((bf16[8,96,128]{2,1,0:T(8,128)(2,1)}), bf16[8,96,128]{2,1,0:T(8,128)(2,1)}, u32[]{:S(2)}, u32[]{:S(2)}) %all-to-all-start.2) | async-done | bytes 196640 | tf_op jit(solution)/shard_map/all_to_all | solution.py:340
  93.1 2.3 %all_gather.11.pre_ref = bf16[16,96,128]{2,1,0:T(8,128)(2,1)S(1)} all-gather(bf16[8,96,128]{2,1,0:T(8,128)(2,1)} %all-to-all-done.2), channel_id=1, replica_groups=mesh['x'=4,'z'=8,'y'=8,'c'=2] {'c'}, dimensions={0}, use_global_device_ids=true | all-gather | bytes 589824 | tf_op jit(solution)/shard_map/all_gather | solution.py:390
  95.4 0.0 collective-permute-done.7.refs_6_
  95.4 0.0 collective-permute-done.8.refs_7_
  95.4 0.0 copy-done
  95.4 0.0 copy-done.4
  95.4 0.0 copy-done.6
  95.4 2.0 %second_layer.1 = (bf16[172,192]{1,0:T(8,128)(2,1)}, bf16[4,192,256]{2,1,0:T(8,128)(2,1)S(1)}) custom-call(bf16[16,96,128]{2,1,0:T(8,128)(2,1)S(1)} %all_gather.11.pre_ref, bf16[192,192]{1,0:T(8,128)(2,1)S(1)} %add_convert_fusion.adj_ref, bf16[1024,1024]{1,0:T(8,128)(2,1)S(1)} %copy-done, bf16[172,1024]{1,0:T(8,128)(2,1)S(1)} %bitcast.18, ...), custom_call_target="tpu_custom_call" | custom-call | tf_op jit(solution)/shard_map/second_layer/pallas_call | solution.py:249
  97.5 10.6 %all_to_all.35.refs_8_ = bf16[4,192,256]{2,1,0:T(8,128)(2,1)S(1)} all-to-all(bf16[4,192,256]{2,1,0:T(8,128)(2,1)S(1)} %get-tuple-element.41), channel_id=1, replica_groups=mesh['x'=4,'z'=8,'y'=8,'c'=2] {'x'}, dimensions={0} | all-to-all | bytes 786432 | tf_op jit(solution)/shard_map/all_to_all | solution.py:340
  108.1 0.5 gradient_part.1
  108.6 13.3 %all_to_all.36.recv_ref = bf16[8,64,256]{2,1,0:T(8,128)(2,1)S(1)} all-to-all(bf16[8,64,256]{2,1,0:T(8,128)(2,1)S(1)} %bitcast.17), channel_id=1, replica_groups=mesh['x'=4,'z'=8,'y'=8,'c'=2] {'z'}, dimensions={0} | all-to-all | bytes 524288 | tf_op jit(solution)/shard_map/all_to_all | solution.py:340
  121.9 12.9 %all_to_all.37 = bf16[8,64,256]{2,1,0:T(8,128)(2,1)S(1)} all-to-all(bf16[8,64,256]{2,1,0:T(8,128)(2,1)S(1)} %sum_and_spread.4), channel_id=1, replica_groups=mesh['x'=4,'z'=8,'y'=8,'c'=2] {'z'}, dimensions={0} | all-to-all | bytes 524288 | tf_op jit(solution)/shard_map/all_to_all | solution.py:340
  134.8 0.1 sum_and_spread.5
  134.9 14.1 %all_to_all.38 = bf16[4,512,256]{2,1,0:T(8,128)(2,1)S(1)} all-to-all(bf16[4,512,256]{2,1,0:T(8,128)(2,1)S(1)} %sum_and_spread.5), channel_id=1, replica_groups=mesh['x'=4,'z'=8,'y'=8,'c'=2] {'x'}, dimensions={0} | all-to-all | bytes 2097152 | tf_op jit(solution)/shard_map/all_to_all | solution.py:340
  148.9 1.0 assemble.1
  (4 shorter events, 0.1 us)
Async XLA Ops:
  2.7 15.7 %collective-permute-start = (bf16[544,256]{1,0:T(8,128)(2,1)}, bf16[544,256]{1,0:T(8,128)(2,1)S(1)}, u32[]{:S(2)}, u32[]{:S(2)}) collective-permute-start(bf16[544,256]{1,0:T(8,128)(2,1)} %get-tuple-element.25), channel_id=1, source_target_pairs={{0,128},{128,256},{256,384},{384,0},{1,129},{129,257},{257,385},{3... | collective-permute-start | bytes 835592 | tf_op jit(solution)/shard_map/ppermute | solution.py:344
  6.1 13.2 %collective-permute-start.1 = (bf16[544,256]{1,0:T(8,128)(2,1)}, bf16[544,256]{1,0:T(8,128)(2,1)S(1)}, u32[]{:S(2)}, u32[]{:S(2)}) collective-permute-start(bf16[544,256]{1,0:T(8,128)(2,1)} %get-tuple-element.26), channel_id=1, source_target_pairs={{0,384},{128,0},{256,128},{384,256},{1,385},{129,1},{257,129},{385... | collective-permute-start | bytes 835592 | tf_op jit(solution)/shard_map/ppermute | solution.py:344
  12.5 10.6 %collective-permute-start.2 = (bf16[544,256]{1,0:T(8,128)(2,1)}, bf16[544,256]{1,0:T(8,128)(2,1)S(1)}, u32[]{:S(2)}, u32[]{:S(2)}) collective-permute-start(bf16[544,256]{1,0:T(8,128)(2,1)} %get-tuple-element.27), channel_id=1, source_target_pairs={{0,256},{128,384},{256,0},{384,128},{1,257},{129,385},{257,1},{385... | collective-permute-start | bytes 835592 | tf_op jit(solution)/shard_map/ppermute | solution.py:344
  16.5 1.0 copy-start.5
  20.9 14.2 %copy-start.3 = (bf16[192,256]{1,0:T(8,128)(2,1)S(1)}, bf16[192,256]{1,0:T(8,128)(2,1)}, u32[]{:S(2)}) copy-start(bf16[192,256]{1,0:T(8,128)(2,1)} %refs_0_.1) | copy-start | bytes 294916
  20.9 25.9 %copy-start.9 = (s32[192]{0:T(256)S(1)}, s32[192]{0:T(256)}, u32[]{:S(2)}) copy-start(s32[192]{0:T(256)} %param.16) | copy-start | bytes 2308
  20.9 36.1 %copy-start.1 = (bf16[256,1024]{1,0:T(8,128)(2,1)S(1)}, bf16[256,1024]{1,0:T(8,128)(2,1)}, u32[]{:S(2)}) copy-start(bf16[256,1024]{1,0:T(8,128)(2,1)} %self_ref.1) | copy-start | bytes 1572868
  20.9 36.0 %copy-start.2 = (bf16[256,1024]{1,0:T(8,128)(2,1)S(1)}, bf16[256,1024]{1,0:T(8,128)(2,1)}, u32[]{:S(2)}) copy-start(bf16[256,1024]{1,0:T(8,128)(2,1)} %neigh_ref.1) | copy-start | bytes 1572868
  24.8 32.1 %all-to-all-start = ((bf16[8,192,256]{2,1,0:T(8,128)(2,1)}), bf16[8,192,256]{2,1,0:T(8,128)(2,1)S(1)}, u32[]{:S(2)}, u32[]{:S(2)}) async-start(bf16[8,192,256]{2,1,0:T(8,128)(2,1)} %bitcast.3), calls=%async_computation | async-start | bytes 1572864 | tf_op jit(solution)/shard_map/all_to_all | solution.py:340
  35.1 11.9 %collective-permute-start.3 = (bf16[192,256]{1,0:T(8,128)(2,1)S(1)}, bf16[192,256]{1,0:T(8,128)(2,1)S(1)}, u32[]{:S(2)}, u32[]{:S(2)}) collective-permute-start(bf16[192,256]{1,0:T(8,128)(2,1)S(1)} %copy-done.3), channel_id=1, source_target_pairs={{0,128},{128,256},{256,384},{384,0},{1,129},{129,257},{257,385},{3... | collective-permute-start | bytes 294920 | tf_op jit(solution)/shard_map/ppermute | solution.py:344
  37.0 9.9 %collective-permute-start.4 = (bf16[192,256]{1,0:T(8,128)(2,1)S(1)}, bf16[192,256]{1,0:T(8,128)(2,1)S(1)}, u32[]{:S(2)}, u32[]{:S(2)}) collective-permute-start(bf16[192,256]{1,0:T(8,128)(2,1)S(1)} %copy-done.3), channel_id=1, source_target_pairs={{0,256},{128,384},{256,0},{384,128},{1,257},{129,385},{257,1},{385... | collective-permute-start | bytes 294920 | tf_op jit(solution)/shard_map/ppermute | solution.py:344
  42.2 6.7 %collective-permute-start.5 = (bf16[192,256]{1,0:T(8,128)(2,1)S(1)}, bf16[192,256]{1,0:T(8,128)(2,1)S(1)}, u32[]{:S(2)}, u32[]{:S(2)}) collective-permute-start(bf16[192,256]{1,0:T(8,128)(2,1)S(1)} %copy-done.3), channel_id=1, source_target_pairs={{0,384},{128,0},{256,128},{384,256},{1,385},{129,1},{257,129},{385... | collective-permute-start | bytes 294920 | tf_op jit(solution)/shard_map/ppermute | solution.py:344
  46.9 22.8 %copy-start.8 = (s32[192]{0:T(256)S(1)}, s32[192]{0:T(256)}, u32[]{:S(2)}) copy-start(s32[192]{0:T(256)} %param.18) | copy-start | bytes 2308
  57.4 25.9 %copy-start.7 = (s32[192,10]{0,1:T(8,128)S(1)}, s32[192,10]{0,1:T(8,128)}, u32[]{:S(2)}) copy-start(s32[192,10]{0,1:T(8,128)} %param.17) | copy-start | bytes 23044
  57.5 37.9 %copy-start = (bf16[1024,1024]{1,0:T(8,128)(2,1)S(1)}, bf16[1024,1024]{1,0:T(8,128)(2,1)}, u32[]{:S(2)}) copy-start(bf16[1024,1024]{1,0:T(8,128)(2,1)} %two_ref.1) | copy-start | bytes 6291460
  57.5 37.9 %copy-start.4 = (bf16[1024,172]{0,1:T(8,128)(2,1)S(1)}, bf16[1024,172]{0,1:T(8,128)(2,1)}, u32[]{:S(2)}) copy-start(bf16[1024,172]{0,1:T(8,128)(2,1)} %param.22) | copy-start | bytes 1056772
  57.5 37.9 %copy-start.6 = (bf16[192,172]{0,1:T(8,128)(2,1)S(1)}, bf16[192,172]{0,1:T(8,128)(2,1)}, u32[]{:S(2)}) copy-start(bf16[192,172]{0,1:T(8,128)(2,1)} %param.23) | copy-start | bytes 198148
  60.7 17.9 %all-to-all-start.1 = ((bf16[8,96,128]{2,1,0:T(8,128)(2,1)}), bf16[8,96,128]{2,1,0:T(8,128)(2,1)S(1)}, u32[]{:S(2)}, u32[]{:S(2)}) async-start(bf16[8,96,128]{2,1,0:T(8,128)(2,1)} %pair_sum.1), calls=%async_computation.1 | async-start | bytes 393216 | tf_op jit(solution)/shard_map/all_to_all | solution.py:340
  67.8 6.5 %collective-permute-start.6 = (bf16[192,256]{1,0:T(8,128)(2,1)S(1)}, bf16[192,256]{1,0:T(8,128)(2,1)S(1)}, u32[]{:S(2)}, u32[]{:S(2)}) collective-permute-start(bf16[192,256]{1,0:T(8,128)(2,1)S(1)} %get-tuple-element.34.refs_4_), channel_id=1, source_target_pairs={{0,128},{128,256},{256,384},{384,0},{1,129},{129,257},{257,385},{3... | collective-permute-start | bytes 294920 | tf_op jit(solution)/shard_map/ppermute | solution.py:344
  79.3 13.8 %all-to-all-start.2 = ((bf16[8,96,128]{2,1,0:T(8,128)(2,1)}), bf16[8,96,128]{2,1,0:T(8,128)(2,1)}, u32[]{:S(2)}, u32[]{:S(2)}) async-start(bf16[8,96,128]{2,1,0:T(8,128)(2,1)} %sum_and_spread.3), calls=%async_computation.2 | async-start | bytes 393216 | tf_op jit(solution)/shard_map/all_to_all | solution.py:340
  84.2 11.2 %collective-permute-start.7 = (bf16[192,256]{1,0:T(8,128)(2,1)S(1)}, bf16[192,256]{1,0:T(8,128)(2,1)S(1)}, u32[]{:S(2)}, u32[]{:S(2)}) collective-permute-start(bf16[192,256]{1,0:T(8,128)(2,1)S(1)} %get-tuple-element.34.refs_4_), channel_id=1, source_target_pairs={{0,256},{128,384},{256,0},{384,128},{1,257},{129,385},{257,1},{385... | collective-permute-start | bytes 294920 | tf_op jit(solution)/shard_map/ppermute | solution.py:344
  87.6 7.8 %collective-permute-start.8 = (bf16[192,256]{1,0:T(8,128)(2,1)S(1)}, bf16[192,256]{1,0:T(8,128)(2,1)S(1)}, u32[]{:S(2)}, u32[]{:S(2)}) collective-permute-start(bf16[192,256]{1,0:T(8,128)(2,1)S(1)} %get-tuple-element.34.refs_4_), channel_id=1, source_target_pairs={{0,384},{128,0},{256,128},{384,256},{1,385},{129,1},{257,129},{385... | collective-permute-start | bytes 294920 | tf_op jit(solution)/shard_map/ppermute | solution.py:344

commit v10 on v9

--- a/solution.py
+++ b/solution.py
@@ -370,8 +370,7 @@
     running = gather_sum(slots, per_x, jnp.float32, None, payloads[:1])
     running = gather_sum(slots, per_x, jnp.float32, running, arrived[1:])
     parts = gather_sum(slots, per_x, jnp.bfloat16, running, arrived[:1], staged=True)
-    parts, own_late = lax.optimization_barrier((parts, own_features))
-    own = [shift_x(own_late, s) for s in range(1, XS)]
+    own = [shift_x(own_features, s) for s in range(1, XS)]
     recv = exchange(parts.reshape(groups // XS, own_rows, width), "z")
     recv, *own = lax.optimization_barrier((recv, *own))
     mean_rows, pieces = first_layer(

time: 151 us -> 151 us (level)
  no operation moved by 1% of the time
where the time goes in v10:
time: 151 us; the launch traced here: 150 us
  blocking collectives  55.6 us (37%)
  starting transfers between devices  54 us (36%)
  waiting for transfers between devices  25.5 us (17%)
  Pallas kernels  11.9 us (8%)
    all_to_all x4, blocking collectives, exchange(): return lax.all_to_all(pieces, axis, split_axis=0, concat_axis=0, tiled=True)  50.8 us
    ppermute x9, starting transfers between devices, shift_x(): return lax.ppermute(array, 'x', [(i, (i + steps) % XS) for i in range(XS)])  32.6 us
    all_to_all x3, starting transfers between devices, exchange(): return lax.all_to_all(pieces, axis, split_axis=0, concat_axis=0, tiled=True)  21.4 us
    all_to_all x3, waiting for transfers between devices, exchange(): return lax.all_to_all(pieces, axis, split_axis=0, concat_axis=0, tiled=True)  15.9 us
    ppermute x9, waiting for transfers between devices, shift_x(): return lax.ppermute(array, 'x', [(i, (i + steps) % XS) for i in range(XS)])  9.6 us
    pallas_call x3, Pallas kernels, gather_sum(): pl.pallas_call(functools.partial(gather_kernel, slots, int(carried is not...  4.32 us
  transfers between devices with their start and end apart: 12, of which 7 were waited for; matrix products, arithmetic and copies ran while one was open for 1% of the time, Pallas kernels for 2%

profile of v10, /device:TPU:2, one launch (start us, length us, event | category | flops | bytes accessed | tf_op | source)
XLA Modules:
  0.0 150.0 jit_solution(4522934618057443520)
XLA Ops:
  0.6 2.1 %payloads.1 = (bf16[544,256]{1,0:T(8,128)(2,1)}, bf16[544,256]{1,0:T(8,128)(2,1)}, bf16[544,256]{1,0:T(8,128)(2,1)}, bf16[544,256]{1,0:T(8,128)(2,1)}) custom-call(s32[1]{0:T(128)} %bitcast.place_ref, s32[4,6144]{1,0:T(4,128)} %bitcast.20, s32[1,6144]{1,0:T(1,128)} %count_hbm.1, bf16[512,256]{1,0:T(8,128)(2,1)} %table_hbm.1), custom_call_target="tpu_custom_call" | custom-call | tf_op jit(solution)/shard_map/payloads/pallas_call | solution.py:78
  2.7 3.4 %collective-permute-start = (bf16[544,256]{1,0:T(8,128)(2,1)}, bf16[544,256]{1,0:T(8,128)(2,1)S(1)}, u32[]{:S(2)}, u32[]{:S(2)}) collective-permute-start(bf16[544,256]{1,0:T(8,128)(2,1)} %get-tuple-element.23), channel_id=1, source_target_pairs={{0,128},{128,256},{256,384},{384,0},{1,129},{129,257},{257,385},{3... | collective-permute-start | bytes 835592 | tf_op jit(solution)/shard_map/ppermute | solution.py:344
  6.1 6.3 %collective-permute-start.1 = (bf16[544,256]{1,0:T(8,128)(2,1)}, bf16[544,256]{1,0:T(8,128)(2,1)S(1)}, u32[]{:S(2)}, u32[]{:S(2)}) collective-permute-start(bf16[544,256]{1,0:T(8,128)(2,1)} %get-tuple-element.24), channel_id=1, source_target_pairs={{0,384},{128,0},{256,128},{384,256},{1,385},{129,1},{257,129},{385... | collective-permute-start | bytes 835592 | tf_op jit(solution)/shard_map/ppermute | solution.py:344
  12.5 4.0 %collective-permute-start.2 = (bf16[544,256]{1,0:T(8,128)(2,1)}, bf16[544,256]{1,0:T(8,128)(2,1)S(1)}, u32[]{:S(2)}, u32[]{:S(2)}) collective-permute-start(bf16[544,256]{1,0:T(8,128)(2,1)} %get-tuple-element.25), channel_id=1, source_target_pairs={{0,256},{128,384},{256,0},{384,128},{1,257},{129,385},{257,1},{385... | collective-permute-start | bytes 835592 | tf_op jit(solution)/shard_map/ppermute | solution.py:344
  16.5 0.0 copy-start.5
  16.5 0.9 copy-done.5
  17.4 1.0 gather_sum.3.refs_0_
  18.4 0.0 collective-permute-done.refs_1_
  18.4 0.9 collective-permute-done.1.refs_2_
  19.3 1.6 %gather_sum.4.refs_0_ = f32[1536,256]{1,0:T(8,128)S(1)} custom-call(f32[1536,256]{1,0:T(8,128)S(1)} %gather_sum.3.refs_0_, bf16[544,256]{1,0:T(8,128)(2,1)S(1)} %collective-permute-done.refs_1_, bf16[544,256]{1,0:T(8,128)(2,1)S(1)} %collective-permute-done.1.refs_2_), custom_call_target="tpu_custom_call" | custom-call | tf_op jit(solution)/shard_map/gather_sum/pallas_call | solution.py:135
  20.9 0.0 copy-start.3
  20.9 0.0 copy-start.9
  20.9 0.0 copy-start.1
  20.9 0.0 copy-start.2
  21.0 2.1 %collective-permute-done.2.refs_1_ = bf16[544,256]{1,0:T(8,128)(2,1)S(1)} collective-permute-done((bf16[544,256]{1,0:T(8,128)(2,1)}, bf16[544,256]{1,0:T(8,128)(2,1)S(1)}, u32[]{:S(2)}, u32[]{:S(2)}) %collective-permute-start.2) | collective-permute-done | bytes 278560 | tf_op jit(solution)/shard_map/ppermute | solution.py:344
  23.1 1.8 %gather_sum.5 = bf16[1536,256]{1,0:T(8,128)(2,1)} custom-call(f32[1536,256]{1,0:T(8,128)S(1)} %gather_sum.4.refs_0_, bf16[544,256]{1,0:T(8,128)(2,1)S(1)} %collective-permute-done.2.refs_1_), custom_call_target="tpu_custom_call" | custom-call | tf_op jit(solution)/shard_map/gather_sum/pallas_call | solution.py:135
  24.8 10.2 %all-to-all-start = ((bf16[8,192,256]{2,1,0:T(8,128)(2,1)}), bf16[8,192,256]{2,1,0:T(8,128)(2,1)S(1)}, u32[]{:S(2)}, u32[]{:S(2)}) async-start(bf16[8,192,256]{2,1,0:T(8,128)(2,1)} %bitcast.3), calls=%async_computation | async-start | bytes 1572864 | tf_op jit(solution)/shard_map/all_to_all | solution.py:340
  35.1 0.0 copy-done.3
  35.1 1.9 %collective-permute-start.3 = (bf16[192,256]{1,0:T(8,128)(2,1)S(1)}, bf16[192,256]{1,0:T(8,128)(2,1)S(1)}, u32[]{:S(2)}, u32[]{:S(2)}) collective-permute-start(bf16[192,256]{1,0:T(8,128)(2,1)S(1)} %copy-done.3), channel_id=1, source_target_pairs={{0,128},{128,256},{256,384},{384,0},{1,129},{129,257},{257,385},{3... | collective-permute-start | bytes 294920 | tf_op jit(solution)/shard_map/ppermute | solution.py:344
  37.0 5.2 %collective-permute-start.4 = (bf16[192,256]{1,0:T(8,128)(2,1)S(1)}, bf16[192,256]{1,0:T(8,128)(2,1)S(1)}, u32[]{:S(2)}, u32[]{:S(2)}) collective-permute-start(bf16[192,256]{1,0:T(8,128)(2,1)S(1)} %copy-done.3), channel_id=1, source_target_pairs={{0,256},{128,384},{256,0},{384,128},{1,257},{129,385},{257,1},{385... | collective-permute-start | bytes 294920 | tf_op jit(solution)/shard_map/ppermute | solution.py:344
  42.2 4.5 %collective-permute-start.5 = (bf16[192,256]{1,0:T(8,128)(2,1)S(1)}, bf16[192,256]{1,0:T(8,128)(2,1)S(1)}, u32[]{:S(2)}, u32[]{:S(2)}) collective-permute-start(bf16[192,256]{1,0:T(8,128)(2,1)S(1)} %copy-done.3), channel_id=1, source_target_pairs={{0,384},{128,0},{256,128},{384,256},{1,385},{129,1},{257,129},{385... | collective-permute-start | bytes 294920 | tf_op jit(solution)/shard_map/ppermute | solution.py:344
  46.8 0.0 copy-done.9
  46.8 0.1 copy.20.degree_ref
  46.9 0.0 copy-start.8
  46.9 0.0 collective-permute-done.3.refs_1_
  46.9 0.0 collective-permute-done.4.refs_2_
  46.9 2.0 %collective-permute-done.5.refs_3_ = bf16[192,256]{1,0:T(8,128)(2,1)S(1)} collective-permute-done((bf16[192,256]{1,0:T(8,128)(2,1)S(1)}, bf16[192,256]{1,0:T(8,128)(2,1)S(1)}, u32[]{:S(2)}, u32[]{:S(2)}) %collective-permute-start.5) | collective-permute-done | bytes 98336 | tf_op jit(solution)/shard_map/ppermute | solution.py:344
  49.0 8.0 %all-to-all-done.recv_ref = bf16[8,192,256]{2,1,0:T(8,128)(2,1)S(1)} async-done(((bf16[8,192,256]{2,1,0:T(8,128)(2,1)}), bf16[8,192,256]{2,1,0:T(8,128)(2,1)S(1)}, u32[]{:S(2)}, u32[]{:S(2)}) %all-to-all-start) | async-done | bytes 786464 | tf_op jit(solution)/shard_map/all_to_all | solution.py:340
  57.0 0.0 copy-done.1
  57.0 0.0 copy-done.2
  57.0 0.4 first_layer.1
  57.4 0.0 copy-start.7
  57.5 0.0 copy-start
  57.5 0.0 copy-start.4
  57.5 0.0 copy-start.6
  57.5 2.5 %all-gather = bf16[32,96,128]{2,1,0:T(8,128)(2,1)S(1)} all-gather(bf16[16,96,128]{2,1,0:T(8,128)(2,1)S(1)} %get-tuple-element.31), channel_id=2, replica_groups=mesh['x'=4,'z'=8,'y'=8,'c'=2] {'c'}, dimensions={0}, use_global_device_ids=true | all-gather | bytes 1179648 | tf_op jit(solution)/shard_map/all_gather | solution.py:386
  60.0 0.7 pair_sum.1
  60.7 7.1 %all-to-all-start.1 = ((bf16[8,96,128]{2,1,0:T(8,128)(2,1)}), bf16[8,96,128]{2,1,0:T(8,128)(2,1)S(1)}, u32[]{:S(2)}, u32[]{:S(2)}) async-start(bf16[8,96,128]{2,1,0:T(8,128)(2,1)} %pair_sum.1), calls=%async_computation.1 | async-start | bytes 393216 | tf_op jit(solution)/shard_map/all_to_all | solution.py:340
  67.8 1.9 %collective-permute-start.6 = (bf16[192,256]{1,0:T(8,128)(2,1)S(1)}, bf16[192,256]{1,0:T(8,128)(2,1)S(1)}, u32[]{:S(2)}, u32[]{:S(2)}) collective-permute-start(bf16[192,256]{1,0:T(8,128)(2,1)S(1)} %get-tuple-element.30.refs_4_), channel_id=1, source_target_pairs={{0,128},{128,256},{256,384},{384,0},{1,129},{129,257},{257,385},{3... | collective-permute-start | bytes 294920 | tf_op jit(solution)/shard_map/ppermute | solution.py:344
  69.7 0.0 copy-done.8
  69.8 4.6 %collective-permute-done.6.refs_5_ = bf16[192,256]{1,0:T(8,128)(2,1)S(1)} collective-permute-done((bf16[192,256]{1,0:T(8,128)(2,1)S(1)}, bf16[192,256]{1,0:T(8,128)(2,1)S(1)}, u32[]{:S(2)}, u32[]{:S(2)}) %collective-permute-start.6) | collective-permute-done | bytes 98336 | tf_op jit(solution)/shard_map/ppermute | solution.py:344
  74.3 4.3 %all-to-all-done.1.recv_ref = bf16[8,96,128]{2,1,0:T(8,128)(2,1)S(1)} async-done(((bf16[8,96,128]{2,1,0:T(8,128)(2,1)}), bf16[8,96,128]{2,1,0:T(8,128)(2,1)S(1)}, u32[]{:S(2)}, u32[]{:S(2)}) %all-to-all-start.1) | async-done | bytes 196640 | tf_op jit(solution)/shard_map/all_to_all | solution.py:340
  78.6 0.7 sum_and_spread.3
  79.3 4.0 %all-to-all-start.2 = ((bf16[8,96,128]{2,1,0:T(8,128)(2,1)}), bf16[8,96,128]{2,1,0:T(8,128)(2,1)}, u32[]{:S(2)}, u32[]{:S(2)}) async-start(bf16[8,96,128]{2,1,0:T(8,128)(2,1)} %sum_and_spread.3), calls=%async_computation.2 | async-start | bytes 393216 | tf_op jit(solution)/shard_map/all_to_all | solution.py:340
  83.3 0.0 copy-done.7
  83.3 0.8 convert_reduce_fusion
  84.2 3.4 %collective-permute-start.7 = (bf16[192,256]{1,0:T(8,128)(2,1)S(1)}, bf16[192,256]{1,0:T(8,128)(2,1)S(1)}, u32[]{:S(2)}, u32[]{:S(2)}) collective-permute-start(bf16[192,256]{1,0:T(8,128)(2,1)S(1)} %get-tuple-element.30.refs_4_), channel_id=1, source_target_pairs={{0,256},{128,384},{256,0},{384,128},{1,257},{129,385},{257,1},{385... | collective-permute-start | bytes 294920 | tf_op jit(solution)/shard_map/ppermute | solution.py:344
  87.6 1.9 %collective-permute-start.8 = (bf16[192,256]{1,0:T(8,128)(2,1)S(1)}, bf16[192,256]{1,0:T(8,128)(2,1)S(1)}, u32[]{:S(2)}, u32[]{:S(2)}) collective-permute-start(bf16[192,256]{1,0:T(8,128)(2,1)S(1)} %get-tuple-element.30.refs_4_), channel_id=1, source_target_pairs={{0,384},{128,0},{256,128},{384,256},{1,385},{129,1},{257,129},{385... | collective-permute-start | bytes 294920 | tf_op jit(solution)/shard_map/ppermute | solution.py:344
  89.5 3.6 %all-to-all-done.2 = bf16[8,96,128]{2,1,0:T(8,128)(2,1)} async-done(((bf16[8,96,128]{2,1,0:T(8,128)(2,1)}), bf16[8,96,128]{2,1,0:T(8,128)(2,1)}, u32[]{:S(2)}, u32[]{:S(2)}) %all-to-all-start.2) | async-done | bytes 196640 | tf_op jit(solution)/shard_map/all_to_all | solution.py:340
  93.1 2.3 %all_gather.11.pre_ref = bf16[16,96,128]{2,1,0:T(8,128)(2,1)S(1)} all-gather(bf16[8,96,128]{2,1,0:T(8,128)(2,1)} %all-to-all-done.2), channel_id=1, replica_groups=mesh['x'=4,'z'=8,'y'=8,'c'=2] {'c'}, dimensions={0}, use_global_device_ids=true | all-gather | bytes 589824 | tf_op jit(solution)/shard_map/all_gather | solution.py:389
  95.4 0.0 collective-permute-done.7.refs_6_
  95.4 0.0 collective-permute-done.8.refs_7_
  95.4 0.0 copy-done
  95.4 0.0 copy-done.4
  95.4 0.0 copy-done.6
  95.4 2.0 %second_layer.1 = (bf16[172,192]{1,0:T(8,128)(2,1)}, bf16[4,192,256]{2,1,0:T(8,128)(2,1)S(1)}) custom-call(bf16[16,96,128]{2,1,0:T(8,128)(2,1)S(1)} %all_gather.11.pre_ref, bf16[192,192]{1,0:T(8,128)(2,1)S(1)} %add_convert_fusion.adj_ref, bf16[1024,1024]{1,0:T(8,128)(2,1)S(1)} %copy-done, bf16[172,1024]{1,0:T(8,128)(2,1)S(1)} %bitcast.18, ...), custom_call_target="tpu_custom_call" | custom-call | tf_op jit(solution)/shard_map/second_layer/pallas_call | solution.py:249
  97.5 10.6 %all_to_all.35.refs_8_ = bf16[4,192,256]{2,1,0:T(8,128)(2,1)S(1)} all-to-all(bf16[4,192,256]{2,1,0:T(8,128)(2,1)S(1)} %get-tuple-element.37), channel_id=1, replica_groups=mesh['x'=4,'z'=8,'y'=8,'c'=2] {'x'}, dimensions={0} | all-to-all | bytes 786432 | tf_op jit(solution)/shard_map/all_to_all | solution.py:340
  108.1 0.5 gradient_part.1
  108.6 13.3 %all_to_all.36.recv_ref = bf16[8,64,256]{2,1,0:T(8,128)(2,1)S(1)} all-to-all(bf16[8,64,256]{2,1,0:T(8,128)(2,1)S(1)} %bitcast.17), channel_id=1, replica_groups=mesh['x'=4,'z'=8,'y'=8,'c'=2] {'z'}, dimensions={0} | all-to-all | bytes 524288 | tf_op jit(solution)/shard_map/all_to_all | solution.py:340
  121.9 12.9 %all_to_all.37 = bf16[8,64,256]{2,1,0:T(8,128)(2,1)S(1)} all-to-all(bf16[8,64,256]{2,1,0:T(8,128)(2,1)S(1)} %sum_and_spread.4), channel_id=1, replica_groups=mesh['x'=4,'z'=8,'y'=8,'c'=2] {'z'}, dimensions={0} | all-to-all | bytes 524288 | tf_op jit(solution)/shard_map/all_to_all | solution.py:340
  134.8 0.1 sum_and_spread.5
  134.9 14.1 %all_to_all.38 = bf16[4,512,256]{2,1,0:T(8,128)(2,1)S(1)} all-to-all(bf16[4,512,256]{2,1,0:T(8,128)(2,1)S(1)} %sum_and_spread.5), channel_id=1, replica_groups=mesh['x'=4,'z'=8,'y'=8,'c'=2] {'x'}, dimensions={0} | all-to-all | bytes 2097152 | tf_op jit(solution)/shard_map/all_to_all | solution.py:340
  148.9 1.0 assemble.1
  (4 shorter events, 0.1 us)
Async XLA Ops:
  2.7 15.7 %collective-permute-start = (bf16[544,256]{1,0:T(8,128)(2,1)}, bf16[544,256]{1,0:T(8,128)(2,1)S(1)}, u32[]{:S(2)}, u32[]{:S(2)}) collective-permute-start(bf16[544,256]{1,0:T(8,128)(2,1)} %get-tuple-element.23), channel_id=1, source_target_pairs={{0,128},{128,256},{256,384},{384,0},{1,129},{129,257},{257,385},{3... | collective-permute-start | bytes 835592 | tf_op jit(solution)/shard_map/ppermute | solution.py:344
  6.1 13.2 %collective-permute-start.1 = (bf16[544,256]{1,0:T(8,128)(2,1)}, bf16[544,256]{1,0:T(8,128)(2,1)S(1)}, u32[]{:S(2)}, u32[]{:S(2)}) collective-permute-start(bf16[544,256]{1,0:T(8,128)(2,1)} %get-tuple-element.24), channel_id=1, source_target_pairs={{0,384},{128,0},{256,128},{384,256},{1,385},{129,1},{257,129},{385... | collective-permute-start | bytes 835592 | tf_op jit(solution)/shard_map/ppermute | solution.py:344
  12.5 10.6 %collective-permute-start.2 = (bf16[544,256]{1,0:T(8,128)(2,1)}, bf16[544,256]{1,0:T(8,128)(2,1)S(1)}, u32[]{:S(2)}, u32[]{:S(2)}) collective-permute-start(bf16[544,256]{1,0:T(8,128)(2,1)} %get-tuple-element.25), channel_id=1, source_target_pairs={{0,256},{128,384},{256,0},{384,128},{1,257},{129,385},{257,1},{385... | collective-permute-start | bytes 835592 | tf_op jit(solution)/shard_map/ppermute | solution.py:344
  16.5 1.0 copy-start.5
  20.9 14.2 %copy-start.3 = (bf16[192,256]{1,0:T(8,128)(2,1)S(1)}, bf16[192,256]{1,0:T(8,128)(2,1)}, u32[]{:S(2)}) copy-start(bf16[192,256]{1,0:T(8,128)(2,1)} %refs_0_.1) | copy-start | bytes 294916
  20.9 25.9 %copy-start.9 = (s32[192]{0:T(256)S(1)}, s32[192]{0:T(256)}, u32[]{:S(2)}) copy-start(s32[192]{0:T(256)} %param.16) | copy-start | bytes 2308
  20.9 36.1 %copy-start.1 = (bf16[256,1024]{1,0:T(8,128)(2,1)S(1)}, bf16[256,1024]{1,0:T(8,128)(2,1)}, u32[]{:S(2)}) copy-start(bf16[256,1024]{1,0:T(8,128)(2,1)} %self_ref.1) | copy-start | bytes 1572868
  20.9 36.0 %copy-start.2 = (bf16[256,1024]{1,0:T(8,128)(2,1)S(1)}, bf16[256,1024]{1,0:T(8,128)(2,1)}, u32[]{:S(2)}) copy-start(bf16[256,1024]{1,0:T(8,128)(2,1)} %neigh_ref.1) | copy-start | bytes 1572868
  24.8 32.1 %all-to-all-start = ((bf16[8,192,256]{2,1,0:T(8,128)(2,1)}), bf16[8,192,256]{2,1,0:T(8,128)(2,1)S(1)}, u32[]{:S(2)}, u32[]{:S(2)}) async-start(bf16[8,192,256]{2,1,0:T(8,128)(2,1)} %bitcast.3), calls=%async_computation | async-start | bytes 1572864 | tf_op jit(solution)/shard_map/all_to_all | solution.py:340
  35.1 11.9 %collective-permute-start.3 = (bf16[192,256]{1,0:T(8,128)(2,1)S(1)}, bf16[192,256]{1,0:T(8,128)(2,1)S(1)}, u32[]{:S(2)}, u32[]{:S(2)}) collective-permute-start(bf16[192,256]{1,0:T(8,128)(2,1)S(1)} %copy-done.3), channel_id=1, source_target_pairs={{0,128},{128,256},{256,384},{384,0},{1,129},{129,257},{257,385},{3... | collective-permute-start | bytes 294920 | tf_op jit(solution)/shard_map/ppermute | solution.py:344
  37.0 9.9 %collective-permute-start.4 = (bf16[192,256]{1,0:T(8,128)(2,1)S(1)}, bf16[192,256]{1,0:T(8,128)(2,1)S(1)}, u32[]{:S(2)}, u32[]{:S(2)}) collective-permute-start(bf16[192,256]{1,0:T(8,128)(2,1)S(1)} %copy-done.3), channel_id=1, source_target_pairs={{0,256},{128,384},{256,0},{384,128},{1,257},{129,385},{257,1},{385... | collective-permute-start | bytes 294920 | tf_op jit(solution)/shard_map/ppermute | solution.py:344
  42.2 6.7 %collective-permute-start.5 = (bf16[192,256]{1,0:T(8,128)(2,1)S(1)}, bf16[192,256]{1,0:T(8,128)(2,1)S(1)}, u32[]{:S(2)}, u32[]{:S(2)}) collective-permute-start(bf16[192,256]{1,0:T(8,128)(2,1)S(1)} %copy-done.3), channel_id=1, source_target_pairs={{0,384},{128,0},{256,128},{384,256},{1,385},{129,1},{257,129},{385... | collective-permute-start | bytes 294920 | tf_op jit(solution)/shard_map/ppermute | solution.py:344
  46.9 22.8 %copy-start.8 = (s32[192]{0:T(256)S(1)}, s32[192]{0:T(256)}, u32[]{:S(2)}) copy-start(s32[192]{0:T(256)} %param.18) | copy-start | bytes 2308
  57.4 25.9 %copy-start.7 = (s32[192,10]{0,1:T(8,128)S(1)}, s32[192,10]{0,1:T(8,128)}, u32[]{:S(2)}) copy-start(s32[192,10]{0,1:T(8,128)} %param.17) | copy-start | bytes 23044
  57.5 37.9 %copy-start = (bf16[1024,1024]{1,0:T(8,128)(2,1)S(1)}, bf16[1024,1024]{1,0:T(8,128)(2,1)}, u32[]{:S(2)}) copy-start(bf16[1024,1024]{1,0:T(8,128)(2,1)} %two_ref.1) | copy-start | bytes 6291460
  57.5 37.9 %copy-start.4 = (bf16[1024,172]{0,1:T(8,128)(2,1)S(1)}, bf16[1024,172]{0,1:T(8,128)(2,1)}, u32[]{:S(2)}) copy-start(bf16[1024,172]{0,1:T(8,128)(2,1)} %param.22) | copy-start | bytes 1056772
  57.5 37.9 %copy-start.6 = (bf16[192,172]{0,1:T(8,128)(2,1)S(1)}, bf16[192,172]{0,1:T(8,128)(2,1)}, u32[]{:S(2)}) copy-start(bf16[192,172]{0,1:T(8,128)(2,1)} %param.23) | copy-start | bytes 198148
  60.7 17.9 %all-to-all-start.1 = ((bf16[8,96,128]{2,1,0:T(8,128)(2,1)}), bf16[8,96,128]{2,1,0:T(8,128)(2,1)S(1)}, u32[]{:S(2)}, u32[]{:S(2)}) async-start(bf16[8,96,128]{2,1,0:T(8,128)(2,1)} %pair_sum.1), calls=%async_computation.1 | async-start | bytes 393216 | tf_op jit(solution)/shard_map/all_to_all | solution.py:340
  67.8 6.5 %collective-permute-start.6 = (bf16[192,256]{1,0:T(8,128)(2,1)S(1)}, bf16[192,256]{1,0:T(8,128)(2,1)S(1)}, u32[]{:S(2)}, u32[]{:S(2)}) collective-permute-start(bf16[192,256]{1,0:T(8,128)(2,1)S(1)} %get-tuple-element.30.refs_4_), channel_id=1, source_target_pairs={{0,128},{128,256},{256,384},{384,0},{1,129},{129,257},{257,385},{3... | collective-permute-start | bytes 294920 | tf_op jit(solution)/shard_map/ppermute | solution.py:344
  79.3 13.8 %all-to-all-start.2 = ((bf16[8,96,128]{2,1,0:T(8,128)(2,1)}), bf16[8,96,128]{2,1,0:T(8,128)(2,1)}, u32[]{:S(2)}, u32[]{:S(2)}) async-start(bf16[8,96,128]{2,1,0:T(8,128)(2,1)} %sum_and_spread.3), calls=%async_computation.2 | async-start | bytes 393216 | tf_op jit(solution)/shard_map/all_to_all | solution.py:340
  84.2 11.2 %collective-permute-start.7 = (bf16[192,256]{1,0:T(8,128)(2,1)S(1)}, bf16[192,256]{1,0:T(8,128)(2,1)S(1)}, u32[]{:S(2)}, u32[]{:S(2)}) collective-permute-start(bf16[192,256]{1,0:T(8,128)(2,1)S(1)} %get-tuple-element.30.refs_4_), channel_id=1, source_target_pairs={{0,256},{128,384},{256,0},{384,128},{1,257},{129,385},{257,1},{385... | collective-permute-start | bytes 294920 | tf_op jit(solution)/shard_map/ppermute | solution.py:344
  87.6 7.8 %collective-permute-start.8 = (bf16[192,256]{1,0:T(8,128)(2,1)S(1)}, bf16[192,256]{1,0:T(8,128)(2,1)S(1)}, u32[]{:S(2)}, u32[]{:S(2)}) collective-permute-start(bf16[192,256]{1,0:T(8,128)(2,1)S(1)} %get-tuple-element.30.refs_4_), channel_id=1, source_target_pairs={{0,384},{128,0},{256,128},{384,256},{1,385},{129,1},{257,129},{385... | collective-permute-start | bytes 294920 | tf_op jit(solution)/shard_map/ppermute | solution.py:344
